TPU v7x, 32 devices: a whole 2x2x4 slice. The times are simulated.
32 devices in a mesh: section: 4 (over y, x), seq: 8 (over z, core).
Axes of the slice: x: 2, y: 2, z: 4, core: 2. Of those that a mesh axis runs over, the one named last changes fastest.
Arguments:
- inputs: bfloat16 [4, 512, 2048], P(None, 'seq'), may hold values from -6 to 6
- doc_starts: int32 [4, 2], replicated, may hold values from 1 to 511, as said below
- valid_mask: int32 [4, 512], P(None, 'seq'), may hold values 0 or 1
- cotangent: bfloat16 [4, 512, 2048], P(None, 'seq'), may hold values from -6 to 6
- prev_state: bfloat16 [4, 2, 2560], replicated, may hold values from -6 to 6
- prev_inputs: bfloat16 [4, 2, 3, 2560], replicated, may hold values from -6 to 6
- rec_gain: bfloat16 [2, 2048], P(None, 'seq'), may hold values from 0.25 to 1.75
- in_weight: bfloat16 [2, 2048, 2560], P(None, 'seq'), may hold values from -0.125 to 0.125
- side_weight: bfloat16 [2, 2048, 2560], P(None, 'seq'), may hold values from -0.125 to 0.125
- out_weight: bfloat16 [2, 2560, 2048], P(None, 'seq'), may hold values from -0.3125 to 0.3125
- rate_blocks: bfloat16 [2, 10, 256, 256], P(None, None, 'seq'), may hold values from -0.375 to 0.375
- inflow_blocks: bfloat16 [2, 10, 256, 256], P(None, None, 'seq'), may hold values from -0.375 to 0.375
- rate_bias: bfloat16 [2, 2560], P(None, 'seq'), may hold values from -4 to 4
- inflow_bias: bfloat16 [2, 2560], P(None, 'seq'), may hold values from -4 to 4
- conv_taps: bfloat16 [2, 4, 2560], P(None, None, 'seq'), may hold values from -3 to 3
- conv_bias: bfloat16 [2, 2560], P(None, 'seq'), may hold values from -3 to 3
- lru_param: bfloat16 [2, 2560], P(None, 'seq'), may hold values from 4 to 11
- mlp_gain: bfloat16 [2, 2048], P(None, 'seq'), may hold values from 0.25 to 1.75
- gate_weight: bfloat16 [2, 2048, 6144], P(None, 'seq'), may hold values from -0.125 to 0.125
- up_weight: bfloat16 [2, 2048, 6144], P(None, 'seq'), may hold values from -0.125 to 0.125
- down_weight: bfloat16 [2, 6144, 2048], P(None, 'seq'), may hold values from -0.15625 to 0.15625
Outputs:
- outputs: bfloat16 [4, 512, 2048], P('section', 'seq')
- input_grad: bfloat16 [4, 512, 2048], P('section', 'seq')
- rec_gain_grad: float32 [2, 2048], P(None, 'seq')
- in_weight_grad: float32 [2, 2048, 2560], P(None, 'seq')
- side_weight_grad: float32 [2, 2048, 2560], P(None, 'seq')
- out_weight_grad: float32 [2, 2560, 2048], P(None, 'seq')
- rate_blocks_grad: float32 [2, 10, 256, 256], P(None, None, 'seq')
- inflow_blocks_grad: float32 [2, 10, 256, 256], P(None, None, 'seq')
- rate_bias_grad: float32 [2, 2560], P(None, 'seq')
- inflow_bias_grad: float32 [2, 2560], P(None, 'seq')
- conv_taps_grad: float32 [2, 4, 2560], P(None, None, 'seq')
- conv_bias_grad: float32 [2, 2560], P(None, 'seq')
- lru_param_grad: float32 [2, 2560], P(None, 'seq')
- mlp_gain_grad: float32 [2, 2048], P(None, 'seq')
- gate_weight_grad: float32 [2, 2048, 6144], P(None, 'seq')
- up_weight_grad: float32 [2, 2048, 6144], P(None, 'seq')
- down_weight_grad: float32 [2, 6144, 2048], P(None, 'seq')
Inputs may be any that keep to these rules, and one draw needn't show every extreme that they name: `doc_starts`: each row holds two document starts in increasing order: the first on the stream's first 64 tokens, the second on its last 64 tokens; tokens before the first start continue the document of prev_state and prev_inputs.
All inputs are finite; a program needn't handle non-finite values. No bound on the sum of `valid_mask` on one device may be relied on, other than what follows from the above.
Results may differ from a plain program's by a relative error of at most 0.022.
Values may be sent and summed in bfloat16 or wider, within the bound.
A program may use at most 512 MiB of HBM per device.

v0:
```python
from functools import partial

import jax
import jax.numpy as jnp
from jax import lax
from jax.sharding import PartitionSpec as P

epsilon = 1e-06
rate_scale = 8.0


def carried_in(part, axis, combine, identity, reverse):
    count = lax.axis_size(axis)
    place = lax.axis_index(axis)
    ahead = count - 1 - place if reverse else place
    gathered = jax.tree.map(lambda a: lax.all_gather(a, axis), part)
    state = jax.tree.map(lambda a, e: jnp.zeros_like(a) + jnp.asarray(e, a.dtype), part, identity)

    def one(hop, state):
        source = count - 1 - hop if reverse else hop
        return combine(
            state, jax.tree.map(lambda a: lax.dynamic_index_in_dim(a, source, 0, False), gathered)
        )

    return lax.fori_loop(0, ahead, one, state)


def from_behind(value, axis, steps):
    count = lax.axis_size(axis)
    initial, last = (max(0, -steps), min(count, count - steps))
    return lax.ppermute(value, axis, [(source, source + steps) for source in range(initial, last)])


def rms_scale(values, gain_row):
    factor = lax.rsqrt(jnp.mean(values * values, axis=-1, keepdims=True) + epsilon)
    return values * factor * gain_row


def compose(earlier, later_pair):
    return (earlier[0] * later_pair[0], later_pair[0] * earlier[1] + later_pair[1])


def resets_at(places, starts):
    return jnp.any(places[:, None] == starts[None, :], axis=1).astype(jnp.float32)


def keep_masks(places, starts):
    first_keep = 1.0 - resets_at(places, starts)
    second_keep = first_keep * (1.0 - resets_at(places - 1, starts))
    third_keep = second_keep * (1.0 - resets_at(places - 2, starts))
    return (first_keep, second_keep, third_keep)


def lru_terms(pre_rate, pre_inflow, mixed_rows, lru_wide, resets):
    rate_gate = jax.nn.sigmoid(pre_rate)
    inflow = jax.nn.sigmoid(pre_inflow)
    log_decay = -rate_scale * rate_gate * jax.nn.softplus(-lru_wide)
    keep_state = 1.0 - resets[:, None]
    decays = jnp.exp(log_decay) * keep_state
    factor = resets[:, None] + keep_state * jnp.sqrt(-jnp.expm1(2.0 * log_decay))
    return (decays, factor * inflow * mixed_rows)


def block_product(values, blocks):
    shaped = values.reshape(values.shape[0], blocks.shape[0], blocks.shape[1])
    result = jnp.einsum("tbi,bij->tbj", shaped, blocks, preferred_element_type=jnp.float32)
    return result.reshape(values.shape[0], -1)


def block_back(gradients, blocks):
    shaped = gradients.reshape(gradients.shape[0], blocks.shape[0], blocks.shape[2])
    result = jnp.einsum("tbj,bij->tbi", shaped, blocks, preferred_element_type=jnp.float32)
    return result.reshape(gradients.shape[0], -1)


def block_outer(values, gradients, block_count):
    first_rows = values.reshape(values.shape[0], block_count, -1)
    second_rows = gradients.reshape(gradients.shape[0], block_count, -1)
    return jnp.einsum("tbi,tbj->bij", first_rows, second_rows, preferred_element_type=jnp.float32)


def contract_rows(first_rows, second_rows):
    return lax.dot_general(
        first_rows, second_rows, (((0,), (0,)), ((), ())), preferred_element_type=jnp.float32
    )


def times_transposed(first_rows, second_rows):
    return lax.dot_general(
        first_rows, second_rows, (((1,), (1,)), ((), ())), preferred_element_type=jnp.float32
    )


def plain_product(first_rows, second_rows):
    return jnp.dot(first_rows, second_rows, preferred_element_type=jnp.float32)


def guarded_dot(running, first_rows, second_rows, transposed):
    if transposed:
        out_width = second_rows.shape[0]
        product_fn = times_transposed
    else:
        out_width = second_rows.shape[1]
        product_fn = plain_product
    return lax.cond(
        running,
        lambda: product_fn(first_rows, second_rows),
        lambda: jnp.zeros((first_rows.shape[0], out_width), jnp.float32),
    )


def guarded_block(running, block_fn, values, blocks):
    return lax.cond(
        running,
        lambda: block_fn(values, blocks),
        lambda: jnp.zeros((values.shape[0], values.shape[1]), jnp.float32),
    )


def carry_forward(pair_terms):
    channel_count = pair_terms[0].shape[0]
    identity_pair = (
        jnp.ones((channel_count,), jnp.float32),
        jnp.zeros((channel_count,), jnp.float32),
    )
    return carried_in((pair_terms[0], pair_terms[1]), "seq", compose, identity_pair, False)


def carry_backward(pair_terms):
    channel_count = pair_terms[0].shape[0]
    identity_pair = (
        jnp.ones((channel_count,), jnp.float32),
        jnp.zeros((channel_count,), jnp.float32),
    )
    return carried_in((pair_terms[0], pair_terms[1]), "seq", compose, identity_pair, True)


def recurrent_forward(x_rows, weights, starts, state_init, rim_init, running):
    (
        gain_row,
        in_weight,
        side_weight,
        out_weight,
        rate_blocks,
        inflow_blocks,
        rate_bias,
        inflow_bias,
        conv_taps,
        conv_bias,
        lru_param,
    ) = weights
    token_count = x_rows.shape[0]
    seq_index = lax.axis_index("seq")
    places = seq_index * token_count + jnp.arange(token_count + 3, dtype=jnp.int32)
    first_keep, second_keep, third_keep = keep_masks(places, starts)
    resets = resets_at(places[:token_count], starts)
    x_wide = x_rows.astype(jnp.float32)
    gain_wide = gain_row.astype(jnp.float32)
    normed = rms_scale(x_wide, gain_wide).astype(jnp.bfloat16)
    inner_rows = guarded_dot(running, normed, in_weight, False).astype(jnp.bfloat16)
    branch_pre = guarded_dot(running, normed, side_weight, False)
    side_gate = jax.nn.gelu(branch_pre)
    rim_rows = from_behind(inner_rows[token_count - 3 :], "seq", 1)
    rim_rows = jnp.where(seq_index == 0, rim_init, rim_rows)
    extended = jnp.concatenate([rim_rows, inner_rows], axis=0).astype(jnp.float32)
    tap_values = conv_taps.astype(jnp.float32)
    lagged = (
        extended[3:],
        extended[2:-1] * first_keep[:token_count, None],
        extended[1:-2] * second_keep[:token_count, None],
        extended[:-3] * third_keep[:token_count, None],
    )
    mixed_rows = (
        conv_bias.astype(jnp.float32)
        + tap_values[0] * lagged[0]
        + tap_values[1] * lagged[1]
        + tap_values[2] * lagged[2]
        + tap_values[3] * lagged[3]
    )
    mixed_low = mixed_rows.astype(jnp.bfloat16)
    pre_rate = guarded_block(running, block_product, mixed_low, rate_blocks) + rate_bias.astype(
        jnp.float32
    )
    pre_inflow = guarded_block(
        running, block_product, mixed_low, inflow_blocks
    ) + inflow_bias.astype(jnp.float32)
    lru_wide = lru_param.astype(jnp.float32)
    decays, drives = lru_terms(pre_rate, pre_inflow, mixed_rows, lru_wide, resets)
    run_decay, run_state = lax.associative_scan(compose, (decays, drives), axis=0)
    prior_decay, prior_state = carry_forward((run_decay[-1], run_state[-1]))
    state_in = prior_decay * state_init + prior_state
    states = run_state + run_decay * state_in
    gated_rows = (states * side_gate).astype(jnp.bfloat16)
    branch_out = guarded_dot(running, gated_rows, out_weight, False)
    result = (x_wide + branch_out).astype(jnp.bfloat16)
    saved = (
        x_wide,
        gain_wide,
        normed,
        branch_pre,
        side_gate,
        lagged,
        (first_keep, second_keep, third_keep),
        resets,
        mixed_rows,
        mixed_low,
        pre_rate,
        pre_inflow,
        lru_wide,
        decays,
        states,
        state_in,
        gated_rows,
    )
    return (result, saved)


def recurrent_backward(x_rows, grad_rows, weights, starts, state_init, rim_init, running):
    (
        gain_row,
        in_weight,
        side_weight,
        out_weight,
        rate_blocks,
        inflow_blocks,
        rate_bias,
        inflow_bias,
        conv_taps,
        conv_bias,
        lru_param,
    ) = weights
    saved = recurrent_forward(x_rows, weights, starts, state_init, rim_init, running)[1]
    (
        x_wide,
        gain_wide,
        normed,
        branch_pre,
        side_gate,
        lagged,
        keep_rows,
        resets,
        mixed_rows,
        mixed_low,
        pre_rate,
        pre_inflow,
        lru_wide,
        decays,
        states,
        state_in,
        gated_rows,
    ) = saved
    first_keep, second_keep, third_keep = keep_rows
    token_count = x_rows.shape[0]
    grad_gated = guarded_dot(running, grad_rows, out_weight, True)
    grad_states = grad_gated * side_gate
    grad_side = grad_gated * states
    gelu_back = jax.vjp(jax.nn.gelu, branch_pre)[1]
    grad_branch = gelu_back(grad_side)[0].astype(jnp.bfloat16)
    next_decay = jnp.concatenate([decays[1:], jnp.ones_like(decays[:1])], axis=0)
    flip_decay, flip_grad = lax.associative_scan(
        compose, (jnp.flip(next_decay, 0), jnp.flip(grad_states, 0)), axis=0
    )
    after_decay = jnp.flip(flip_decay, 0)
    local_grad = jnp.flip(flip_grad, 0)
    incoming = carry_backward((decays[0] * after_decay[0], decays[0] * local_grad[0]))[1]
    grad_full = local_grad + after_decay * incoming
    prev_states = jnp.concatenate([state_in[None], states[:-1]], axis=0)
    lru_back = jax.vjp(
        partial(lru_terms, resets=resets), pre_rate, pre_inflow, mixed_rows, lru_wide
    )[1]
    grad_pre_rate, grad_pre_inflow, grad_mixed_lru, grad_lru = lru_back(
        (grad_full * prev_states, grad_full)
    )
    grad_pre_rate = grad_pre_rate.astype(jnp.bfloat16)
    grad_pre_inflow = grad_pre_inflow.astype(jnp.bfloat16)
    grad_mixed = (
        grad_mixed_lru
        + guarded_block(running, block_back, grad_pre_rate, rate_blocks)
        + guarded_block(running, block_back, grad_pre_inflow, inflow_blocks)
    ).astype(jnp.bfloat16)
    rim_back = from_behind(grad_mixed[:3], "seq", -1)
    spread = jnp.concatenate([grad_mixed, rim_back], axis=0).astype(jnp.float32)
    tap_values = conv_taps.astype(jnp.float32)
    grad_inner = (
        tap_values[0] * spread[:token_count]
        + tap_values[1] * spread[1 : token_count + 1] * first_keep[1 : token_count + 1, None]
        + tap_values[2] * spread[2 : token_count + 2] * second_keep[2 : token_count + 2, None]
        + tap_values[3] * spread[3:] * third_keep[3:, None]
    ).astype(jnp.bfloat16)
    mixed_grad = spread[:token_count]
    grad_taps = jnp.stack(
        [
            jnp.sum(mixed_grad * lagged[0], axis=0),
            jnp.sum(mixed_grad * lagged[1], axis=0),
            jnp.sum(mixed_grad * lagged[2], axis=0),
            jnp.sum(mixed_grad * lagged[3], axis=0),
        ]
    )
    grad_conv_bias = jnp.sum(mixed_grad, axis=0)
    grad_normed = guarded_dot(running, grad_inner, in_weight, True) + guarded_dot(
        running, grad_branch, side_weight, True
    )
    norm_back = jax.vjp(rms_scale, x_wide, gain_wide)[1]
    grad_x_norm, grad_gain = norm_back(grad_normed)
    grad_input = (grad_rows.astype(jnp.float32) + grad_x_norm).astype(jnp.bfloat16)
    big_rows = (
        normed,
        grad_inner,
        grad_branch,
        gated_rows,
        grad_rows,
        mixed_low,
        grad_pre_rate,
        grad_pre_inflow,
    )
    small_terms = (
        grad_gain,
        jnp.sum(grad_pre_rate.astype(jnp.float32), axis=0),
        jnp.sum(grad_pre_inflow.astype(jnp.float32), axis=0),
        grad_taps,
        grad_conv_bias,
        grad_lru,
    )
    return (grad_input, big_rows, small_terms)


def mlp_forward(x_rows, weights):
    gain_row, gate_weight, up_weight, down_weight = weights
    x_wide = x_rows.astype(jnp.float32)
    gain_wide = gain_row.astype(jnp.float32)
    normed = rms_scale(x_wide, gain_wide).astype(jnp.bfloat16)
    gate_pre = jnp.dot(normed, gate_weight, preferred_element_type=jnp.float32)
    up_pre = jnp.dot(normed, up_weight, preferred_element_type=jnp.float32)
    hidden = (jax.nn.gelu(gate_pre) * up_pre).astype(jnp.bfloat16)
    result = (x_wide + jnp.dot(hidden, down_weight, preferred_element_type=jnp.float32)).astype(
        jnp.bfloat16
    )
    return (result, (x_wide, gain_wide, normed, gate_pre, up_pre, hidden))


def mlp_backward(x_rows, grad_rows, weights):
    gain_row, gate_weight, up_weight, down_weight = weights
    x_wide, gain_wide, normed, gate_pre, up_pre, hidden = mlp_forward(x_rows, weights)[1]
    grad_hidden = times_transposed(grad_rows, down_weight)
    gelu_gate, gelu_back = jax.vjp(jax.nn.gelu, gate_pre)
    grad_gate = gelu_back(grad_hidden * up_pre)[0].astype(jnp.bfloat16)
    grad_up = (grad_hidden * gelu_gate).astype(jnp.bfloat16)
    grad_normed = times_transposed(grad_gate, gate_weight) + times_transposed(grad_up, up_weight)
    norm_back = jax.vjp(rms_scale, x_wide, gain_wide)[1]
    grad_x_norm, grad_gain = norm_back(grad_normed)
    grad_input = (grad_rows.astype(jnp.float32) + grad_x_norm).astype(jnp.bfloat16)
    return (grad_input, (normed, grad_gate, grad_up, hidden, grad_rows), (grad_gain,))


def on_device(
    inputs,
    doc_starts,
    valid_mask,
    cotangent,
    prev_state,
    prev_inputs,
    rec_gain,
    in_weight,
    side_weight,
    out_weight,
    rate_blocks,
    inflow_blocks,
    rate_bias,
    inflow_bias,
    conv_taps,
    conv_bias,
    lru_param,
    mlp_gain,
    gate_weight,
    up_weight,
    down_weight,
):
    micro_count = inputs.shape[0]
    token_count = inputs.shape[1]
    model_width = inputs.shape[2]
    lru_width = in_weight.shape[2]
    hidden_width = gate_weight.shape[2]
    layer_count = rec_gain.shape[0]
    section_count = lax.axis_size("section")
    section_index = lax.axis_index("section")
    layer_index = section_index // 2
    is_recurrent = section_index % 2 == 0
    is_feedforward = jnp.logical_not(is_recurrent)
    tick_total = micro_count + section_count - 1
    rec_args = (
        rec_gain,
        in_weight,
        side_weight,
        out_weight,
        rate_blocks,
        inflow_blocks,
        rate_bias,
        inflow_bias,
        conv_taps,
        conv_bias,
        lru_param,
    )
    mlp_args = (mlp_gain, gate_weight, up_weight, down_weight)
    rec_local = tuple(
        (
            lax.dynamic_index_in_dim(shard_piece, layer_index, 0, keepdims=False)
            for shard_piece in rec_args
        )
    )
    mlp_local = tuple(
        (
            lax.dynamic_index_in_dim(shard_piece, layer_index, 0, keepdims=False)
            for shard_piece in mlp_args
        )
    )
    (
        gain_part,
        in_part,
        side_part,
        out_part,
        rate_part,
        inflow_part,
        rate_bias_part,
        inflow_bias_part,
        taps_part,
        conv_bias_part,
        lru_part,
    ) = rec_local
    mlp_gain_part, gate_part, up_part, down_part = mlp_local

    def fetch_weights():
        rec_gathered = (
            lax.all_gather(gain_part, "seq", axis=0, tiled=True),
            lax.all_gather(in_part, "seq", axis=0, tiled=True),
            lax.all_gather(side_part, "seq", axis=0, tiled=True),
            lax.all_gather(out_part, "seq", axis=0, tiled=True),
            lax.all_gather(rate_part, "seq", axis=1, tiled=True),
            lax.all_gather(inflow_part, "seq", axis=1, tiled=True),
            lax.all_gather(rate_bias_part, "seq", axis=0, tiled=True),
            lax.all_gather(inflow_bias_part, "seq", axis=0, tiled=True),
            lax.all_gather(taps_part, "seq", axis=1, tiled=True),
            lax.all_gather(conv_bias_part, "seq", axis=0, tiled=True),
            lax.all_gather(lru_part, "seq", axis=0, tiled=True),
        )
        mlp_gathered = (
            lax.all_gather(mlp_gain_part, "seq", axis=0, tiled=True),
            lax.all_gather(gate_part, "seq", axis=0, tiled=True),
            lax.all_gather(up_part, "seq", axis=0, tiled=True),
            lax.all_gather(down_part, "seq", axis=0, tiled=True),
        )
        return (tuple(rec_gathered), tuple(mlp_gathered))

    def section_forward(rows_in, slot_index, weights, active):
        rec_running = jnp.logical_and(active, is_recurrent)
        mlp_running = jnp.logical_and(active, is_feedforward)
        rec_out = recurrent_forward(
            rows_in,
            weights[0],
            doc_starts[slot_index],
            prev_state[slot_index, layer_index].astype(jnp.float32),
            prev_inputs[slot_index, layer_index],
            rec_running,
        )[0]
        mlp_out = lax.cond(
            mlp_running,
            lambda: mlp_forward(rows_in, weights[1])[0],
            lambda: jnp.zeros_like(rows_in),
        )
        return jnp.where(active, jnp.where(is_recurrent, rec_out, mlp_out), jnp.zeros_like(rows_in))

    weights_now = fetch_weights()

    def forward_tick(carried, tick_index):
        kept_inputs, finals, arriving = carried
        batch_index = tick_index - section_index
        active = jnp.logical_and(batch_index >= 0, batch_index < micro_count)
        slot_index = jnp.clip(batch_index, 0, micro_count - 1)
        entering = jnp.where(section_index == 0, inputs[slot_index], arriving)
        leaving = section_forward(entering, slot_index, weights_now, active)
        kept_inputs = lax.dynamic_update_index_in_dim(
            kept_inputs, jnp.where(active, entering, kept_inputs[slot_index]), slot_index, 0
        )
        last_active = jnp.logical_and(active, section_index == section_count - 1)
        finals = lax.dynamic_update_index_in_dim(
            finals, jnp.where(last_active, leaving, finals[slot_index]), slot_index, 0
        )
        arriving = from_behind(leaving, "section", 1)
        return ((kept_inputs, finals, arriving), None)

    forward_init = (jnp.zeros_like(inputs), jnp.zeros_like(inputs), jnp.zeros_like(inputs[0]))
    kept_inputs, finals, arriving = lax.scan(
        forward_tick, forward_init, jnp.arange(tick_total, dtype=jnp.int32)
    )[0]
    weights_back = fetch_weights()
    masked = (cotangent.astype(jnp.float32) * valid_mask[:, :, None].astype(jnp.float32)).astype(
        jnp.bfloat16
    )
    rec_widths = (
        model_width,
        lru_width,
        lru_width,
        lru_width,
        model_width,
        lru_width,
        lru_width,
        lru_width,
    )
    mlp_widths = (model_width, hidden_width, hidden_width, hidden_width, model_width)
    rec_big = tuple(
        (
            jnp.zeros((micro_count, token_count, lane_width), jnp.bfloat16)
            for lane_width in rec_widths
        )
    )
    mlp_big = tuple(
        (
            jnp.zeros((micro_count, token_count, lane_width), jnp.bfloat16)
            for lane_width in mlp_widths
        )
    )
    rec_small = (
        jnp.zeros((model_width,), jnp.float32),
        jnp.zeros((lru_width,), jnp.float32),
        jnp.zeros((lru_width,), jnp.float32),
        jnp.zeros((4, lru_width), jnp.float32),
        jnp.zeros((lru_width,), jnp.float32),
        jnp.zeros((lru_width,), jnp.float32),
    )
    mlp_small = (jnp.zeros((model_width,), jnp.float32),)

    def section_backward(rows_in, grad_in, slot_index, weights, stores, active):
        rec_running = jnp.logical_and(active, is_recurrent)
        mlp_running = jnp.logical_and(active, is_feedforward)
        rec_grad, big_rows, small_terms = recurrent_backward(
            rows_in,
            grad_in,
            weights[0],
            doc_starts[slot_index],
            prev_state[slot_index, layer_index].astype(jnp.float32),
            prev_inputs[slot_index, layer_index],
            rec_running,
        )
        rec_big_new = tuple(
            (
                lax.dynamic_update_index_in_dim(
                    buffer, jnp.where(rec_running, written, buffer[slot_index]), slot_index, 0
                )
                for buffer, written in zip(stores[0], big_rows)
            )
        )
        rec_small_new = tuple(
            (
                running_sum + jnp.where(rec_running, addend, jnp.zeros_like(addend))
                for running_sum, addend in zip(stores[1], small_terms)
            )
        )

        def run_mlp():
            grad_input, mlp_rows, mlp_terms = mlp_backward(rows_in, grad_in, weights[1])
            new_big = tuple(
                (
                    lax.dynamic_update_index_in_dim(buffer, written, slot_index, 0)
                    for buffer, written in zip(stores[2], mlp_rows)
                )
            )
            new_small = tuple(
                (running_sum + addend for running_sum, addend in zip(stores[3], mlp_terms))
            )
            return (grad_input, new_big, new_small)

        def skip_mlp():
            return (jnp.zeros_like(grad_in), stores[2], stores[3])

        mlp_grad, mlp_big_new, mlp_small_new = lax.cond(mlp_running, run_mlp, skip_mlp)
        grad_out = jnp.where(
            active, jnp.where(is_recurrent, rec_grad, mlp_grad), jnp.zeros_like(grad_in)
        )
        return (grad_out, (rec_big_new, rec_small_new, mlp_big_new, mlp_small_new))

    def backward_tick(carried, tick_index):
        stores, back_rows, returning = carried
        batch_index = tick_index - (section_count - 1 - section_index)
        active = jnp.logical_and(batch_index >= 0, batch_index < micro_count)
        slot_index = jnp.clip(batch_index, 0, micro_count - 1)
        incoming_grad = jnp.where(section_index == section_count - 1, masked[slot_index], returning)
        rows_in = kept_inputs[slot_index]
        grad_out, stores = section_backward(
            rows_in, incoming_grad, slot_index, weights_back, stores, active
        )
        first_active = jnp.logical_and(active, section_index == 0)
        back_rows = lax.dynamic_update_index_in_dim(
            back_rows, jnp.where(first_active, grad_out, back_rows[slot_index]), slot_index, 0
        )
        returning = from_behind(grad_out, "section", -1)
        return ((stores, back_rows, returning), None)

    backward_init = (
        (rec_big, rec_small, mlp_big, mlp_small),
        jnp.zeros_like(inputs),
        jnp.zeros_like(inputs[0]),
    )
    stores, back_rows, returning = lax.scan(
        backward_tick, backward_init, jnp.arange(tick_total, dtype=jnp.int32)
    )[0]

    def place_layer(shares):
        return tuple(
            (
                lax.dynamic_update_index_in_dim(
                    jnp.zeros((layer_count,) + share_part.shape, jnp.float32),
                    share_part,
                    layer_index,
                    0,
                )
                for share_part in shares
            )
        )

    rec_zero_terms = tuple(
        (jnp.zeros(whole_piece.shape, jnp.float32) for whole_piece in weights_back[0])
    )
    mlp_zero_terms = tuple(
        (jnp.zeros(whole_piece.shape, jnp.float32) for whole_piece in weights_back[1])
    )

    def rec_terms():
        flat_rows = tuple(
            (buffer.reshape(micro_count * token_count, buffer.shape[2]) for buffer in stores[0])
        )
        (
            normed_all,
            inner_all,
            branch_all,
            gated_all,
            grad_out_all,
            mixed_all,
            rate_all,
            inflow_all,
        ) = flat_rows
        grad_gain, grad_rate_bias, grad_inflow_bias, grad_taps, grad_conv_bias, grad_lru = stores[1]
        block_count = rate_blocks.shape[1]
        return (
            grad_gain,
            contract_rows(normed_all, inner_all),
            contract_rows(normed_all, branch_all),
            contract_rows(gated_all, grad_out_all),
            block_outer(mixed_all, rate_all, block_count),
            block_outer(mixed_all, inflow_all, block_count),
            grad_rate_bias,
            grad_inflow_bias,
            grad_taps,
            grad_conv_bias,
            grad_lru,
        )

    def mlp_terms():
        flat_rows = tuple(
            (buffer.reshape(micro_count * token_count, buffer.shape[2]) for buffer in stores[2])
        )
        normed_all, gate_all, up_all, hidden_all, grad_out_all = flat_rows
        return (
            stores[3][0],
            contract_rows(normed_all, gate_all),
            contract_rows(normed_all, up_all),
            contract_rows(hidden_all, grad_out_all),
        )

    rec_pieces = lax.cond(is_recurrent, rec_terms, lambda: rec_zero_terms)
    mlp_pieces = lax.cond(is_feedforward, mlp_terms, lambda: mlp_zero_terms)
    rec_shares = (
        lax.psum_scatter(
            rec_pieces[0].astype(jnp.bfloat16), "seq", scatter_dimension=0, tiled=True
        ).astype(jnp.float32),
        lax.psum_scatter(
            rec_pieces[1].astype(jnp.bfloat16), "seq", scatter_dimension=0, tiled=True
        ).astype(jnp.float32),
        lax.psum_scatter(
            rec_pieces[2].astype(jnp.bfloat16), "seq", scatter_dimension=0, tiled=True
        ).astype(jnp.float32),
        lax.psum_scatter(
            rec_pieces[3].astype(jnp.bfloat16), "seq", scatter_dimension=0, tiled=True
        ).astype(jnp.float32),
        lax.psum_scatter(
            rec_pieces[4].astype(jnp.bfloat16), "seq", scatter_dimension=1, tiled=True
        ).astype(jnp.float32),
        lax.psum_scatter(
            rec_pieces[5].astype(jnp.bfloat16), "seq", scatter_dimension=1, tiled=True
        ).astype(jnp.float32),
        lax.psum_scatter(
            rec_pieces[6].astype(jnp.bfloat16), "seq", scatter_dimension=0, tiled=True
        ).astype(jnp.float32),
        lax.psum_scatter(
            rec_pieces[7].astype(jnp.bfloat16), "seq", scatter_dimension=0, tiled=True
        ).astype(jnp.float32),
        lax.psum_scatter(
            rec_pieces[8].astype(jnp.bfloat16), "seq", scatter_dimension=1, tiled=True
        ).astype(jnp.float32),
        lax.psum_scatter(
            rec_pieces[9].astype(jnp.bfloat16), "seq", scatter_dimension=0, tiled=True
        ).astype(jnp.float32),
        lax.psum_scatter(
            rec_pieces[10].astype(jnp.bfloat16), "seq", scatter_dimension=0, tiled=True
        ).astype(jnp.float32),
    )
    mlp_shares = (
        lax.psum_scatter(
            mlp_pieces[0].astype(jnp.bfloat16), "seq", scatter_dimension=0, tiled=True
        ).astype(jnp.float32),
        lax.psum_scatter(
            mlp_pieces[1].astype(jnp.bfloat16), "seq", scatter_dimension=0, tiled=True
        ).astype(jnp.float32),
        lax.psum_scatter(
            mlp_pieces[2].astype(jnp.bfloat16), "seq", scatter_dimension=0, tiled=True
        ).astype(jnp.float32),
        lax.psum_scatter(
            mlp_pieces[3].astype(jnp.bfloat16), "seq", scatter_dimension=0, tiled=True
        ).astype(jnp.float32),
    )
    rec_sums = place_layer(rec_shares)
    mlp_sums = place_layer(mlp_shares)
    (
        sum_rec_gain,
        sum_in_weight,
        sum_side_weight,
        sum_out_weight,
        sum_rate_blocks,
        sum_inflow_blocks,
        sum_rate_bias,
        sum_inflow_bias,
        sum_conv_taps,
        sum_conv_bias,
        sum_lru_param,
    ) = rec_sums
    sum_mlp_gain, sum_gate_weight, sum_up_weight, sum_down_weight = mlp_sums
    totals = (
        lax.psum(sum_rec_gain.astype(jnp.bfloat16), "section").astype(jnp.float32),
        lax.psum(sum_in_weight.astype(jnp.bfloat16), "section").astype(jnp.float32),
        lax.psum(sum_side_weight.astype(jnp.bfloat16), "section").astype(jnp.float32),
        lax.psum(sum_out_weight.astype(jnp.bfloat16), "section").astype(jnp.float32),
        lax.psum(sum_rate_blocks.astype(jnp.bfloat16), "section").astype(jnp.float32),
        lax.psum(sum_inflow_blocks.astype(jnp.bfloat16), "section").astype(jnp.float32),
        lax.psum(sum_rate_bias.astype(jnp.bfloat16), "section").astype(jnp.float32),
        lax.psum(sum_inflow_bias.astype(jnp.bfloat16), "section").astype(jnp.float32),
        lax.psum(sum_conv_taps.astype(jnp.bfloat16), "section").astype(jnp.float32),
        lax.psum(sum_conv_bias.astype(jnp.bfloat16), "section").astype(jnp.float32),
        lax.psum(sum_lru_param.astype(jnp.bfloat16), "section").astype(jnp.float32),
        lax.psum(sum_mlp_gain.astype(jnp.bfloat16), "section").astype(jnp.float32),
        lax.psum(sum_gate_weight.astype(jnp.bfloat16), "section").astype(jnp.float32),
        lax.psum(sum_up_weight.astype(jnp.bfloat16), "section").astype(jnp.float32),
        lax.psum(sum_down_weight.astype(jnp.bfloat16), "section").astype(jnp.float32),
    )
    delivered = (
        lax.all_to_all(finals, "section", split_axis=0, concat_axis=0, tiled=True),
        lax.all_to_all(back_rows, "section", split_axis=0, concat_axis=0, tiled=True),
    )
    outputs = delivered[0][section_count - 1 : section_count]
    input_grad = delivered[1][0:1]
    return (outputs, input_grad) + tuple(totals)


def solution(mesh):
    return jax.shard_map(
        on_device,
        mesh=mesh,
        in_specs=(
            P(None, "seq", None),
            P(),
            P(None, "seq"),
            P(None, "seq", None),
            P(),
            P(),
            P(None, "seq"),
            P(None, "seq", None),
            P(None, "seq", None),
            P(None, "seq", None),
            P(None, None, "seq", None),
            P(None, None, "seq", None),
            P(None, "seq"),
            P(None, "seq"),
            P(None, None, "seq"),
            P(None, "seq"),
            P(None, "seq"),
            P(None, "seq"),
            P(None, "seq", None),
            P(None, "seq", None),
            P(None, "seq", None),
        ),
        out_specs=(
            P("section", "seq", None),
            P("section", "seq", None),
            P(None, "seq"),
            P(None, "seq", None),
            P(None, "seq", None),
            P(None, "seq", None),
            P(None, None, "seq", None),
            P(None, None, "seq", None),
            P(None, "seq"),
            P(None, "seq"),
            P(None, None, "seq"),
            P(None, "seq"),
            P(None, "seq"),
            P(None, "seq"),
            P(None, "seq", None),
            P(None, "seq", None),
            P(None, "seq", None),
        ),
        check_vma=False,
    )
```

profile of v0, /device:TPU:18, one launch (start us, length us, event | category | flops | bytes accessed | tf_op | source)
XLA Modules:
  0.0 6982.5 jit_solution(18107523180342499829)
XLA Ops:
  70.7 34.3 all-reduce.85
  106.3 53.8 all-gather.46.cloned.1.call-done
  160.1 99.9 %all-gather.52.cloned.1.call-done = bf16[1,2048,2560]{2,1,0:T(8,128)(2,1)} async-done(((bf16[1,256,2560]{2,1,0:T(8,128)(2,1)}), bf16[1,2048,2560]{2,1,0:T(8,128)(2,1)}) %all-gather.52.cloned.1.call-update) | async-done | bytes 10485776 | tf_op jit(solution)/shard_map/all_gather | solution.py:435
  260.0 99.9 %all-gather.54.cloned.1.call-done = bf16[1,2560,2048]{2,1,0:T(8,128)(2,1)} async-done(((bf16[1,320,2048]{2,1,0:T(8,128)(2,1)}), bf16[1,2560,2048]{2,1,0:T(8,128)(2,1)}) %all-gather.54.cloned.1.call-update) | async-done | bytes 10485776 | tf_op jit(solution)/shard_map/all_gather | solution.py:436
  359.8 220.2 %all-gather.56.cloned.1.call-done = bf16[1,2048,6144]{2,1,0:T(8,128)(2,1)} async-done(((bf16[1,256,6144]{2,1,0:T(8,128)(2,1)}), bf16[1,2048,6144]{2,1,0:T(8,128)(2,1)}) %all-gather.56.cloned.1.call-update) | async-done | bytes 25165840 | tf_op jit(solution)/shard_map/all_gather | solution.py:447
  580.0 220.3 %all-gather.58.cloned.1.call-done = bf16[1,2048,6144]{2,1,0:T(8,128)(2,1)} async-done(((bf16[1,256,6144]{2,1,0:T(8,128)(2,1)}), bf16[1,2048,6144]{2,1,0:T(8,128)(2,1)}) %all-gather.58.cloned.1.call-update) | async-done | bytes 25165840 | tf_op jit(solution)/shard_map/all_gather | solution.py:448
  800.3 220.3 %all-gather.60.cloned.1.call-done = bf16[1,6144,2048]{2,1,0:T(8,128)(2,1)} async-done(((bf16[1,768,2048]{2,1,0:T(8,128)(2,1)}), bf16[1,6144,2048]{2,1,0:T(8,128)(2,1)}) %all-gather.60.cloned.1.call-update) | async-done | bytes 25165840 | tf_op jit(solution)/shard_map/all_gather | solution.py:449
  1022.8 792.7 %while.142 = (s32[]{:T(128)}, bf16[4,64,2048]{2,1,0:T(8,128)(2,1)}, bf16[4,64,2048]{2,1,0:T(8,128)(2,1)}, bf16[64,2048]{1,0:T(8,128)(2,1)S(1)}, s32[7]{0:T(128)S...) while((s32[]{:T(128)}, bf16[4,64,2048]{2,1,0:T(8,128)(2,1)}, ...), condition=%wide.region_21.22_spmd, body=%wide.region_0.21_spmd.sunk | while | flops 7030099456 | bytes 191723824 | solution.py:491
  1834.6 3396.8 %while.145 = (s32[]{:T(128)}, bf16[4,64,2048]{2,1,0:T(8,128)(2,1)}, bf16[4,64,2560]{2,1,0:T(8,128)(2,1)}, bf16[4,64,2560]{2,1,0:T(8,128)(2,1)}, bf16[4,64,2560]{...) while((s32[]{:T(128)}, bf16[4,64,2048]{2,1,0:T(8,128)(2,1)}, ...), condition=%wide.region_65.66_spmd.clone, body=%wide.region_22.65_spmd.clone.sunk | while | flops 11797250048 | bytes 401202304 | solution.py:602
  2253.8 35.9 collective-permute-done.2
  2707.8 107.5 %collective-permute-done.2 = bf16[64,2048]{1,0:T(8,128)(2,1)S(1)} collective-permute-done((bf16[64,2048]{1,0:T(8,128)(2,1)S(1)}, bf16[64,2048]{1,0:T(8,128)(2,1)S(1)}, u32[]{:S(2)}, u32[]{:S(2)}) %collective-permute-start.2) | collective-permute-done | bytes 262176 | tf_op jit(solution)/shard_map/while/body/eval_jaxpr/ppermute | solution.py:31
  2858.4 69.7 conditional.52
  3345.1 69.6 conditional.52
  3831.4 69.7 conditional.52
  4318.1 69.6 conditional.52
  5177.4 41.2 collective-permute-start.2
  5255.9 41.7 conditional.19
  5336.8 113.6 %reduce-scatter.16.cloned.1.call-done = bf16[320,2048]{1,0:T(8,128)(2,1)} async-done(((bf16[2560,2048]{1,0:T(8,128)(2,1)}), bf16[320,2048]{1,0:T(8,128)(2,1)}) %reduce-scatter.16.cloned.1.call-update) | async-done | bytes 1310736 | tf_op jit(solution)/shard_map/reduce_scatter | solution.py:680
  5451.9 109.0 %reduce-scatter.14.cloned.1.call-done = bf16[256,2560]{1,0:T(8,128)(2,1)} async-done(((bf16[2048,2560]{1,0:T(8,128)(2,1)}), bf16[256,2560]{1,0:T(8,128)(2,1)}) %reduce-scatter.14.cloned.1.call-update) | async-done | bytes 1310736 | tf_op jit(solution)/shard_map/reduce_scatter | solution.py:677
  5563.9 107.7 %reduce-scatter.12.cloned.1.call-done = bf16[256,2560]{1,0:T(8,128)(2,1)} async-done(((bf16[2048,2560]{1,0:T(8,128)(2,1)}), bf16[256,2560]{1,0:T(8,128)(2,1)}) %reduce-scatter.12.cloned.1.call-update) | async-done | bytes 1310736 | tf_op jit(solution)/shard_map/reduce_scatter | solution.py:674
  5673.1 246.3 %reduce-scatter.24.cloned.1.call-done = bf16[256,6144]{1,0:T(8,128)(2,1)} async-done(((bf16[2048,6144]{1,0:T(8,128)(2,1)}), bf16[256,6144]{1,0:T(8,128)(2,1)}) %reduce-scatter.24.cloned.1.call-update) | async-done | bytes 3145744 | tf_op jit(solution)/shard_map/reduce_scatter | solution.py:712
  5924.8 242.4 %reduce-scatter.22.cloned.1.call-done = bf16[256,6144]{1,0:T(8,128)(2,1)} async-done(((bf16[2048,6144]{1,0:T(8,128)(2,1)}), bf16[256,6144]{1,0:T(8,128)(2,1)}) %reduce-scatter.22.cloned.1.call-update) | async-done | bytes 3145744 | tf_op jit(solution)/shard_map/reduce_scatter | solution.py:709
  6172.5 242.4 %reduce-scatter.26.cloned.1.call-done = bf16[768,2048]{1,0:T(8,128)(2,1)} async-done(((bf16[6144,2048]{1,0:T(8,128)(2,1)}), bf16[768,2048]{1,0:T(8,128)(2,1)}) %reduce-scatter.26.cloned.1.call-update) | async-done | bytes 3145744 | tf_op jit(solution)/shard_map/reduce_scatter | solution.py:715
  6486.4 455.7 %all-reduce.90.cloned.1.call-done = (bf16[2,256,2560]{2,1,0:T(8,128)(2,1)}, bf16[2,256,2560]{2,1,0:T(8,128)(2,1)}, bf16[2,320,2048]{2,1,0:T(8,128)(2,1)}, bf16[2...) async-done(((bf16[2,256,2560]{2,1,0:T(8,128)(2,1)}, ...) | async-done | bytes 27394064 | tf_op jit(solution)/shard_map/psum | solution.py:737
  (5049 shorter events, 4447.7 us)
Async XLA Ops:
  7.2 99.1 %all-gather.48.cloned.1.call-start = ((), (), s32[]{:S(2)}) async-start(), calls=%async_computation.20 | async-start | bytes 1474560 | tf_op jit(solution)/shard_map/all_gather | solution.py:437
  9.0 97.2 %all-gather.50.cloned.1.call-start = ((), (), s32[]{:S(2)}) async-start(), calls=%async_computation.21 | async-start | bytes 1474560 | tf_op jit(solution)/shard_map/all_gather | solution.py:438
  10.7 149.4 %all-gather.46.cloned.1.call-start = ((), (), s32[]{:S(2)}) async-start(), calls=%async_computation.19 | async-start | bytes 11796480 | tf_op jit(solution)/shard_map/all_gather | solution.py:434
  12.0 248.0 %all-gather.52.cloned.1.call-start = ((), (), s32[]{:S(2)}) async-start(), calls=%async_computation.22 | async-start | bytes 11796480 | tf_op jit(solution)/shard_map/all_gather | solution.py:435
  14.6 345.2 %all-gather.54.cloned.1.call-start = ((), (), s32[]{:S(2)}) async-start(), calls=%async_computation.23 | async-start | bytes 11796480 | tf_op jit(solution)/shard_map/all_gather | solution.py:436
  15.9 564.1 %all-gather.56.cloned.1.call-start = ((), (), s32[]{:S(2)}) async-start(), calls=%async_computation.24 | async-start | bytes 28311552 | tf_op jit(solution)/shard_map/all_gather | solution.py:447
  19.9 780.4 %all-gather.58.cloned.1.call-start = ((), (), s32[]{:S(2)}) async-start(), calls=%async_computation.25 | async-start | bytes 28311552 | tf_op jit(solution)/shard_map/all_gather | solution.py:448
  23.9 996.7 %all-gather.60.cloned.1.call-start = ((), (), s32[]{:S(2)}) async-start(), calls=%async_computation.26 | async-start | bytes 28311552 | tf_op jit(solution)/shard_map/all_gather | solution.py:449
  28.1 5274.2 %reduce-scatter.20.cloned.1.call-start = ((), (), s32[]{:S(2)}) async-start(), calls=%async_computation.15 | async-start | bytes 1474560 | tf_op jit(solution)/shard_map/reduce_scatter | solution.py:686
  2293.6 49.9 collective-permute-start
  2705.7 109.6 %collective-permute-start.2 = (bf16[64,2048]{1,0:T(8,128)(2,1)S(1)}, bf16[64,2048]{1,0:T(8,128)(2,1)S(1)}, u32[]{:S(2)}, u32[]{:S(2)}) collective-permute-start(bf16[64,2048]{1,0:T(8,128)(2,1)S(1)} %get-tuple-element.3505), channel_id=1, source_target_pairs={{8,0},{16,8},{24,16},{9,1},{17,9},{25,17},{10,2},{18,10},{26,18},{... | collective-permute-start | bytes 786440 | tf_op jit(solution)/shard_map/while/body/eval_jaxpr/ppermute | solution.py:31
  2819.3 110.2 %collective-permute-start = (bf16[3,2560]{1,0:T(4,128)(2,1)S(1)}, bf16[3,2560]{1,0:T(4,128)(2,1)S(1)}, u32[]{:S(2)}, u32[]{:S(2)}) collective-permute-start(bf16[3,2560]{1,0:T(4,128)(2,1)S(1)} %slice.2090), channel_id=1, source_target_pairs={{0,1},{1,2},{2,3},{3,4},{4,5},{5,6},{6,7},{8,9},{9,10},{10,11},{11... | collective-permute-start | bytes 46088 | tf_op jit(solution)/shard_map/while/body/eval_jaxpr/ppermute | solution.py:31
  3306.0 110.1 %collective-permute-start = (bf16[3,2560]{1,0:T(4,128)(2,1)S(1)}, bf16[3,2560]{1,0:T(4,128)(2,1)S(1)}, u32[]{:S(2)}, u32[]{:S(2)}) collective-permute-start(bf16[3,2560]{1,0:T(4,128)(2,1)S(1)} %slice.2090), channel_id=1, source_target_pairs={{0,1},{1,2},{2,3},{3,4},{4,5},{5,6},{6,7},{8,9},{9,10},{10,11},{11... | collective-permute-start | bytes 46088 | tf_op jit(solution)/shard_map/while/body/eval_jaxpr/ppermute | solution.py:31
  3792.2 110.2 %collective-permute-start = (bf16[3,2560]{1,0:T(4,128)(2,1)S(1)}, bf16[3,2560]{1,0:T(4,128)(2,1)S(1)}, u32[]{:S(2)}, u32[]{:S(2)}) collective-permute-start(bf16[3,2560]{1,0:T(4,128)(2,1)S(1)} %slice.2090), channel_id=1, source_target_pairs={{0,1},{1,2},{2,3},{3,4},{4,5},{5,6},{6,7},{8,9},{9,10},{10,11},{11... | collective-permute-start | bytes 46088 | tf_op jit(solution)/shard_map/while/body/eval_jaxpr/ppermute | solution.py:31
  4278.9 110.1 %collective-permute-start = (bf16[3,2560]{1,0:T(4,128)(2,1)S(1)}, bf16[3,2560]{1,0:T(4,128)(2,1)S(1)}, u32[]{:S(2)}, u32[]{:S(2)}) collective-permute-start(bf16[3,2560]{1,0:T(4,128)(2,1)S(1)} %slice.2090), channel_id=1, source_target_pairs={{0,1},{1,2},{2,3},{3,4},{4,5},{5,6},{6,7},{8,9},{9,10},{10,11},{11... | collective-permute-start | bytes 46088 | tf_op jit(solution)/shard_map/while/body/eval_jaxpr/ppermute | solution.py:31
  5252.4 83.4 %reduce-scatter.18.cloned.1.call-start = ((), (), s32[]{:S(2)}) async-start(), calls=%async_computation.14 | async-start | bytes 1474560 | tf_op jit(solution)/shard_map/reduce_scatter | solution.py:683
  5253.0 197.4 %reduce-scatter.16.cloned.1.call-start = ((), (), s32[]{:S(2)}) async-start(), calls=%async_computation.13 | async-start | bytes 11796480 | tf_op jit(solution)/shard_map/reduce_scatter | solution.py:680
  5253.8 307.2 %reduce-scatter.14.cloned.1.call-start = ((), (), s32[]{:S(2)}) async-start(), calls=%async_computation.12 | async-start | bytes 11796480 | tf_op jit(solution)/shard_map/reduce_scatter | solution.py:677
  5254.3 417.3 %reduce-scatter.12.cloned.1.call-start = ((), (), s32[]{:S(2)}) async-start(), calls=%async_computation.11 | async-start | bytes 11796480 | tf_op jit(solution)/shard_map/reduce_scatter | solution.py:674
  5255.1 664.4 %reduce-scatter.24.cloned.1.call-start = ((), (), s32[]{:S(2)}) async-start(), calls=%async_computation.17 | async-start | bytes 28311552 | tf_op jit(solution)/shard_map/reduce_scatter | solution.py:712
  5297.7 869.5 %reduce-scatter.22.cloned.1.call-start = ((), (), s32[]{:S(2)}) async-start(), calls=%async_computation.16 | async-start | bytes 28311552 | tf_op jit(solution)/shard_map/reduce_scatter | solution.py:709
  5298.3 1116.7 %reduce-scatter.26.cloned.1.call-start = ((), (), s32[]{:S(2)}) async-start(), calls=%async_computation.18 | async-start | bytes 28311552 | tf_op jit(solution)/shard_map/reduce_scatter | solution.py:715
  5298.9 1166.6 %reduce-scatter.28.cloned.1.call-start = ((), (), s32[]{:S(2)}) async-start(), calls=%async_computation.27 | async-start | bytes 737280
  5300.3 1641.9 %all-reduce.90.cloned.1.call-start = ((), (), s32[]{:S(2)}) async-start(), calls=%async_computation.28 | async-start | bytes 54788096 | tf_op jit(solution)/shard_map/psum | solution.py:737
  (852 other events, 14724.3 us)
Sparse Core Ops, SparseCore 0:
  10.2 23.5 all-gather.47
  36.0 23.0 all-gather.49
  61.3 98.6 all-gather.45
  162.2 97.7 all-gather.51
  262.0 97.7 all-gather.53
  361.9 218.0 all-gather.55
  582.2 218.0 all-gather.57
  802.5 218.0 all-gather.59
  5252.6 49.6 reduce-scatter.19
  5304.4 31.3 reduce-scatter.17
  5338.7 111.6 reduce-scatter.15
  5453.2 107.7 reduce-scatter.13
  5563.8 107.7 reduce-scatter.11
  5673.8 245.5 reduce-scatter.23
  5921.6 245.5 reduce-scatter.21
  6169.4 245.5 reduce-scatter.25
  6417.7 25.9 reduce-scatter.27
  6449.8 492.2 all-reduce.89
where the time goes:
time: 7060 us; the launch traced here: 6980 us
  waiting for transfers between devices  2720 us (39%)
  local copies, waits for them, and re-layouts  1900 us (27%)
  other arithmetic  975 us (14%)
  blocking collectives  714 us (10%)
  matrix products  431 us (6%)
  starting transfers between devices  162 us (2%)
    slice x287, local copies, waits for them, and re-layouts, recurrent_backward(): lax.associative_scan(compose, (jnp.flip(next_decay, 0), jnp.flip(grad_sta...  611 us
    all_gather x42, blocking collectives, carried_in(): gathered = jax.tree.map(lambda a: lax.all_gather(a, axis), part)  590 us
    psum x1, waiting for transfers between devices, on_device(): lax.psum(sum_in_weight.astype(jnp.bfloat16), 'section').astype(jnp.float32)  456 us
    slice x497, local copies, waits for them, and re-layouts, recurrent_forward(): lax.associative_scan(compose, (decays, drives), axis=0)  404 us
    ppermute x35, waiting for transfers between devices, from_behind(): lax.ppermute(value, axis, [(source, source + steps) for source in range(i...  248 us
    reduce_scatter x1, waiting for transfers between devices, on_device(): lax.psum_scatter(mlp_pieces[2].astype(jnp.bfloat16), 'seq', scatter_dimen...  246 us
    reduce_scatter x1, waiting for transfers between devices, on_device(): lax.psum_scatter(mlp_pieces[3].astype(jnp.bfloat16), 'seq', scatter_dimen...  242 us
    reduce_scatter x1, waiting for transfers between devices, on_device(): lax.psum_scatter(mlp_pieces[1].astype(jnp.bfloat16), 'seq', scatter_dimen...  242 us

commit v1 on v0

v1 whole, which is shorter than its diff:
```python
from functools import partial

import jax
import jax.numpy as jnp
import numpy as np
from jax import lax
from jax.experimental import pallas as pl
from jax.experimental.pallas import tpu as pltpu
from jax.sharding import PartitionSpec as P


epsilon = 1e-06
rate_scale = 8.0
MESH = pl.DeviceIdType.MESH
VMEM_LIMIT = 60 * 1024 * 1024
f32 = jnp.float32
bf16 = jnp.bfloat16


def line_place():
    place = lax.axis_index("seq")
    chip = place // 2
    core = place % 2
    return place, chip, core, chip * 2 + 1 - core


def enter(chips, mate):
    _, chip, core, _ = line_place()
    barrier = pltpu.get_barrier_semaphore()
    pl.semaphore_signal(barrier, inc=1, device_id={"seq": mate}, device_id_type=MESH)
    for k in range(1, chips):
        peer = ((chip + k) % chips) * 2 + core
        pl.semaphore_signal(barrier, inc=1, device_id={"seq": peer}, device_id_type=MESH)
    pl.semaphore_wait(barrier, chips)


def exchange_body(mode, count, refs):
    chips = count // 2
    has_sum = mode != "start"
    has_gather = mode != "last"
    refs = list(refs)
    take = refs.pop
    part_ref = take(0) if has_sum else None
    x_ref = take(0)
    dy_ref = take(0) if mode in ("back", "last") else None
    gain_ref = take(0)
    out_ref = take(0) if has_gather else None
    rows_ref = take(0) if has_sum else None
    dgain_ref = take(0) if mode in ("back", "last") else None
    if has_sum:
        pair_ref, staged_ref, landed_ref, pair_sem, sum_sem = (take(0) for _ in range(5))
    if has_gather:
        gather_sem, mate_sem = (take(0) for _ in range(2))
    place, chip, core, mate = line_place()
    enter(chips, mate)

    if has_sum:
        pair_copies = []
        for k in list(range(1, chips)) + [0]:
            to_chip = (chip + k) % chips
            copy = pltpu.make_async_remote_copy(
                src_ref=part_ref.at[to_chip * 2 + 1 - core],
                dst_ref=pair_ref.at[k],
                send_sem=pair_sem.at[0, k],
                recv_sem=pair_sem.at[1, k],
                device_id={"seq": mate},
                device_id_type=MESH,
            )
            copy.start()
            pair_copies.append((k, copy))
        sum_copies = []
        total = None
        for k, copy in pair_copies:
            to_chip = (chip + k) % chips
            copy.wait_recv()
            both = part_ref[to_chip * 2 + core].astype(f32) + pair_ref[k].astype(f32)
            if k == 0:
                total = both
            else:
                staged_ref[k] = both.astype(bf16)
                send = pltpu.make_async_remote_copy(
                    src_ref=staged_ref.at[k],
                    dst_ref=landed_ref.at[k],
                    send_sem=sum_sem.at[0, k],
                    recv_sem=sum_sem.at[1, k],
                    device_id={"seq": to_chip * 2 + core},
                    device_id_type=MESH,
                )
                send.start()
                sum_copies.append((k, send))
        for k, send in sum_copies:
            send.wait_recv()
            total = total + landed_ref[k].astype(f32)

    gain = gain_ref[...]
    x_wide = x_ref[...].astype(f32)
    if mode in ("start", "forward"):
        if mode == "forward":
            x_low = (x_wide + total).astype(bf16)
            rows_ref[...] = x_low
            x_wide = x_low.astype(f32)
        scale = lax.rsqrt(jnp.mean(x_wide * x_wide, axis=-1, keepdims=True) + epsilon)
        sent = (x_wide * scale * gain).astype(bf16)
    else:
        scale = lax.rsqrt(jnp.mean(x_wide * x_wide, axis=-1, keepdims=True) + epsilon)
        scaled = total * gain
        inner_mean = jnp.mean(scaled * x_wide, axis=-1, keepdims=True)
        back = scale * scaled - x_wide * (scale * scale * scale * inner_mean)
        dgain_ref[...] = jnp.sum(total * x_wide * scale, axis=0, keepdims=True)
        sent = (dy_ref[...].astype(f32) + back).astype(bf16)
        rows_ref[...] = sent

    if has_gather:
        out_ref[place] = sent
        sends = []
        for k in range(1, chips):
            copy = pltpu.make_async_remote_copy(
                src_ref=out_ref.at[place],
                dst_ref=out_ref.at[place],
                send_sem=gather_sem.at[0, k],
                recv_sem=gather_sem.at[1, k],
                device_id={"seq": ((chip + k) % chips) * 2 + core},
                device_id_type=MESH,
            )
            copy.start()
            sends.append(copy)
        mates = []

        def to_mate(slot, k):
            copy = pltpu.make_async_remote_copy(
                src_ref=out_ref.at[slot],
                dst_ref=out_ref.at[slot],
                send_sem=mate_sem.at[0, k],
                recv_sem=mate_sem.at[1, k],
                device_id={"seq": mate},
                device_id_type=MESH,
            )
            copy.start()
            mates.append(copy)

        to_mate(place, 0)
        for k in range(1, chips):
            sends[k - 1].wait_recv()
            to_mate(((chip + chips - k) % chips) * 2 + core, k)
        for copy in mates:
            copy.wait()
        for copy in sends:
            copy.wait_send()
    if has_sum:
        for _, copy in pair_copies:
            copy.wait_send()
        for _, send in sum_copies:
            send.wait_send()


def exchange(mode, collective_id, part, x, dy, gain):
    rows, width = x.shape
    count = lax.axis_size("seq")
    chips = count // 2
    has_sum = mode != "start"
    has_gather = mode != "last"
    backward = mode in ("back", "last")
    operands = ([part.reshape(count, rows, width)] if has_sum else []) + [x]
    operands += ([dy] if backward else []) + [gain.astype(f32).reshape(1, width)]
    shapes = []
    if has_gather:
        shapes.append(jax.ShapeDtypeStruct((count, rows, width), bf16))
    if has_sum:
        shapes.append(jax.ShapeDtypeStruct((rows, width), bf16))
    if backward:
        shapes.append(jax.ShapeDtypeStruct((1, width), f32))
    scratch = []
    if has_sum:
        scratch += [pltpu.VMEM((chips, rows, width), bf16)] * 3
        scratch += [pltpu.SemaphoreType.DMA((2, chips))] * 2
    if has_gather:
        scratch += [pltpu.SemaphoreType.DMA((2, chips))] * 2
    whole = pl.BlockSpec(memory_space=pltpu.VMEM)
    outs = pl.pallas_call(
        lambda *refs: exchange_body(mode, count, refs),
        out_shape=shapes,
        in_specs=[whole] * len(operands),
        out_specs=[whole] * len(shapes),
        scratch_shapes=scratch,
        compiler_params=pltpu.CompilerParams(
            collective_id=collective_id, has_side_effects=True, vmem_limit_bytes=VMEM_LIMIT
        ),
    )(*operands)
    outs = list(outs)
    if has_gather:
        outs[0] = outs[0].reshape(count * rows, width)
    return outs


def swap_body(count, x_ref, out_ref, send_sem, recv_sem, own_sem):
    place = lax.axis_index("seq")
    barrier = pltpu.get_barrier_semaphore()
    for k in range(1, count):
        peer = (place + k) % count
        pl.semaphore_signal(barrier, inc=1, device_id={"seq": peer}, device_id_type=MESH)
    pl.semaphore_wait(barrier, count - 1)
    copies = []
    for k in range(1, count):
        peer = (place + k) % count
        copy = pltpu.make_async_remote_copy(
            src_ref=x_ref.at[peer],
            dst_ref=out_ref.at[place],
            send_sem=send_sem.at[k],
            recv_sem=recv_sem.at[k],
            device_id={"seq": peer},
            device_id_type=MESH,
        )
        copy.start()
        copies.append(copy)
    own = pltpu.make_async_copy(x_ref.at[place], out_ref.at[place], own_sem)
    own.start()
    own.wait()
    for copy in copies:
        copy.wait()


def swap(x, collective_id):
    count = lax.axis_size("seq")
    return pl.pallas_call(
        partial(swap_body, count),
        out_shape=jax.ShapeDtypeStruct(x.shape, x.dtype),
        in_specs=[pl.BlockSpec(memory_space=pl.ANY)],
        out_specs=pl.BlockSpec(memory_space=pl.ANY),
        scratch_shapes=[
            pltpu.SemaphoreType.DMA((count,)),
            pltpu.SemaphoreType.DMA((count,)),
            pltpu.SemaphoreType.DMA,
        ],
        compiler_params=pltpu.CompilerParams(collective_id=collective_id, has_side_effects=True),
    )(x)


def less_exp(doubled):
    small = doubled * (
        1.0
        - doubled
        * (
            0.5
            - doubled
            * (1.0 / 6 - doubled * (1.0 / 24 - doubled * (1.0 / 120 - doubled * (1.0 / 720))))
        )
    )
    return jnp.where(doubled < 0.25, small, 1.0 - jnp.exp(-doubled))


def gelu_pair(v):
    c = np.float32(np.sqrt(2 / np.pi))
    t = jnp.tanh(c * (v + 0.044715 * v * v * v))
    slope = 0.5 * (1.0 + t) + 0.5 * v * (1.0 - t * t) * c * (1.0 + 3 * 0.044715 * v * v)
    return 0.5 * v * (1.0 + t), slope


def dot(a, b):
    return jnp.dot(a, b, preferred_element_type=f32)


def dot_t(a, b):
    return lax.dot_general(a, b, (((1,), (1,)), ((), ())), preferred_element_type=f32)


def dot_rows(a, b):
    return lax.dot_general(a, b, (((0,), (0,)), ((), ())), preferred_element_type=f32)


def soft(lru):
    spread = jnp.maximum(-lru, 0.0) + jnp.log1p(jnp.exp(-jnp.abs(lru)))
    return spread, -1.0 / (1.0 + jnp.exp(lru))


def middle_forward_body(
    rows,
    width,
    is_ref,
    marks_ref,
    blocks_ref,
    small_ref,
    rim_ref,
    first_ref,
    gated_ref,
    mixed_ref,
    rate_ref,
    inflow_ref,
    states_ref,
    before_ref,
    ext,
    decays,
    drives,
    carry,
):
    @pl.when(pl.program_id(0) == 0)
    def _():
        ext[0:8] = rim_ref[...]
        carry[...] = first_ref[...]

    block = width // 2
    inner = is_ref[:, :width].astype(bf16).astype(f32)
    ext[8 : 8 + rows] = inner
    reset = marks_ref[:, 0:1]
    mixed = (
        small_ref[6:7]
        + small_ref[2:3] * inner
        + small_ref[3:4] * (ext[7 : 7 + rows] * marks_ref[:, 1:2])
        + small_ref[4:5] * (ext[6 : 6 + rows] * marks_ref[:, 2:3])
        + small_ref[5:6] * (ext[5 : 5 + rows] * marks_ref[:, 3:4])
    )
    ext[0:8] = ext[rows : rows + 8]
    mixed_ref[...] = mixed
    low = mixed.astype(bf16)
    for b in range(2):
        lanes = slice(b * block, (b + 1) * block)
        rate_ref[:, lanes] = dot(low[:, lanes], blocks_ref[0, b]) + small_ref[0:1, lanes]
        inflow_ref[:, lanes] = dot(low[:, lanes], blocks_ref[1, b]) + small_ref[1:2, lanes]
    spread, _ = soft(small_ref[7:8])
    log_decay = (-rate_scale * spread) * jax.nn.sigmoid(rate_ref[...])
    kept = 1.0 - reset
    decays[...] = jnp.exp(log_decay) * kept
    factor = reset + kept * jnp.sqrt(less_exp(-2.0 * log_decay))
    drives[...] = factor * jax.nn.sigmoid(inflow_ref[...]) * mixed

    place = lax.broadcasted_iota(jnp.int32, (8, width), 0)

    def step(j, last):
        at = pl.ds(pl.multiple_of(j * 8, 8), 8)
        a, h = decays[at], drives[at]
        for k in (1, 2, 4):
            inside = place >= k
            h = jnp.where(inside, a * pltpu.roll(h, k, 0) + h, h)
            a = jnp.where(inside, a * pltpu.roll(a, k, 0), a)
        h = h + a * last
        states_ref[at] = h
        before_ref[at] = jnp.where(place >= 1, pltpu.roll(h, 1, 0), last)
        return jnp.broadcast_to(h[7:8], (8, width))

    carry[...] = lax.fori_loop(0, rows // 8, step, carry[...])
    gated_ref[...] = (states_ref[...] * gelu_pair(is_ref[:, width:])[0]).astype(bf16)


def middle_backward_body(
    rows,
    width,
    dg_ref,
    is_ref,
    mixed_ref,
    rate_ref,
    inflow_ref,
    states_ref,
    before_ref,
    marks_ref,
    blocks_ref,
    small_ref,
    rim_ref,
    own_ref,
    dib_ref,
    drate_ref,
    dinflow_ref,
    sums_ref,
    dm_ext,
    decays,
    dstates,
    carry,
):
    @pl.when(pl.program_id(0) == 0)
    def _():
        dm_ext[rows : rows + 8] = jnp.zeros((8, width), f32)
        carry[...] = jnp.zeros((8, width), f32)
        sums_ref[...] = jnp.zeros_like(sums_ref)

    block = width // 2
    own = own_ref[0:1]
    reset = marks_ref[:, 0:1]
    kept = 1.0 - reset
    side, slope = gelu_pair(is_ref[:, width:])
    d_gated = dg_ref[...]
    dib_ref[:, width:] = (d_gated * states_ref[...] * slope * own).astype(bf16)
    dstates[...] = d_gated * side
    spread, spread_slope = soft(small_ref[7:8])
    rate = jax.nn.sigmoid(rate_ref[...])
    log_decay = (-rate_scale * spread) * rate
    decays[...] = jnp.exp(log_decay) * kept

    place = lax.broadcasted_iota(jnp.int32, (8, width), 0)

    def step(j, after):
        at = pl.ds(pl.multiple_of(rows - 8 - j * 8, 8), 8)
        own_decay, h = decays[at], dstates[at]
        a = jnp.where(place < 7, pltpu.roll(own_decay, 7, 0), 1.0)
        for k in (1, 2, 4):
            inside = place < 8 - k
            h = jnp.where(inside, a * pltpu.roll(h, 8 - k, 0) + h, h)
            a = jnp.where(inside, a * pltpu.roll(a, 8 - k, 0), a)
        h = h + a * after
        dstates[at] = h
        return jnp.broadcast_to((own_decay * h)[0:1], (8, width))

    carry[...] = lax.fori_loop(0, rows // 8, step, carry[...])

    d_h = dstates[...]
    mixed = mixed_ref[...]
    inflow = jax.nn.sigmoid(inflow_ref[...])
    root = jnp.sqrt(less_exp(-2.0 * log_decay))
    factor = reset + kept * root
    decay = decays[...]
    twice = jnp.exp(2.0 * log_decay)
    d_log = d_h * before_ref[...] * decay - d_h * inflow * mixed * kept * (twice / root)
    d_lru = jnp.sum(d_log * rate, axis=0, keepdims=True) * (-rate_scale * spread_slope)
    d_rate = (d_log * (-rate_scale * spread) * rate * (1.0 - rate)).astype(bf16)
    through = d_h * factor
    d_inflow = (through * mixed * inflow * (1.0 - inflow)).astype(bf16)
    drate_ref[...] = d_rate
    dinflow_ref[...] = d_inflow
    for b in range(2):
        lanes = slice(b * block, (b + 1) * block)
        dm_ext[0:rows, lanes] = (
            ((through * inflow)[:, lanes] + dot_t(d_rate[:, lanes], blocks_ref[0, b]) + dot_t(d_inflow[:, lanes], blocks_ref[1, b]))
            .astype(bf16)
            .astype(f32)
        )
    d_mixed = dm_ext[0:rows]
    inner = is_ref[:, :width].astype(bf16).astype(f32)
    shifted = [d_mixed] + [dm_ext[k : k + rows] * marks_ref[:, 3 + k : 4 + k] for k in (1, 2, 3)]
    d_inner = small_ref[2:3] * shifted[0]
    for k in (1, 2, 3):
        d_inner = d_inner + small_ref[2 + k : 3 + k] * shifted[k]
    dib_ref[:, :width] = (d_inner * own).astype(bf16)

    def add(row, value):
        sums_ref[row : row + 1] += value

    add(0, jnp.sum(d_rate.astype(f32), axis=0, keepdims=True))
    add(1, jnp.sum(d_inflow.astype(f32), axis=0, keepdims=True))
    for k in range(4):
        add(2 + k, jnp.sum(shifted[k] * inner, axis=0, keepdims=True))
    add(6, jnp.sum(d_mixed, axis=0, keepdims=True))
    add(7, d_lru)

    @pl.when(pl.program_id(0) == pl.num_programs(0) - 1)
    def _():
        for k in (1, 2, 3):
            for t in range(k):
                add(2 + k, dm_ext[t : t + 1] * marks_ref[t : t + 1, k : k + 1] * rim_ref[8 + t - k : 9 + t - k])

    dm_ext[rows : rows + 8] = dm_ext[0:8]


def row_spec(rows, width, steps, reverse):
    if reverse:
        return pl.BlockSpec((rows, width), lambda i: (steps - 1 - i, 0))
    return pl.BlockSpec((rows, width), lambda i: (i, 0))


def whole_spec(shape):
    return pl.BlockSpec(shape, lambda i: (0,) * len(shape))


def middle_forward(wide, marks, blocks, small, rim, first):
    tokens, width = wide.shape[0], wide.shape[1] // 2
    rows = min(256, tokens)
    steps = tokens // rows
    here = partial(row_spec, rows, steps=steps, reverse=False)
    whole = [blocks, small, rim, first]
    kinds = [bf16, f32, f32, f32, f32, f32]
    return pl.pallas_call(
        partial(middle_forward_body, rows, width),
        grid=(steps,),
        out_shape=[jax.ShapeDtypeStruct((tokens, width), kind) for kind in kinds],
        in_specs=[here(2 * width), here(8)] + [whole_spec(a.shape) for a in whole],
        out_specs=[here(width)] * 6,
        scratch_shapes=[
            pltpu.VMEM((rows + 8, width), f32),
            pltpu.VMEM((rows, width), f32),
            pltpu.VMEM((rows, width), f32),
            pltpu.VMEM((8, width), f32),
        ],
        compiler_params=pltpu.CompilerParams(vmem_limit_bytes=VMEM_LIMIT),
    )(wide, marks, *whole)


def middle_backward(d_gated, wide, saved, marks, blocks, small, rim, own):
    tokens, width = d_gated.shape
    rows = min(256, tokens)
    steps = tokens // rows
    here = partial(row_spec, rows, steps=steps, reverse=True)
    whole = [blocks, small, rim, own]
    return pl.pallas_call(
        partial(middle_backward_body, rows, width),
        grid=(steps,),
        out_shape=[
            jax.ShapeDtypeStruct((tokens, 2 * width), bf16),
            jax.ShapeDtypeStruct((tokens, width), bf16),
            jax.ShapeDtypeStruct((tokens, width), bf16),
            jax.ShapeDtypeStruct((8, width), f32),
        ],
        in_specs=[here(width), here(2 * width)] + [here(width)] * 5 + [here(8)] + [whole_spec(a.shape) for a in whole],
        out_specs=[here(2 * width), here(width), here(width), whole_spec((8, width))],
        scratch_shapes=[
            pltpu.VMEM((rows + 8, width), f32),
            pltpu.VMEM((rows, width), f32),
            pltpu.VMEM((rows, width), f32),
            pltpu.VMEM((8, width), f32),
        ],
        compiler_params=pltpu.CompilerParams(vmem_limit_bytes=VMEM_LIMIT),
    )(d_gated, wide, *saved, marks, *whole)


def stream_marks(starts, tokens):
    places = jnp.arange(tokens + 3, dtype=jnp.int32)

    def resets(p):
        return jnp.any(p[:, None] == starts[None, :], axis=1).astype(f32)

    first = 1.0 - resets(places)
    second = first * (1.0 - resets(places - 1))
    third = second * (1.0 - resets(places - 2))
    inside = (places < tokens).astype(f32)
    columns = [resets(places)[:tokens], first[:tokens], second[:tokens], third[:tokens]]
    for k, keep in ((1, first), (2, second), (3, third)):
        columns.append((keep * inside)[k : k + tokens])
    columns.append(jnp.zeros((tokens,), f32))
    return jnp.stack(columns, axis=1)


def on_device(
    inputs,
    doc_starts,
    valid_mask,
    cotangent,
    prev_state,
    prev_inputs,
    rec_gain,
    in_weight,
    side_weight,
    out_weight,
    rate_blocks,
    inflow_blocks,
    rate_bias,
    inflow_bias,
    conv_taps,
    conv_bias,
    lru_param,
    mlp_gain,
    gate_weight,
    up_weight,
    down_weight,
):
    sections = lax.axis_size("section")
    section = lax.axis_index("section")
    count = lax.axis_size("seq")
    place = lax.axis_index("seq")
    layers, d_rows, lru_width = in_weight.shape
    model = inputs.shape[2]
    tokens = inputs.shape[1] * count
    hidden_part = down_weight.shape[1]
    own_width = out_weight.shape[1]
    block_count, block_rows, block_width = rate_blocks.shape[1:]
    window = 2 * block_width
    quarter = d_rows // sections
    block_quarter = block_rows // sections
    pad_rows = -(-block_quarter * 4 * block_width // (2 * window) // 16) * 16
    first_block = [min(q * own_width // block_width, block_count - 2) for q in range(count)]
    owner = [min(q for q in range(count) if first_block[q] <= b <= first_block[q] + 1) for b in range(block_count)]
    block_start = jnp.asarray(first_block, jnp.int32)[place]
    offset = place * own_width - block_start * block_width
    window_start = block_start * block_width
    next_id = iter(range(64))

    def quarter_of(a, axis):
        size = a.shape[axis] // sections
        return lax.dynamic_slice_in_dim(a, section * size, size, axis)

    def window_of(a, axis):
        return lax.dynamic_slice_in_dim(a, window_start, window, axis)

    packed = jnp.concatenate(
        [rate_bias[:, None], inflow_bias[:, None], conv_taps, conv_bias[:, None], lru_param[:, None]], axis=1
    )
    gains_own = jnp.stack([rec_gain, mlp_gain], axis=1)
    flat = jnp.concatenate([packed.reshape(-1), gains_own.reshape(-1)])
    flat = lax.all_gather(flat, "seq", axis=0)
    small_all = flat[:, : packed.size].reshape(count, layers, 8, own_width)
    small_all = jnp.transpose(small_all, (1, 2, 0, 3)).reshape(layers, 8, lru_width)
    gains = flat[:, packed.size :].reshape(count, layers, 2, d_rows)
    gains = jnp.transpose(gains, (1, 2, 0, 3)).reshape(layers, 2, model)
    small = window_of(small_all, 2).astype(f32)

    x0 = lax.dynamic_index_in_dim(inputs, section, 0, False)
    cot = lax.dynamic_index_in_dim(cotangent, section, 0, False)
    valid = lax.dynamic_index_in_dim(valid_mask, section, 0, False)
    masked = (cot.astype(f32) * valid[:, None].astype(f32)).astype(bf16)
    masked_all = lax.all_gather(masked, "seq", axis=0, tiled=True)
    marks = stream_marks(lax.dynamic_index_in_dim(doc_starts, section, 0, False), tokens)
    first_state = window_of(lax.dynamic_index_in_dim(prev_state, section, 0, False), 1).astype(f32)
    first_state = jnp.broadcast_to(first_state[:, None], (layers, 8, window))
    rim = window_of(lax.dynamic_index_in_dim(prev_inputs, section, 0, False), 2).astype(f32)
    rim = jnp.concatenate([jnp.zeros((layers, 5, window), f32), rim], axis=1)
    channel = jnp.arange(window, dtype=jnp.int32)
    own = jnp.logical_and(channel >= offset, channel < offset + own_width).astype(f32)
    own = jnp.broadcast_to(own[None], (8, window))

    def across(blocks):
        return lax.all_gather(swap(blocks, next(next_id)), "section", axis=1)

    def fetch_rec(l):
        in_q, side_q = quarter_of(in_weight[l], 0), quarter_of(side_weight[l], 0)
        rate_q, inflow_q = quarter_of(rate_blocks[l], 1), quarter_of(inflow_blocks[l], 1)
        pieces = []
        for q in range(count):
            b = first_block[q]
            lanes = slice(b * block_width, b * block_width + window)
            wide = jnp.concatenate([in_q[:, lanes], side_q[:, lanes]], axis=1)
            gates = jnp.stack([rate_q[b : b + 2], inflow_q[b : b + 2]]).reshape(-1, 2 * window)
            gates = jnp.pad(gates, ((0, pad_rows - gates.shape[0]), (0, 0)))
            pieces.append(jnp.concatenate([wide, gates], axis=0))
        got = across(jnp.stack(pieces))
        wide = got[:, :, :quarter].reshape(model, 2 * window)
        gate_rows = block_quarter * 4 * block_width // (2 * window)
        gates = got[:, :, quarter : quarter + gate_rows]
        gates = gates.reshape(count, sections, 2, 2, block_quarter, block_width)
        gates = jnp.transpose(gates, (2, 3, 0, 1, 4, 5)).reshape(2, 2, block_width, block_width)
        return wide, gates

    def fetch_mlp(l):
        both = jnp.stack([quarter_of(gate_weight[l], 0), quarter_of(up_weight[l], 0)], axis=1)
        both = both.reshape(quarter, 2, count, hidden_part)
        both = jnp.transpose(both, (2, 0, 1, 3)).reshape(count, quarter, 2 * hidden_part)
        return across(both).reshape(model, 2 * hidden_part)

    def fetch_out():
        part = lax.all_gather(quarter_of(out_weight, 2), "seq", axis=1, tiled=True)
        return lax.all_gather(window_of(part, 1), "section", axis=2, tiled=True)

    own_out = [
        lax.dynamic_update_slice(jnp.zeros((window, model), bf16), out_weight[l], (offset, 0)) for l in range(layers)
    ]

    x = x0
    kept = []
    normed = exchange("start", next(next_id), None, x0, None, gains[0, 0])[0]
    rec_weights, mlp_weights = [], []
    for l in range(layers):
        rec_weights.append(fetch_rec(l))
        mlp_weights.append(fetch_mlp(l))
    out_windows = fetch_out()
    for l in range(layers):
        wide_weight, gates = rec_weights[l]
        wide = dot(normed, wide_weight)
        gated, *saved = middle_forward(wide, marks, gates, small[l], rim[l], first_state[l])
        part = dot(gated, own_out[l]).astype(bf16)
        kept.append((x, normed, wide, gated, saved))
        normed, x = exchange("forward", next(next_id), part, x, None, gains[l, 1])
        both = dot(normed, mlp_weights[l])
        hidden = (jax.nn.gelu(both[:, :hidden_part]) * both[:, hidden_part:]).astype(bf16)
        part = dot(hidden, down_weight[l]).astype(bf16)
        kept.append((x, normed, both, hidden))
        if l + 1 < layers:
            normed, x = exchange("forward", next(next_id), part, x, None, gains[l + 1, 0])
        else:
            branch = lax.psum_scatter(part, "seq", scatter_dimension=0, tiled=True)
            outputs = (x.astype(f32) + branch.astype(f32)).astype(bf16)

    def sum_rows(grad):
        cols = grad.shape[1]
        grad = grad.astype(bf16).reshape(count, sections, quarter, cols)
        grad = jnp.transpose(grad, (1, 0, 2, 3)).reshape(sections * count * quarter, cols)
        grad = lax.psum_scatter(grad, "section", scatter_dimension=0, tiled=True)
        got = swap(grad.reshape(count, quarter, cols), next(next_id))
        return lax.all_gather(got, "section", axis=0)

    def spread_rows(got, lanes):
        part = got[..., lanes]
        return jnp.transpose(part, (0, 2, 1, 3)).reshape(d_rows, -1).astype(f32)

    d_rows_own, d_all = masked, masked_all
    dgains = [[None, None] for _ in range(layers)]
    grads = {}
    for l in reversed(range(layers)):
        x, normed, both, hidden = kept[2 * l + 1]
        d_hidden = dot_t(d_all, down_weight[l])
        gate, slope = gelu_pair(both[:, :hidden_part])
        d_gate = (d_hidden * both[:, hidden_part:] * slope).astype(bf16)
        d_up = (d_hidden * gate).astype(bf16)
        d_both = jnp.concatenate([d_gate, d_up], axis=1)
        part = dot_t(d_both, mlp_weights[l]).astype(bf16)
        grads["down", l] = lax.psum(dot_rows(hidden, d_all).astype(bf16), "section")
        grads["both", l] = sum_rows(dot_rows(normed, d_both))
        d_all, d_rows_own, dgains[l][1] = exchange("back", next(next_id), part, x, d_rows_own, gains[l, 1])

        x, normed, wide, gated, saved = kept[2 * l]
        wide_weight, gates = rec_weights[l]
        d_gated = dot_t(d_all, out_windows[l])
        dib, d_rate, d_inflow, sums = middle_backward(
            d_gated, wide, saved, marks, gates, small[l], rim[l], own
        )
        part = dot_t(dib, wide_weight).astype(bf16)
        grad_out = lax.dynamic_slice_in_dim(dot_rows(gated, d_all), offset, own_width, 0)
        grads["out", l] = lax.psum(grad_out.astype(bf16), "section")
        grad_wide = dot_rows(normed, dib)
        grads["wide", l] = sum_rows(
            jnp.concatenate(
                [
                    lax.dynamic_slice_in_dim(grad_wide, offset, own_width, 1),
                    lax.dynamic_slice_in_dim(grad_wide, offset + window, own_width, 1),
                ],
                axis=1,
            )
        )
        low = saved[0].astype(bf16).reshape(tokens, 2, block_width)
        d_gates = jnp.stack([d_rate, d_inflow]).reshape(2, tokens, 2, block_width)
        grads["gates", l] = jnp.einsum("tbi,gtbj->gbij", low, d_gates, preferred_element_type=f32)
        grads["sums", l] = lax.dynamic_slice_in_dim(sums, offset, own_width, 1)
        if l > 0:
            d_all, d_rows_own, dgains[l][0] = exchange("back", next(next_id), part, x, d_rows_own, gains[l, 0])
        else:
            input_grad, dgains[l][0] = exchange("last", next(next_id), part, x, d_rows_own, gains[l, 0])

    gate_grads = jnp.stack([grads["gates", l] for l in range(layers)]).astype(bf16)
    gate_grads = lax.psum(gate_grads, "section")
    gate_grads = gate_grads.reshape(layers * 4, count, block_rows, block_width)
    got = swap(
        jnp.transpose(gate_grads, (1, 0, 2, 3)).reshape(count, layers * 4 * block_rows, block_width), next(next_id)
    )
    got = got.reshape(count, layers, 2, 2, block_rows, block_width)
    gate_out = jnp.stack([got[owner[b], :, :, b - first_block[owner[b]]] for b in range(block_count)], axis=2)
    gate_out = gate_out.astype(f32)

    sums = lax.psum(jnp.stack([grads["sums", l] for l in range(layers)]), "section")
    dgain_all = jnp.stack([jnp.concatenate(dgains[l], axis=0) for l in range(layers)])
    dgain_all = lax.psum(dgain_all, ("section", "seq"))
    dgain_all = lax.dynamic_slice_in_dim(dgain_all, place * d_rows, d_rows, 2)

    def stacked(name, lanes):
        return jnp.stack([spread_rows(grads[name, l], lanes) for l in range(layers)])

    return (
        outputs[None],
        input_grad[None],
        dgain_all[:, 0],
        stacked("wide", slice(0, own_width)),
        stacked("wide", slice(own_width, None)),
        jnp.stack([grads["out", l] for l in range(layers)]).astype(f32),
        gate_out[:, 0],
        gate_out[:, 1],
        sums[:, 0],
        sums[:, 1],
        sums[:, 2:6],
        sums[:, 6],
        sums[:, 7],
        dgain_all[:, 1],
        stacked("both", slice(0, hidden_part)),
        stacked("both", slice(hidden_part, None)),
        jnp.stack([grads["down", l] for l in range(layers)]).astype(f32),
    )


def solution(mesh):
    return jax.shard_map(
        on_device,
        mesh=mesh,
        in_specs=(
            P(None, "seq", None),
            P(),
            P(None, "seq"),
            P(None, "seq", None),
            P(),
            P(),
            P(None, "seq"),
            P(None, "seq", None),
            P(None, "seq", None),
            P(None, "seq", None),
            P(None, None, "seq", None),
            P(None, None, "seq", None),
            P(None, "seq"),
            P(None, "seq"),
            P(None, None, "seq"),
            P(None, "seq"),
            P(None, "seq"),
            P(None, "seq"),
            P(None, "seq", None),
            P(None, "seq", None),
            P(None, "seq", None),
        ),
        out_specs=(
            P("section", "seq", None),
            P("section", "seq", None),
            P(None, "seq"),
            P(None, "seq", None),
            P(None, "seq", None),
            P(None, "seq", None),
            P(None, None, "seq", None),
            P(None, None, "seq", None),
            P(None, "seq"),
            P(None, "seq"),
            P(None, None, "seq"),
            P(None, "seq"),
            P(None, "seq"),
            P(None, "seq"),
            P(None, "seq", None),
            P(None, "seq", None),
            P(None, "seq", None),
        ),
        check_vma=False,
    )
```

time: 7060 us -> 1540 us (0.22)
  waiting for transfers between devices: 2720 us -> 322 us
  local copies, waits for them, and re-layouts: 1900 us -> 172 us
  other arithmetic: 975 us -> 39.3 us
  Pallas kernels: 0 us -> 774 us
  blocking collectives: 714 us -> 82.5 us
  matrix products: 431 us -> 117 us
  starting transfers between devices: 162 us -> 0.71 us
    reduce_scatter x8 -> x5, waiting for transfers between devices: 1100 us -> 79.2 us  [the longest x4 67.3 us: sum_rows(): grad = lax.psum_scatter(grad, 'section', scatter_dimension=0, tiled=True)]
    slice x849 -> x29, local copies, waits for them, and re-layouts: 1030 us -> 26.9 us  [the longest x2 9.85 us: fetch_rec(): wide = got[:, :, :quarter].reshape(model, 2 * window)]
    all_gather x8 -> x11, waiting for transfers between devices: 914 us -> 81.3 us  [the longest x4 81.2 us: sum_rows(): return lax.all_gather(got, 'section', axis=0)]
    pallas_call x0 -> x21, Pallas kernels: none -> 774 us  [the longest x8 412 us: exchange(): pl.pallas_call(lambda *refs: exchange_body(mode, count, refs), out_shape=...]
    all_gather x46 -> x1, blocking collectives: 661 us -> 24.9 us  [on_device(): flat = lax.all_gather(flat, 'seq', axis=0)]
    pad x420 -> x0, local copies, waits for them, and re-layouts: 453 us -> none  [the longest x280 235 us: recurrent_forward(): lax.associative_scan(compose, (decays, drives), axis=0)]
    add x508 -> x0, other arithmetic: 350 us -> none  [the longest x210 125 us: compose(): later_pair[0] * earlier[1] + later_pair[1]]
    dot_general x31 -> x26, matrix products: 431 us -> 117 us  [the longest x8 45.7 us: dot_t(): lax.dot_general(a, b, (((1,), (1,)), ((), ())), preferred_element_type=f32)]
where the time goes in v1:
time: 1540 us; the launch traced here: 1520 us
  Pallas kernels  774 us (50%)
  waiting for transfers between devices  322 us (21%)
  local copies, waits for them, and re-layouts  172 us (11%)
  matrix products  117 us (8%)
  blocking collectives  82.5 us (5%)
  other arithmetic  39.3 us (3%)
  between operations  16.8 us (1%)
    pallas_call x8, Pallas kernels, exchange(): pl.pallas_call(lambda *refs: exchange_body(mode, count, refs), out_shape=...  412 us
    pallas_call x9, Pallas kernels, swap(): pl.pallas_call(partial(swap_body, count), out_shape=jax.ShapeDtypeStruct(...  324 us
    psum x1, waiting for transfers between devices, on_device(): grads['out', l] = lax.psum(grad_out.astype(bf16), 'section')  161 us
    all_gather x4, waiting for transfers between devices, sum_rows(): return lax.all_gather(got, 'section', axis=0)  81.2 us
    convert_element_type x20, local copies, waits for them, and re-layouts, spread_rows(): return jnp.transpose(part, (0, 2, 1, 3)).reshape(d_rows, -1).astype(f32)  72.3 us
    reduce_scatter x4, waiting for transfers between devices, sum_rows(): grad = lax.psum_scatter(grad, 'section', scatter_dimension=0, tiled=True)  67.3 us
    dot_general x8, matrix products, dot_t(): lax.dot_general(a, b, (((1,), (1,)), ((), ())), preferred_element_type=f32)  45.7 us
    psum x1, blocking collectives, on_device(): dgain_all = lax.psum(dgain_all, ('section', 'seq'))  43.2 us
  transfers between devices with their start and end apart: 17, of which 6 were waited for; matrix products, arithmetic and copies ran while one was open for 17% of the time, Pallas kernels for 50%

profile of v1, /device:TPU:18, one launch (start us, length us, event | category | flops | bytes accessed | tf_op | source)
XLA Modules:
  0.0 1524.2 jit_solution(8030647324980500142)
XLA Ops:
  14.0 62.1 %shard_map.342 = bf16[8,80,1024]{2,1,0:T(8,128)(2,1)} custom-call(bf16[8,80,1024]{2,1,0:T(8,128)(2,1)} %copy-done.17), custom_call_target="tpu_custom_call" | custom-call | tf_op jit(solution)/shard_map/pallas_call | solution.py:224
  77.9 36.9 %shard_map.347 = bf16[8,80,1024]{2,1,0:T(8,128)(2,1)} custom-call(bf16[8,80,1024]{2,1,0:T(8,128)(2,1)} %copy-done.18), custom_call_target="tpu_custom_call" | custom-call | tf_op jit(solution)/shard_map/pallas_call | solution.py:224
  130.0 37.5 %shard_map.345 = bf16[8,64,1536]{2,1,0:T(8,128)(2,1)} custom-call(bf16[8,64,1536]{2,1,0:T(8,128)(2,1)} %reshape.561.x_ref), custom_call_target="tpu_custom_call" | custom-call | tf_op jit(solution)/shard_map/pallas_call | solution.py:224
  173.0 37.7 %shard_map.350 = bf16[8,64,1536]{2,1,0:T(8,128)(2,1)} custom-call(bf16[8,64,1536]{2,1,0:T(8,128)(2,1)} %reshape.578.x_ref), custom_call_target="tpu_custom_call" | custom-call | tf_op jit(solution)/shard_map/pallas_call | solution.py:224
  213.7 24.9 %all-gather = bf16[49152]{0:T(1024)(128)(2,1)S(1)} all-gather(bf16[6144]{0:T(1024)(128)(2,1)S(1)} %pad_maximum_fusion.25), channel_id=2, replica_groups=mesh['section'=4,'seq'=8] {'seq'}, dimensions={0}, use_global_device_ids=true | all-gather | bytes 110592 | tf_op jit(solution)/shard_map/all_gather | solution.py:583
  243.9 28.1 %shard_map.341 = bf16[8,64,2048]{2,1,0:T(8,128)(2,1)} custom-call(bf16[64,2048]{1,0:T(8,128)(2,1)} %dynamic-slice_bitcast_fusion.4.refs_0_.refs_1_, f32[1,2048]{1,0:T(1,128)} %get-tuple-element.302.refs_1_.refs_3_), custom_call_target="tpu_custom_call" | custom-call | tf_op jit(solution)/shard_map/pallas_call | solution.py:179
  315.4 55.4 %shard_map.344 = (bf16[8,64,2048]{2,1,0:T(8,128)(2,1)}, bf16[64,2048]{1,0:T(8,128)(2,1)}) custom-call(bf16[8,64,2048]{2,1,0:T(8,128)(2,1)} %bitcast.488, bf16[64,2048]{1,0:T(8,128)(2,1)} %dynamic-slice_bitcast_fusion.4.refs_0_.refs_1_, f32[1,2048]{1,0:T(1,128)} %get-tuple-element.301.refs_2_.refs_3_), custom_call_target="tpu_custom_call" | custom-call | tf_op jit(solution)/shard_map/pallas_call | solution.py:179
  380.9 73.5 %shard_map.346 = (bf16[8,64,2048]{2,1,0:T(8,128)(2,1)}, bf16[64,2048]{1,0:T(8,128)(2,1)}) custom-call(bf16[8,64,2048]{2,1,0:T(8,128)(2,1)} %bitcast.489, bf16[64,2048]{1,0:T(8,128)(2,1)} %get-tuple-element.56.refs_1_, f32[1,2048]{1,0:T(1,128)} %get-tuple-element.300.refs_2_.refs_3_), custom_call_target="tpu_custom_call" | custom-call | tf_op jit(solution)/shard_map/pallas_call | solution.py:179
  473.3 55.7 %shard_map.349 = (bf16[8,64,2048]{2,1,0:T(8,128)(2,1)}, bf16[64,2048]{1,0:T(8,128)(2,1)}) custom-call(bf16[8,64,2048]{2,1,0:T(8,128)(2,1)} %bitcast.487, bf16[64,2048]{1,0:T(8,128)(2,1)} %get-tuple-element.59.refs_1_, f32[1,2048]{1,0:T(1,128)} %get-tuple-element.299.refs_2_.refs_3_), custom_call_target="tpu_custom_call" | custom-call | tf_op jit(solution)/shard_map/pallas_call | solution.py:179
  546.7 57.1 %shard_map.351 = (bf16[8,64,2048]{2,1,0:T(8,128)(2,1)}, bf16[64,2048]{1,0:T(8,128)(2,1)}, f32[1,2048]{1,0:T(1,128)}) custom-call(bf16[8,64,2048]{2,1,0:T(8,128)(2,1)} %bitcast.482, bf16[64,2048]{1,0:T(8,128)(2,1)} %get-tuple-element.60.refs_1_, bf16[64,2048]{1,0:T(8,128)(2,1)} %fusion.64.refs_2_, f32[1,2048]{1,0:T(1,128)} %get-tuple-element.299.refs_2_.refs_3_), custom_call_target="tpu_custom_call" | custom-call | tf_op jit(solution)/shard_map/pallas_call | solution.py:179
  637.7 57.2 %shard_map.353 = (bf16[8,64,2048]{2,1,0:T(8,128)(2,1)}, bf16[64,2048]{1,0:T(8,128)(2,1)}, f32[1,2048]{1,0:T(1,128)}) custom-call(bf16[8,64,2048]{2,1,0:T(8,128)(2,1)} %bitcast.481, bf16[64,2048]{1,0:T(8,128)(2,1)} %get-tuple-element.59.refs_1_, bf16[64,2048]{1,0:T(8,128)(2,1)} %get-tuple-element.69.refs_2_, f32[1,2048]{1,0:T(1,128)} %get-tuple-element.300.refs_2_.refs_3_), custom_call_target="tpu_custom_call" | custom-call | tf_op jit(solution)/shard_map/pallas_call | solution.py:179
  708.1 57.2 %shard_map.354 = (bf16[8,64,2048]{2,1,0:T(8,128)(2,1)}, bf16[64,2048]{1,0:T(8,128)(2,1)}, f32[1,2048]{1,0:T(1,128)}) custom-call(bf16[8,64,2048]{2,1,0:T(8,128)(2,1)} %bitcast.483, bf16[64,2048]{1,0:T(8,128)(2,1)} %get-tuple-element.56.refs_1_, bf16[64,2048]{1,0:T(8,128)(2,1)} %get-tuple-element.71.refs_2_, f32[1,2048]{1,0:T(1,128)} %get-tuple-element.301.refs_2_.refs_3_), custom_call_target="tpu_custom_call" | custom-call | tf_op jit(solution)/shard_map/pallas_call | solution.py:179
  818.4 21.1 %shard_map.358 = bf16[8,64,640]{2,1,0:T(8,128)(2,1)} custom-call(bf16[8,64,640]{2,1,0:T(8,128)(2,1)} %bitcast.494), custom_call_target="tpu_custom_call" | custom-call | tf_op jit(solution)/shard_map/pallas_call | solution.py:224
  839.6 18.0 %shard_map.357 = bf16[8,64,640]{2,1,0:T(8,128)(2,1)} custom-call(bf16[8,64,640]{2,1,0:T(8,128)(2,1)} %bitcast.495), custom_call_target="tpu_custom_call" | custom-call | tf_op jit(solution)/shard_map/pallas_call | solution.py:224
  881.3 29.7 %reduce-scatter.14.cloned.1.call-done = bf16[512,1536]{1,0:T(8,128)(2,1)} async-done(((bf16[2048,1536]{1,0:T(8,128)(2,1)}), bf16[512,1536]{1,0:T(8,128)(2,1)}) %reduce-scatter.14.cloned.1.call-update) | async-done | bytes 1572880 | tf_op jit(solution)/shard_map/reduce_scatter | solution.py:669
  911.0 36.2 %shard_map.361 = bf16[8,64,1536]{2,1,0:T(8,128)(2,1)} custom-call(bf16[8,64,1536]{2,1,0:T(8,128)(2,1)} %bitcast.492), custom_call_target="tpu_custom_call" | custom-call | tf_op jit(solution)/shard_map/pallas_call | solution.py:224
  947.3 37.5 %reduce-scatter.12.cloned.1.call-done = bf16[512,1536]{1,0:T(8,128)(2,1)} async-done(((bf16[2048,1536]{1,0:T(8,128)(2,1)}), bf16[512,1536]{1,0:T(8,128)(2,1)}) %reduce-scatter.12.cloned.1.call-update) | async-done | bytes 1572880 | tf_op jit(solution)/shard_map/reduce_scatter | solution.py:669
  984.8 49.3 %shard_map.360 = bf16[8,64,1536]{2,1,0:T(8,128)(2,1)} custom-call(bf16[8,64,1536]{2,1,0:T(8,128)(2,1)} %bitcast.493), custom_call_target="tpu_custom_call" | custom-call | tf_op jit(solution)/shard_map/pallas_call | solution.py:224
  1053.7 27.7 %shard_map.356 = (bf16[64,2048]{1,0:T(8,128)(2,1)}, f32[1,2048]{1,0:T(1,128)}) custom-call(bf16[8,64,2048]{2,1,0:T(8,128)(2,1)} %bitcast.484, bf16[64,2048]{1,0:T(8,128)(2,1)} %dynamic-slice_bitcast_fusion.4.refs_0_.refs_1_, bf16[64,2048]{1,0:T(8,128)(2,1)} %get-tuple-element.79.refs_2_, f32[1,2048]{1,0:T(1,128)} %get-tuple-element.302.refs_1_.refs_3_), custom_call_target="tpu_custom_call" | custom-call | tf_op jit(solution)/shard_map/pallas_call | solution.py:179
  1082.2 43.2 %psum.49 = f32[2,2,2048]{2,1,0:T(2,128)S(1)} all-reduce(f32[2,2,2048]{2,1,0:T(2,128)S(1)} %pad_maximum_fusion.7), channel_id=1, replica_groups=mesh['section'=4,'seq'=8] {'section','seq'}, use_global_device_ids=true, to_apply=%region_4.5 | all-reduce | flops 8192 | bytes 65536 | tf_op jit(solution)/shard_map/psum | solution.py:732
  1172.5 161.1 %all-reduce.20.cloned.1.call-done = (bf16[1,320,2048]{2,1,0:T(8,128)(2,1)}, bf16[1,320,2048]{2,1,0:T(8,128)(2,1)}, bf16[8,256,256]{2,1,0:T(8,128)(2,1)}, bf16[1,...) async-done(((bf16[1,320,2048]{2,1,0:T(8,128)(2,1)}, bf16[1,320,2048]{2,1,0:T(8,128)(2,1)}, bf16[8,256,256]{2,1,0:T(8,128)(2,1)}, bf16[1,768,2048]{2,1,0:T(8,128)(2,1)}, ...) | async-done | bytes 9961488 | tf_op jit(solution)/shard_map/psum | solution.py:700
  1333.6 25.0 %shard_map.359 = bf16[8,256,256]{2,1,0:T(8,128)(2,1)} custom-call(bf16[8,256,256]{2,1,0:T(8,128)(2,1)} %get-tuple-element.181.x_ref), custom_call_target="tpu_custom_call" | custom-call | tf_op jit(solution)/shard_map/pallas_call | solution.py:224
  1372.9 33.3 %all-gather.41.cloned.1.call-done = bf16[32,64,1536]{2,1,0:T(8,128)(2,1)} async-done(((bf16[8,64,1536]{2,1,0:T(8,128)(2,1)}), bf16[32,64,1536]{2,1,0:T(8,128)(2,1)}) %all-gather.41.cloned.1.call-update) | async-done | bytes 6291472 | tf_op jit(solution)/shard_map/all_gather | solution.py:671
  1430.2 47.9 %all-gather.39.cloned.1.call-done = bf16[32,64,1536]{2,1,0:T(8,128)(2,1)} async-done(((bf16[8,64,1536]{2,1,0:T(8,128)(2,1)}), bf16[32,64,1536]{2,1,0:T(8,128)(2,1)}) %all-gather.39.cloned.1.call-update) | async-done | bytes 6291472 | tf_op jit(solution)/shard_map/all_gather | solution.py:671
  (435 shorter events, 393.9 us)
Async XLA Ops:
  7.2 235.3 %copy-start = (bf16[4,64,2048]{2,1,0:T(8,128)(2,1)S(1)}, bf16[4,64,2048]{2,1,0:T(8,128)(2,1)}, u32[]{:S(2)}) copy-start(bf16[4,64,2048]{2,1,0:T(8,128)(2,1)} %param.22) | copy-start | bytes 3145732
  7.2 271.6 %all-gather.23.cloned.1.call-start = ((), (), s32[]{:S(2)}) async-start(), calls=%async_computation.7 | async-start | bytes 5898240 | tf_op jit(solution)/shard_map/all_gather | solution.py:633
  9.4 271.9 %all-gather.27.cloned.1.call-start = ((), (), s32[]{:S(2)}) async-start(), calls=%async_computation.13 | async-start | bytes 6553600 | tf_op jit(solution)/shard_map/all_gather | solution.py:605
  76.2 211.1 %all-gather.31.cloned.1.call-start = ((), (), s32[]{:S(2)}) async-start(), calls=%async_computation.15 | async-start | bytes 6553600 | tf_op jit(solution)/shard_map/all_gather | solution.py:605
  114.9 255.9 %all-gather.29.cloned.1.call-start = ((), (), s32[]{:S(2)}) async-start(), calls=%async_computation.14 | async-start | bytes 7864320 | tf_op jit(solution)/shard_map/all_gather | solution.py:605
  167.4 361.6 %all-gather.33.cloned.1.call-start = ((), (), s32[]{:S(2)}) async-start(), calls=%async_computation.16 | async-start | bytes 7864320 | tf_op jit(solution)/shard_map/all_gather | solution.py:605
  210.8 324.4 %all-gather.21.cloned.1.call-start = ((), (), s32[]{:S(2)}) async-start(), calls=%async_computation.6 | async-start | bytes 2359296 | tf_op jit(solution)/shard_map/all_gather | solution.py:594
  213.3 390.5 %all-gather.25.cloned.1.call-start = ((), (), s32[]{:S(2)}) async-start(), calls=%async_computation.8 | async-start | bytes 5242880 | tf_op jit(solution)/shard_map/all_gather | solution.py:634
  281.1 537.2 %reduce-scatter.10.cloned.1.call-start = ((), (), s32[]{:S(2)}) async-start(), calls=%async_computation.10 | async-start | bytes 3276800 | tf_op jit(solution)/shard_map/reduce_scatter | solution.py:669
  315.4 62.3 %slice-start = ((s8[6291456]{0:T(1024)(128)(4,1)}), s8[2097152]{0:T(1024)(128)(4,1)S(1)}, s32[]{:S(2)}) async-start(s8[6291456]{0:T(1024)(128)(4,1)} %bitcast.521), calls=%async_computation.22 | async-start | bytes 4194304
  631.3 208.3 %reduce-scatter.8.cloned.1.call-start = ((), (), s32[]{:S(2)}) async-start(), calls=%async_computation.9 | async-start | bytes 3276800 | tf_op jit(solution)/shard_map/reduce_scatter | solution.py:669
  631.3 63.6 %copy-start.13 = (f32[512,1536]{1,0:T(8,128)S(1)}, f32[512,1536]{1,0:T(8,128)}, u32[]{:S(2)}) copy-start(f32[512,1536]{1,0:T(8,128)} %copy-done.12) | copy-start | bytes 9437188
  792.1 118.9 %reduce-scatter.14.cloned.1.call-start = ((), (), s32[]{:S(2)}) async-start(), calls=%async_computation.12 | async-start | bytes 7864320 | tf_op jit(solution)/shard_map/reduce_scatter | solution.py:669
  802.1 182.7 %reduce-scatter.12.cloned.1.call-start = ((), (), s32[]{:S(2)}) async-start(), calls=%async_computation.11 | async-start | bytes 7864320 | tf_op jit(solution)/shard_map/reduce_scatter | solution.py:669
  812.1 233.9 %reduce-scatter.6.cloned.1.call-start = ((), (), s32[]{:S(2)}) async-start(), calls=%async_computation.5 | async-start | bytes 2359296 | tf_op jit(solution)/shard_map/reduce_scatter | solution.py:662
  818.3 324.1 %all-gather.37.cloned.1.call-start = ((), (), s32[]{:S(2)}) async-start(), calls=%async_computation.18 | async-start | bytes 3276800 | tf_op jit(solution)/shard_map/all_gather | solution.py:671
  839.6 308.6 %all-gather.35.cloned.1.call-start = ((), (), s32[]{:S(2)}) async-start(), calls=%async_computation.17 | async-start | bytes 3276800 | tf_op jit(solution)/shard_map/all_gather | solution.py:671
  857.6 476.0 %all-reduce.20.cloned.1.call-start = ((), (), s32[]{:S(2)}) async-start(), calls=%async_computation.21 | async-start | bytes 19922944 | tf_op jit(solution)/shard_map/psum | solution.py:700
  881.2 525.0 %all-gather.41.cloned.1.call-start = ((), (), s32[]{:S(2)}) async-start(), calls=%async_computation.20 | async-start | bytes 7864320 | tf_op jit(solution)/shard_map/all_gather | solution.py:671
  947.2 530.9 %all-gather.39.cloned.1.call-start = ((), (), s32[]{:S(2)}) async-start(), calls=%async_computation.19 | async-start | bytes 7864320 | tf_op jit(solution)/shard_map/all_gather | solution.py:671
  984.8 61.3 %copy-start.21 = (bf16[64,2048]{1,0:T(8,128)(2,1)S(1)}, bf16[64,2048]{1,0:T(8,128)(2,1)}, u32[]{:S(2)}) copy-start(bf16[64,2048]{1,0:T(8,128)(2,1)} %get-tuple-element.60.refs_1_) | copy-start | bytes 786436
  984.8 63.0 %copy-start.54 = (bf16[512,1024]{1,0:T(8,128)(2,1)S(1)}, bf16[512,1024]{1,0:T(8,128)(2,1)}, u32[]{:S(2)}) copy-start(bf16[512,1024]{1,0:T(8,128)(2,1)} %get-tuple-element.78) | copy-start | bytes 3145732
  1053.7 72.4 %copy-start.34 = (f32[8,512]{1,0:T(8,128)S(1)}, f32[8,512]{1,0:T(8,128)}, u32[]{:S(2)}) copy-start(f32[8,512]{1,0:T(8,128)} %get-tuple-element.90) | copy-start | bytes 49156
  1053.7 72.5 %copy-start.35 = (f32[8,512]{1,0:T(8,128)S(1)}, f32[8,512]{1,0:T(8,128)}, u32[]{:S(2)}) copy-start(f32[8,512]{1,0:T(8,128)} %get-tuple-element.89) | copy-start | bytes 49156
  (61 other events, 681.2 us)
Sparse Core Ops, SparseCore 0:
  10.2 94.1 all-gather.22
  106.3 68.8 all-gather.26
  177.0 61.4 all-gather.30
  240.1 70.1 all-gather.28
  312.1 70.1 all-gather.32
  383.7 44.8 all-gather.20
  430.4 55.9 all-gather.24
  631.4 45.2 reduce-scatter.9
  792.2 45.2 reduce-scatter.7
  840.9 70.0 reduce-scatter.13
  914.5 70.2 reduce-scatter.11
  987.5 58.4 reduce-scatter.5
  1047.9 38.7 all-gather.36
  1088.4 40.3 all-gather.34
  1133.5 200.0 all-reduce.19
  1335.3 70.8 all-gather.40
  1407.9 70.1 all-gather.38

commit v2 on v1

v2 whole, which is shorter than its diff:
```python
from functools import partial

import jax
import jax.numpy as jnp
import numpy as np
from jax import lax
from jax.experimental import pallas as pl
from jax.experimental.pallas import tpu as pltpu
from jax.sharding import PartitionSpec as P


epsilon = 1e-06
rate_scale = 8.0
MESH = pl.DeviceIdType.MESH
VMEM_LIMIT = 60 * 1024 * 1024
f32 = jnp.float32
bf16 = jnp.bfloat16


def plane_place():
    section = lax.axis_index("section")
    column, row = section % 2, section // 2
    return section, row * 2 + 1 - column, (1 - row) * 2 + column


def dma(*shape):
    return pltpu.SemaphoreType.DMA(shape)


def along(source, target, send, receive, peer):
    return pltpu.make_async_remote_copy(
        src_ref=source,
        dst_ref=target,
        send_sem=send,
        recv_sem=receive,
        device_id={"seq": peer},
        device_id_type=MESH,
    )


class Item:
    def __init__(self, first, at, sems, slot, even):
        self.first, self.at, self.sems, self.slot, self.even = first, at, sems, slot, even
        self.section, self.side, self.up = plane_place()

    def copy(self, way, source, holder, target):
        return pltpu.make_async_remote_copy(
            src_ref=source,
            dst_ref=self.at(holder),
            send_sem=self.sems.at[way, 0, self.slot],
            recv_sem=self.sems.at[way, 1, self.slot],
            device_id={"section": target},
            device_id_type=MESH,
        )

    def start(self):
        self.to_side = self.copy(0, self.first, self.section, self.side)
        self.to_up = self.copy(1, self.first, self.section, self.up)
        self.to_side.start()
        self.to_up.start()

    def forward(self):
        self.to_side.wait_recv()
        if self.even:
            self.onward = self.copy(2, self.at(self.side), self.side, self.up)
            self.onward.start()
        self.to_up.wait_recv()
        if not self.even:
            self.onward = self.copy(2, self.at(self.up), self.up, self.side)
            self.onward.start()

    def finish(self):
        self.onward.wait()
        self.to_side.wait_send()
        self.to_up.wait_send()


class Spread:
    on_line, in_plane = True, True

    def __init__(self, arrays, shape, pieces, cut, fill, slot):
        self.arrays, self.pieces, self.cut, self.fill, self.slot = list(arrays), pieces, cut, fill, slot
        self.shape = jax.ShapeDtypeStruct(shape, self.arrays[0].dtype)

    def scratch(self, count):
        return [dma(2, self.pieces, count), dma(3, 2, count)]

    def begin(self, refs, out, sems, place, count):
        line, plane = sems
        self.own, self.sends, self.items = [], [], []
        section = plane_place()[0]
        for i, (piece, there) in enumerate(zip(self.cut(refs, place), self.fill(self.slot(out, place, section)))):
            copy = pltpu.make_async_copy(piece, there, line.at[0, i, 0])
            copy.start()
            self.own.append(copy)
        for k in range(count):
            source = (place + count - k) % count
            self.items.append(
                Item(
                    self.slot(out, source, section),
                    lambda s, source=source: self.slot(out, source, s),
                    plane,
                    k,
                    k % 2 == 0,
                )
            )

        def push():
            for k in range(1, count):
                peer = (place + k) % count
                pieces = zip(self.cut(refs, peer), self.fill(self.slot(out, place, section)))
                group = [
                    along(piece, there, line.at[0, i, k], line.at[1, i, k], peer)
                    for i, (piece, there) in enumerate(pieces)
                ]
                for copy in group:
                    copy.start()
                self.sends.append(group)

        self.push = push

    def own_block(self):
        for copy in self.own:
            copy.wait()
        self.items[0].start()

    def arrive(self, k):
        for copy in self.sends[k - 1]:
            copy.wait_recv()
        self.items[k].start()
        self.items[k - 1].forward()

    def finish(self):
        self.items[-1].forward()
        for item in self.items:
            item.finish()
        for group in self.sends:
            for copy in group:
                copy.wait_send()


class Share:
    on_line, in_plane = False, True

    def __init__(self, array, start, size):
        self.arrays, self.start, self.size = [array], start, size
        self.shape = jax.ShapeDtypeStruct((4, size, array.shape[1]), array.dtype)

    def scratch(self, count):
        return [dma(3, 2, 2), dma(1)]

    def begin(self, refs, out, sems, place, count):
        plane, own = sems
        section = plane_place()[0]
        mine = refs[0].at[pl.ds(self.start, self.size)]
        self.own = pltpu.make_async_copy(mine, out.at[section], own.at[0])
        self.own.start()
        half = self.size // 2
        self.items = []
        for h in range(2):
            rows = pl.ds(h * half, half)
            first = refs[0].at[pl.ds(self.start + h * half, half)]
            item = Item(first, lambda s, rows=rows: out.at[s, rows], plane, h, h == 0)
            item.start()
            self.items.append(item)

    def push(self):
        pass

    def own_block(self):
        self.own.wait()

    def arrive(self, k):
        if k in (4, 6):
            self.items[k // 2 - 2].forward()

    def finish(self):
        for item in self.items:
            item.finish()


class Everyone:
    on_line, in_plane = True, False

    def __init__(self, array, count):
        self.arrays = [array]
        self.shape = jax.ShapeDtypeStruct((count,) + array.shape, array.dtype)

    def scratch(self, count):
        return [dma(2, count)]

    def begin(self, refs, out, sems, place, count):
        self.own = pltpu.make_async_copy(refs[0], out.at[place], sems[0].at[0, 0])
        self.own.start()
        self.sends = []
        for k in range(1, count):
            copy = along(refs[0], out.at[place], sems[0].at[0, k], sems[0].at[1, k], (place + k) % count)
            copy.start()
            self.sends.append(copy)

    def push(self):
        pass

    def own_block(self):
        self.own.wait()

    def arrive(self, k):
        self.sends[k - 1].wait_recv()

    def finish(self):
        for copy in self.sends:
            copy.wait_send()


class Beside:
    on_line, in_plane = True, False

    def __init__(self, array, layer, reach):
        self.arrays, self.layer, self.reach = [array], layer, reach
        self.rows = array.shape[1]
        self.shape = jax.ShapeDtypeStruct((self.rows + 2 * reach, array.shape[2]), array.dtype)
        self.sizes = [min(self.rows, reach - at) for at in range(0, reach, self.rows)]

    def scratch(self, count):
        return [dma(2, 2, len(self.sizes) + 1)]

    def begin(self, refs, out, sems, place, count):
        mine, sem = refs[0].at[self.layer], sems[0]
        self.own = pltpu.make_async_copy(mine, out.at[pl.ds(self.reach, self.rows)], sem.at[0, 0, 0])
        self.own.start()
        self.ends = []
        done = 0
        for k, size in enumerate(self.sizes, 1):
            ahead = along(
                mine.at[pl.ds(self.rows - size, size)],
                out.at[pl.ds(self.reach - done - size, size)],
                sem.at[0, 0, k],
                sem.at[0, 1, k],
                place + k,
            )
            back = along(
                mine.at[pl.ds(0, size)],
                out.at[pl.ds(self.reach + self.rows + done, size)],
                sem.at[1, 0, k],
                sem.at[1, 1, k],
                place - k,
            )
            pl.when(place + k < count)(ahead.start)
            pl.when(place >= k)(back.start)
            self.ends.append((k, ahead, back))
            done += size
        self.place, self.count = place, count

    def push(self):
        pass

    def own_block(self):
        self.own.wait()

    def arrive(self, k):
        pass

    def finish(self):
        for k, ahead, back in self.ends:
            pl.when(self.place >= k)(ahead.wait_recv)
            pl.when(self.place + k < self.count)(back.wait_recv)
            pl.when(self.place + k < self.count)(ahead.wait_send)
            pl.when(self.place >= k)(back.wait_send)


def comm_body(mode, count, jobs, refs):
    chips = count // 2
    has_sum = mode in ("forward", "back", "last", "rows")
    has_gather = mode in ("start", "forward", "back")
    backward = mode in ("back", "last")
    refs = list(refs)
    take = refs.pop
    part_ref = take(0) if has_sum else None
    x_ref = take(0) if mode != "none" else None
    dy_ref = take(0) if backward else None
    gain_ref = take(0) if mode in ("forward", "back", "last") else None
    job_refs = [[take(0) for _ in job.arrays] for job in jobs]
    out_ref = take(0) if has_gather else None
    rows_ref = take(0) if has_sum else None
    dgain_ref = take(0) if backward else None
    job_outs = [take(0) for _ in jobs]
    if has_sum:
        pair_ref, staged_ref, landed_ref, pair_sem, sum_sem = (take(0) for _ in range(5))
    if has_gather:
        hop_sem, mate_sem = (take(0) for _ in range(2))
    job_sems = [[take(0) for _ in job.scratch(count)] for job in jobs]

    place = lax.axis_index("seq")
    chip, core = place // 2, place % 2
    mate = chip * 2 + 1 - core
    section, side, up = plane_place()

    barrier = pltpu.get_barrier_semaphore()
    met = 0
    line = []
    if any(job.on_line for job in jobs):
        line = [(place + k) % count for k in range(1, count)]
    elif mode != "none":
        line = [mate] + [((chip + k) % chips) * 2 + core for k in range(1, chips)]
    for peer in line:
        pl.semaphore_signal(barrier, inc=1, device_id={"seq": peer}, device_id_type=MESH)
        met += 1
    if any(job.in_plane for job in jobs):
        for peer in (side, up):
            pl.semaphore_signal(barrier, inc=1, device_id={"section": peer}, device_id_type=MESH)
            met += 1
    pl.semaphore_wait(barrier, met)

    def origin(way, k):
        return chip - k if way == 0 else chip + k

    def comes(way, k):
        return chip >= k if way == 0 else chip + k < chips

    def goes_on(way):
        return chip + 1 < chips if way == 0 else chip >= 1

    def hop(way, k):
        slot = origin(way, k) * 2 + core
        onward = chip + 1 if way == 0 else chip - 1
        return along(
            out_ref.at[slot], out_ref.at[slot], hop_sem.at[way, 0, k], hop_sem.at[way, 1, k + 1], onward * 2 + core
        )

    def landing(way, k):
        slot = origin(way, k) * 2 + core
        return along(out_ref.at[slot], out_ref.at[slot], hop_sem.at[way, 0, k], hop_sem.at[way, 1, k], mate)

    def across(way, k):
        slot = origin(way, k) * 2 + core
        return along(out_ref.at[slot], out_ref.at[slot], mate_sem.at[way, 0, k], mate_sem.at[way, 1, k], mate)

    def begin_gather(rows):
        out_ref[place] = rows
        for way in range(2):
            pl.when(goes_on(way))(hop(way, 0).start)
        across(0, 0).start()

    def land(k):
        for way in range(2):

            @pl.when(comes(way, k))
            def _(way=way, k=k):
                landing(way, k).wait_recv()
                pl.when(goes_on(way))(hop(way, k).start)
                across(way, k).start()

    if mode == "start":
        begin_gather(x_ref[...])
    if has_sum:
        pair_copies = []
        for k in list(range(1, chips)) + [0]:
            to_chip = (chip + k) % chips
            copy = along(
                part_ref.at[to_chip * 2 + 1 - core], pair_ref.at[k], pair_sem.at[0, k], pair_sem.at[1, k], mate
            )
            copy.start()
            pair_copies.append((k, copy))
    for job, ref, out, sems in zip(jobs, job_refs, job_outs, job_sems):
        job.begin(ref, out, sems, place, count)
    if has_sum:
        sum_copies = []
        total = None
        for k, copy in pair_copies:
            to_chip = (chip + k) % chips
            copy.wait_recv()
            both = part_ref[to_chip * 2 + core].astype(f32) + pair_ref[k].astype(f32)
            if k == 0:
                total = both
            else:
                staged_ref[k] = both.astype(bf16)
                send = along(
                    staged_ref.at[k], landed_ref.at[k], sum_sem.at[0, k], sum_sem.at[1, k], to_chip * 2 + core
                )
                send.start()
                sum_copies.append((k, send))
    for job in jobs:
        job.push()
    for job in jobs:
        job.own_block()
    for k in range(1, count):
        for job in jobs:
            job.arrive(k)
        if mode == "start" and k % 2 == 0:
            land(k // 2)
    if has_sum:
        for k, send in sum_copies:
            send.wait_recv()
            total = total + landed_ref[k].astype(f32)

    if mode != "none":
        x_wide = x_ref[...].astype(f32)
    if mode == "rows":
        rows_ref[...] = (x_wide + total).astype(bf16)
    elif mode == "forward":
        x_low = (x_wide + total).astype(bf16)
        rows_ref[...] = x_low
        x_wide = x_low.astype(f32)
        scale = lax.rsqrt(jnp.mean(x_wide * x_wide, axis=-1, keepdims=True) + epsilon)
        sent = (x_wide * scale * gain_ref[...]).astype(bf16)
    elif backward:
        scale = lax.rsqrt(jnp.mean(x_wide * x_wide, axis=-1, keepdims=True) + epsilon)
        scaled = total * gain_ref[...]
        inner_mean = jnp.mean(scaled * x_wide, axis=-1, keepdims=True)
        back = scale * scaled - x_wide * (scale * scale * scale * inner_mean)
        dgain_ref[...] = jnp.sum(total * x_wide * scale, axis=0, keepdims=True)
        sent = (dy_ref[...].astype(f32) + back).astype(bf16)
        rows_ref[...] = sent

    if has_gather and mode != "start":
        begin_gather(sent)
        for k in range(1, chips):
            land(k)

    for job in jobs:
        job.finish()
    if has_gather:
        across(0, 0).wait()
        for way in range(2):
            pl.when(goes_on(way))(hop(way, 0).wait_send)
        for k in range(1, chips):
            for way in range(2):

                @pl.when(comes(way, k))
                def _(way=way, k=k):
                    across(way, k).wait()
                    pl.when(goes_on(way))(hop(way, k).wait_send)

    if has_sum:
        for _, copy in pair_copies:
            copy.wait_send()
        for _, send in sum_copies:
            send.wait_send()


def comm(mode, collective_id, part=None, x=None, dy=None, gain=None, jobs=(), us=50):
    count = lax.axis_size("seq")
    chips = count // 2
    has_sum = mode in ("forward", "back", "last", "rows")
    has_gather = mode in ("start", "forward", "back")
    backward = mode in ("back", "last")
    in_vmem = pl.BlockSpec(memory_space=pltpu.VMEM)
    in_hbm = pl.BlockSpec(memory_space=pl.ANY)
    operands, in_specs, shapes, out_specs, scratch = [], [], [], [], []

    def give(a, spec):
        operands.append(a)
        in_specs.append(spec)

    def want(shape, spec):
        shapes.append(shape)
        out_specs.append(spec)

    if mode != "none":
        rows, width = x.shape
    if has_sum:
        give(part.reshape(count, rows, width), in_vmem)
    if mode != "none":
        give(x, in_vmem)
    if backward:
        give(dy, in_vmem)
    if mode in ("forward", "back", "last"):
        give(gain.astype(f32).reshape(1, width), in_vmem)
    for job in jobs:
        for a in job.arrays:
            give(a, in_hbm)
    if has_gather:
        want(jax.ShapeDtypeStruct((count, rows, width), bf16), in_vmem)
    if has_sum:
        want(jax.ShapeDtypeStruct((rows, width), bf16), in_vmem)
    if backward:
        want(jax.ShapeDtypeStruct((1, width), f32), in_vmem)
    for job in jobs:
        want(job.shape, in_hbm)
    if has_sum:
        scratch += [pltpu.VMEM((chips, rows, width), bf16)] * 3 + [dma(2, chips)] * 2
    if has_gather:
        scratch += [dma(2, 2, chips + 1), dma(2, 2, chips)]
    for job in jobs:
        scratch += job.scratch(count)
    outs = pl.pallas_call(
        lambda *refs: comm_body(mode, count, jobs, refs),
        out_shape=shapes,
        in_specs=in_specs,
        out_specs=out_specs,
        scratch_shapes=scratch,
        cost_estimate=pl.CostEstimate(flops=us * 1_000_000_000, bytes_accessed=1_000_000, transcendentals=0),
        compiler_params=pltpu.CompilerParams(
            collective_id=collective_id, has_side_effects=True, vmem_limit_bytes=VMEM_LIMIT
        ),
    )(*operands)
    outs = list(outs)
    if has_gather:
        outs[0] = outs[0].reshape(count * rows, width)
    return outs


def less_exp(doubled):
    small = doubled * (
        1.0
        - doubled
        * (
            0.5
            - doubled
            * (1.0 / 6 - doubled * (1.0 / 24 - doubled * (1.0 / 120 - doubled * (1.0 / 720))))
        )
    )
    return jnp.where(doubled < 0.25, small, 1.0 - jnp.exp(-doubled))


def gelu_pair(v):
    c = np.float32(np.sqrt(2 / np.pi))
    t = jnp.tanh(c * (v + 0.044715 * v * v * v))
    slope = 0.5 * (1.0 + t) + 0.5 * v * (1.0 - t * t) * c * (1.0 + 3 * 0.044715 * v * v)
    return 0.5 * v * (1.0 + t), slope


def dot(a, b):
    return jnp.dot(a, b, preferred_element_type=f32)


def dot_t(a, b):
    return lax.dot_general(a, b, (((1,), (1,)), ((), ())), preferred_element_type=f32)


def dot_rows(a, b):
    return lax.dot_general(a, b, (((0,), (0,)), ((), ())), preferred_element_type=f32)


def soft(lru):
    spread = jnp.maximum(-lru, 0.0) + jnp.log1p(jnp.exp(-jnp.abs(lru)))
    return spread, -1.0 / (1.0 + jnp.exp(lru))


def middle_forward_body(
    rows,
    width,
    is_ref,
    marks_ref,
    blocks_ref,
    small_ref,
    rim_ref,
    first_ref,
    gated_ref,
    mixed_ref,
    rate_ref,
    inflow_ref,
    states_ref,
    before_ref,
    ext,
    decays,
    drives,
    carry,
):
    @pl.when(pl.program_id(0) == 0)
    def _():
        ext[0:8] = rim_ref[...]
        carry[...] = first_ref[...]

    block = width // 2
    inner = is_ref[:, :width].astype(bf16).astype(f32)
    ext[8 : 8 + rows] = inner
    reset = marks_ref[:, 0:1]
    mixed = (
        small_ref[6:7]
        + small_ref[2:3] * inner
        + small_ref[3:4] * (ext[7 : 7 + rows] * marks_ref[:, 1:2])
        + small_ref[4:5] * (ext[6 : 6 + rows] * marks_ref[:, 2:3])
        + small_ref[5:6] * (ext[5 : 5 + rows] * marks_ref[:, 3:4])
    )
    ext[0:8] = ext[rows : rows + 8]
    mixed_ref[...] = mixed
    low = mixed.astype(bf16)
    for b in range(2):
        lanes = slice(b * block, (b + 1) * block)
        rate_ref[:, lanes] = dot(low[:, lanes], blocks_ref[0, b]) + small_ref[0:1, lanes]
        inflow_ref[:, lanes] = dot(low[:, lanes], blocks_ref[1, b]) + small_ref[1:2, lanes]
    spread, _ = soft(small_ref[7:8])
    log_decay = (-rate_scale * spread) * jax.nn.sigmoid(rate_ref[...])
    kept = 1.0 - reset
    decays[...] = jnp.exp(log_decay) * kept
    factor = reset + kept * jnp.sqrt(less_exp(-2.0 * log_decay))
    drives[...] = factor * jax.nn.sigmoid(inflow_ref[...]) * mixed

    place = lax.broadcasted_iota(jnp.int32, (8, width), 0)

    def step(j, last):
        at = pl.ds(pl.multiple_of(j * 8, 8), 8)
        a, h = decays[at], drives[at]
        for k in (1, 2, 4):
            inside = place >= k
            h = jnp.where(inside, a * pltpu.roll(h, k, 0) + h, h)
            a = jnp.where(inside, a * pltpu.roll(a, k, 0), a)
        h = h + a * last
        states_ref[at] = h
        before_ref[at] = jnp.where(place >= 1, pltpu.roll(h, 1, 0), last)
        return jnp.broadcast_to(h[7:8], (8, width))

    carry[...] = lax.fori_loop(0, rows // 8, step, carry[...])
    gated_ref[...] = (states_ref[...] * gelu_pair(is_ref[:, width:])[0]).astype(bf16)


def middle_backward_body(
    rows,
    width,
    dg_ref,
    is_ref,
    mixed_ref,
    rate_ref,
    inflow_ref,
    states_ref,
    before_ref,
    marks_ref,
    blocks_ref,
    small_ref,
    rim_ref,
    own_ref,
    dib_ref,
    drate_ref,
    dinflow_ref,
    sums_ref,
    dm_ext,
    decays,
    dstates,
    carry,
):
    @pl.when(pl.program_id(0) == 0)
    def _():
        dm_ext[rows : rows + 8] = jnp.zeros((8, width), f32)
        carry[...] = jnp.zeros((8, width), f32)
        sums_ref[...] = jnp.zeros_like(sums_ref)

    block = width // 2
    own = own_ref[0:1]
    reset = marks_ref[:, 0:1]
    kept = 1.0 - reset
    side, slope = gelu_pair(is_ref[:, width:])
    d_gated = dg_ref[...]
    dib_ref[:, width:] = (d_gated * states_ref[...] * slope * own).astype(bf16)
    dstates[...] = d_gated * side
    spread, spread_slope = soft(small_ref[7:8])
    rate = jax.nn.sigmoid(rate_ref[...])
    log_decay = (-rate_scale * spread) * rate
    decays[...] = jnp.exp(log_decay) * kept

    place = lax.broadcasted_iota(jnp.int32, (8, width), 0)

    def step(j, after):
        at = pl.ds(pl.multiple_of(rows - 8 - j * 8, 8), 8)
        own_decay, h = decays[at], dstates[at]
        a = jnp.where(place < 7, pltpu.roll(own_decay, 7, 0), 1.0)
        for k in (1, 2, 4):
            inside = place < 8 - k
            h = jnp.where(inside, a * pltpu.roll(h, 8 - k, 0) + h, h)
            a = jnp.where(inside, a * pltpu.roll(a, 8 - k, 0), a)
        h = h + a * after
        dstates[at] = h
        return jnp.broadcast_to((own_decay * h)[0:1], (8, width))

    carry[...] = lax.fori_loop(0, rows // 8, step, carry[...])

    d_h = dstates[...]
    mixed = mixed_ref[...]
    inflow = jax.nn.sigmoid(inflow_ref[...])
    root = jnp.sqrt(less_exp(-2.0 * log_decay))
    factor = reset + kept * root
    decay = decays[...]
    twice = jnp.exp(2.0 * log_decay)
    d_log = d_h * before_ref[...] * decay - d_h * inflow * mixed * kept * (twice / root)
    d_lru = jnp.sum(d_log * rate, axis=0, keepdims=True) * (-rate_scale * spread_slope)
    d_rate = (d_log * (-rate_scale * spread) * rate * (1.0 - rate)).astype(bf16)
    through = d_h * factor
    d_inflow = (through * mixed * inflow * (1.0 - inflow)).astype(bf16)
    drate_ref[...] = d_rate
    dinflow_ref[...] = d_inflow
    for b in range(2):
        lanes = slice(b * block, (b + 1) * block)
        dm_ext[0:rows, lanes] = (
            ((through * inflow)[:, lanes] + dot_t(d_rate[:, lanes], blocks_ref[0, b]) + dot_t(d_inflow[:, lanes], blocks_ref[1, b]))
            .astype(bf16)
            .astype(f32)
        )
    d_mixed = dm_ext[0:rows]
    inner = is_ref[:, :width].astype(bf16).astype(f32)
    shifted = [d_mixed] + [dm_ext[k : k + rows] * marks_ref[:, 3 + k : 4 + k] for k in (1, 2, 3)]
    d_inner = small_ref[2:3] * shifted[0]
    for k in (1, 2, 3):
        d_inner = d_inner + small_ref[2 + k : 3 + k] * shifted[k]
    dib_ref[:, :width] = (d_inner * own).astype(bf16)

    def add(row, value):
        sums_ref[row : row + 1] += value

    add(0, jnp.sum(d_rate.astype(f32), axis=0, keepdims=True))
    add(1, jnp.sum(d_inflow.astype(f32), axis=0, keepdims=True))
    for k in range(4):
        add(2 + k, jnp.sum(shifted[k] * inner, axis=0, keepdims=True))
    add(6, jnp.sum(d_mixed, axis=0, keepdims=True))
    add(7, d_lru)

    @pl.when(pl.program_id(0) == pl.num_programs(0) - 1)
    def _():
        for k in (1, 2, 3):
            for t in range(k):
                add(2 + k, dm_ext[t : t + 1] * marks_ref[t : t + 1, k : k + 1] * rim_ref[8 + t - k : 9 + t - k])

    dm_ext[rows : rows + 8] = dm_ext[0:8]


def row_spec(rows, width, steps, reverse):
    if reverse:
        return pl.BlockSpec((rows, width), lambda i: (steps - 1 - i, 0))
    return pl.BlockSpec((rows, width), lambda i: (i, 0))


def whole_spec(shape):
    return pl.BlockSpec(shape, lambda i: (0,) * len(shape))


def middle_forward(wide, marks, blocks, small, rim, first):
    tokens, width = wide.shape[0], wide.shape[1] // 2
    rows = min(256, tokens)
    steps = tokens // rows
    here = partial(row_spec, rows, steps=steps, reverse=False)
    whole = [blocks, small, rim, first]
    kinds = [bf16, f32, f32, f32, f32, f32]
    return pl.pallas_call(
        partial(middle_forward_body, rows, width),
        grid=(steps,),
        out_shape=[jax.ShapeDtypeStruct((tokens, width), kind) for kind in kinds],
        in_specs=[here(2 * width), here(8)] + [whole_spec(a.shape) for a in whole],
        out_specs=[here(width)] * 6,
        scratch_shapes=[
            pltpu.VMEM((rows + 8, width), f32),
            pltpu.VMEM((rows, width), f32),
            pltpu.VMEM((rows, width), f32),
            pltpu.VMEM((8, width), f32),
        ],
        compiler_params=pltpu.CompilerParams(vmem_limit_bytes=VMEM_LIMIT),
    )(wide, marks, *whole)


def middle_backward(d_gated, wide, saved, marks, blocks, small, rim, own):
    tokens, width = d_gated.shape
    rows = min(256, tokens)
    steps = tokens // rows
    here = partial(row_spec, rows, steps=steps, reverse=True)
    whole = [blocks, small, rim, own]
    return pl.pallas_call(
        partial(middle_backward_body, rows, width),
        grid=(steps,),
        out_shape=[
            jax.ShapeDtypeStruct((tokens, 2 * width), bf16),
            jax.ShapeDtypeStruct((tokens, width), bf16),
            jax.ShapeDtypeStruct((tokens, width), bf16),
            jax.ShapeDtypeStruct((8, width), f32),
        ],
        in_specs=[here(width), here(2 * width)] + [here(width)] * 5 + [here(8)] + [whole_spec(a.shape) for a in whole],
        out_specs=[here(2 * width), here(width), here(width), whole_spec((8, width))],
        scratch_shapes=[
            pltpu.VMEM((rows + 8, width), f32),
            pltpu.VMEM((rows, width), f32),
            pltpu.VMEM((rows, width), f32),
            pltpu.VMEM((8, width), f32),
        ],
        compiler_params=pltpu.CompilerParams(vmem_limit_bytes=VMEM_LIMIT),
    )(d_gated, wide, *saved, marks, *whole)


def grads_mlp(normed, d_both, hidden, d_all, sections, count, lanes):
    tokens, model = normed.shape
    d_rows = model // count
    quarter = d_rows // sections
    chunks = d_both.shape[1] // lanes
    rows = chunks * quarter
    down_rows = hidden.shape[1] // sections
    per_block = rows // down_rows
    down_blocks = model // lanes // per_block

    def body(normed_ref, both_ref, hidden_ref, all_ref, out_ref):
        j = pl.program_id(0)

        @pl.when(j < count)
        def _():
            grad = dot_rows(normed_ref[...], both_ref[...])
            for s in range(sections):
                for ch in range(chunks):
                    out_ref[s, 0, ch * quarter : (ch + 1) * quarter] = grad[
                        s * quarter : (s + 1) * quarter, ch * lanes : (ch + 1) * lanes
                    ].astype(bf16)

        @pl.when(j >= count)
        def _():
            grad = dot_rows(hidden_ref[...], all_ref[...])
            for s in range(sections):
                for ch in range(per_block):
                    out_ref[s, 0, ch * down_rows : (ch + 1) * down_rows] = grad[
                        s * down_rows : (s + 1) * down_rows, ch * lanes : (ch + 1) * lanes
                    ].astype(bf16)

    return pl.pallas_call(
        body,
        grid=(count + down_blocks,),
        out_shape=jax.ShapeDtypeStruct((sections, count + down_blocks, rows, lanes), bf16),
        in_specs=[
            pl.BlockSpec((tokens, d_rows), lambda j: (0, jnp.minimum(j, count - 1))),
            pl.BlockSpec(d_both.shape, lambda j: (0, 0)),
            pl.BlockSpec(hidden.shape, lambda j: (0, 0)),
            pl.BlockSpec((tokens, per_block * lanes), lambda j: (0, jnp.maximum(j - count, 0))),
        ],
        out_specs=pl.BlockSpec((sections, 1, rows, lanes), lambda j: (0, j, 0, 0)),
        compiler_params=pltpu.CompilerParams(vmem_limit_bytes=VMEM_LIMIT),
    )(normed, d_both, hidden, d_all)


def grads_rec(normed, dib, gated, d_all, mixed, d_rate, d_inflow, offset, own_width, sections, count, lanes):
    tokens, model = normed.shape
    window = gated.shape[1]
    block = window // 2
    d_rows = model // count
    quarter = d_rows // sections
    chunks = 2 * own_width // lanes
    gate_rows = block // count // sections
    gate_chunks = block // lanes
    rows = chunks * quarter + 4 * gate_chunks * gate_rows
    out_rows = own_width // sections
    padded = out_rows + 16
    per_block = rows // padded
    out_blocks = model // lanes // per_block

    def body(offset_ref, normed_ref, dib_ref, gated_ref, all_ref, mixed_ref, rate_ref, inflow_ref, out_ref, own, gates, out_grad):
        j = pl.program_id(0)
        first = offset_ref[0]

        @pl.when(j == 0)
        def _():
            row = lax.broadcasted_iota(jnp.int32, (window, own_width), 0)
            column = lax.broadcasted_iota(jnp.int32, (window, own_width), 1)
            pick = (row == column + first).astype(f32).astype(bf16)
            own[...] = jnp.concatenate(
                [dot(dib_ref[:, :window], pick), dot(dib_ref[:, window:], pick)], axis=1
            ).astype(bf16)
            low = mixed_ref[...].astype(bf16)
            for i, ref in enumerate((rate_ref, inflow_ref)):
                for b in range(2):
                    at = slice(b * block, (b + 1) * block)
                    gates[2 * i + b] = dot_rows(low[:, at], ref[:, at])

        @pl.when(j < count)
        def _():
            grad = dot_rows(normed_ref[...], own[...])
            for s in range(sections):
                for ch in range(chunks):
                    out_ref[s, 0, ch * quarter : (ch + 1) * quarter] = grad[
                        s * quarter : (s + 1) * quarter, ch * lanes : (ch + 1) * lanes
                    ].astype(bf16)
                here = pl.ds(pl.multiple_of((j * sections + s) * gate_rows, gate_rows), gate_rows)
                pieces = [
                    gates[g, here, ch * lanes : (ch + 1) * lanes] for g in range(4) for ch in range(gate_chunks)
                ]
                out_ref[s, 0, chunks * quarter :] = jnp.concatenate(pieces, axis=0).astype(bf16)

        @pl.when(j >= count)
        def _():
            out_grad[...] = dot_rows(gated_ref[...], all_ref[...])
            for s in range(sections):
                here = pl.ds(pl.multiple_of(first + s * out_rows, 8), out_rows)
                for ch in range(per_block):
                    out_ref[s, 0, ch * padded : ch * padded + out_rows] = out_grad[
                        here, ch * lanes : (ch + 1) * lanes
                    ].astype(bf16)
                    out_ref[s, 0, ch * padded + out_rows : (ch + 1) * padded] = jnp.zeros((16, lanes), bf16)

    whole = lambda a: pl.BlockSpec(a.shape, lambda j, o, n=a.ndim: (0,) * n)
    return pl.pallas_call(
        body,
        grid_spec=pltpu.PrefetchScalarGridSpec(
            num_scalar_prefetch=1,
            grid=(count + out_blocks,),
            in_specs=[
                pl.BlockSpec((tokens, d_rows), lambda j, o: (0, jnp.minimum(j, count - 1))),
                whole(dib),
                whole(gated),
                pl.BlockSpec((tokens, per_block * lanes), lambda j, o: (0, jnp.maximum(j - count, 0))),
                whole(mixed),
                whole(d_rate),
                whole(d_inflow),
            ],
            out_specs=pl.BlockSpec((sections, 1, rows, lanes), lambda j, o: (0, j, 0, 0)),
            scratch_shapes=[
                pltpu.VMEM((tokens, 2 * own_width), bf16),
                pltpu.VMEM((4, block, block), f32),
                pltpu.VMEM((window, per_block * lanes), f32),
            ],
        ),
        out_shape=jax.ShapeDtypeStruct((sections, count + out_blocks, rows, lanes), bf16),
        compiler_params=pltpu.CompilerParams(vmem_limit_bytes=VMEM_LIMIT),
    )(offset.reshape(1), normed, dib, gated, d_all, mixed, d_rate, d_inflow)


def place_mlp(swapped, shared, quarter, hidden_part):
    layers = len(swapped)
    count, sections, rows, lanes = swapped[0].shape
    chunks = rows // quarter
    half = chunks // 2
    model = shared[0].shape[1] // (hidden_part // sections) * lanes
    down_rows = hidden_part // sections

    def columns_body(*refs):
        gate_ref, up_ref = refs[layers:]
        for l in range(layers):
            for s in range(sections):
                for ch in range(chunks):
                    target = gate_ref if ch < half else up_ref
                    at = ch % half
                    target[l, s * quarter : (s + 1) * quarter, at * lanes : (at + 1) * lanes] = refs[l][
                        0, s, ch * quarter : (ch + 1) * quarter
                    ].astype(f32)

    wide = jax.ShapeDtypeStruct((layers, sections * quarter, count * hidden_part), f32)
    gate, up = pl.pallas_call(
        columns_body,
        grid=(count,),
        out_shape=[wide, wide],
        in_specs=[pl.BlockSpec((1, sections, rows, lanes), lambda q: (q, 0, 0, 0))] * layers,
        out_specs=[pl.BlockSpec((layers, sections * quarter, hidden_part), lambda q: (0, 0, q))] * 2,
        compiler_params=pltpu.CompilerParams(vmem_limit_bytes=VMEM_LIMIT),
    )(*swapped)

    def rows_body(*refs):
        for l in range(layers):
            for ch in range(model // lanes):
                refs[layers][l, :, ch * lanes : (ch + 1) * lanes] = refs[l][
                    0, ch * down_rows : (ch + 1) * down_rows
                ].astype(f32)

    down = pl.pallas_call(
        rows_body,
        grid=(sections,),
        out_shape=jax.ShapeDtypeStruct((layers, hidden_part, model), f32),
        in_specs=[pl.BlockSpec((1,) + shared[0].shape[1:], lambda s: (s, 0, 0))] * layers,
        out_specs=pl.BlockSpec((layers, down_rows, model), lambda s: (0, s, 0)),
        compiler_params=pltpu.CompilerParams(vmem_limit_bytes=VMEM_LIMIT),
    )(*shared)
    return gate, up, down


def place_rec(swapped, shared, quarter, own_width):
    layers = len(swapped)
    count, sections, _, lanes = swapped[0].shape
    chunks = 2 * own_width // lanes
    out_rows = own_width // sections
    padded = out_rows + 16
    model = shared[0].shape[1] // padded * lanes

    def body(*refs):
        in_ref, side_ref, out_ref = refs[2 * layers :]
        for l in range(layers):

            @pl.when(pl.program_id(0) == l)
            def _(l=l):
                for q in range(count):
                    for s in range(sections):
                        rows = slice(s * quarter, (s + 1) * quarter)
                        for ch in range(chunks):
                            value = refs[l][q, s, ch * quarter : (ch + 1) * quarter].astype(f32)
                            first, last = ch * lanes, (ch + 1) * lanes
                            base = q * own_width
                            if first < own_width:
                                end = min(last, own_width)
                                in_ref[0, rows, base + first : base + end] = value[:, : end - first]
                            if last > own_width:
                                begin = max(first, own_width)
                                side_ref[0, rows, base + begin - own_width : base + last - own_width] = value[
                                    :, begin - first :
                                ]
                for s in range(sections):
                    for ch in range(model // lanes):
                        out_ref[0, s * out_rows : (s + 1) * out_rows, ch * lanes : (ch + 1) * lanes] = refs[
                            layers + l
                        ][s, ch * padded : ch * padded + out_rows].astype(f32)

    wide = jax.ShapeDtypeStruct((layers, sections * quarter, count * own_width), f32)
    arrays = list(swapped) + list(shared)
    return pl.pallas_call(
        body,
        grid=(layers,),
        out_shape=[wide, wide, jax.ShapeDtypeStruct((layers, own_width, model), f32)],
        in_specs=[pl.BlockSpec(a.shape, lambda l, n=a.ndim: (0,) * n) for a in arrays],
        out_specs=[
            pl.BlockSpec((1, sections * quarter, count * own_width), lambda l: (l, 0, 0)),
            pl.BlockSpec((1, sections * quarter, count * own_width), lambda l: (l, 0, 0)),
            pl.BlockSpec((1, own_width, model), lambda l: (l, 0, 0)),
        ],
        compiler_params=pltpu.CompilerParams(vmem_limit_bytes=VMEM_LIMIT),
    )(*arrays)


def stream_marks(starts, tokens):
    places = jnp.arange(tokens + 3, dtype=jnp.int32)

    def resets(p):
        return jnp.any(p[:, None] == starts[None, :], axis=1).astype(f32)

    first = 1.0 - resets(places)
    second = first * (1.0 - resets(places - 1))
    third = second * (1.0 - resets(places - 2))
    inside = (places < tokens).astype(f32)
    columns = [resets(places)[:tokens], first[:tokens], second[:tokens], third[:tokens]]
    for k, keep in ((1, first), (2, second), (3, third)):
        columns.append((keep * inside)[k : k + tokens])
    columns.append(jnp.zeros((tokens,), f32))
    return jnp.stack(columns, axis=1)


def on_device(
    inputs,
    doc_starts,
    valid_mask,
    cotangent,
    prev_state,
    prev_inputs,
    rec_gain,
    in_weight,
    side_weight,
    out_weight,
    rate_blocks,
    inflow_blocks,
    rate_bias,
    inflow_bias,
    conv_taps,
    conv_bias,
    lru_param,
    mlp_gain,
    gate_weight,
    up_weight,
    down_weight,
):
    sections = lax.axis_size("section")
    section = lax.axis_index("section")
    count = lax.axis_size("seq")
    place = lax.axis_index("seq")
    layers, d_rows, lru_width = in_weight.shape
    model = inputs.shape[2]
    tokens = inputs.shape[1] * count
    hidden_part = down_weight.shape[1]
    own_width = out_weight.shape[1]
    block_count, block_rows, block_width = rate_blocks.shape[1:]
    window = 2 * block_width
    quarter = d_rows // sections
    block_quarter = block_rows // sections
    first_block = [min(q * own_width // block_width, block_count - 2) for q in range(count)]
    owner = [min(q for q in range(count) if first_block[q] <= b <= first_block[q] + 1) for b in range(block_count)]
    block_start = jnp.asarray(first_block, jnp.int32)[place]
    offset = place * own_width - block_start * block_width
    window_start = block_start * block_width
    next_id = iter(range(64))

    def window_of(a, axis):
        return lax.dynamic_slice_in_dim(a, window_start, window, axis)

    x0 = lax.dynamic_index_in_dim(inputs, section, 0, False)
    cot = lax.dynamic_index_in_dim(cotangent, section, 0, False)
    valid = lax.dynamic_index_in_dim(valid_mask, section, 0, False)

    gate_blocks = jnp.stack([rate_blocks, inflow_blocks])

    def block_of(target):
        block = target * own_width // block_width
        return block - block // (block_count - 1)

    def rows_here():
        return pl.ds(pl.multiple_of(lax.axis_index("section") * quarter, quarter), quarter)

    def send_rec(l):
        def cut(refs, target):
            lanes = pl.ds(pl.multiple_of(block_of(target) * block_width, block_width), window)
            return [ref.at[l, rows_here(), lanes] for ref in refs]

        def fill(view):
            return [view.at[:, pl.ds(i * window, window)] for i in range(2)]

        wide = Spread(
            [in_weight, side_weight],
            (count, sections, quarter, 2 * window),
            2,
            cut,
            fill,
            lambda out, source, s: out.at[source, s],
        )

        def cut_gates(refs, target):
            s = lax.axis_index("section")
            return [refs[0].at[s // 2, l, block_of(target) + s % 2]]

        gates = Spread(
            [gate_blocks],
            (sections, count, block_rows, block_width),
            1,
            cut_gates,
            lambda view: [view],
            lambda out, source, s: out.at[s, source],
        )
        return [wide, gates]

    def send_mlp(l):
        shape = (count, sections, quarter, 2 * hidden_part)
        if hidden_part % 128:
            pair = [
                lax.dynamic_slice_in_dim(a[l], section * quarter, quarter, 0).reshape(quarter, count, hidden_part)
                for a in (gate_weight, up_weight)
            ]
            packed = jnp.transpose(jnp.concatenate(pair, axis=2), (1, 0, 2))
            return [
                Spread(
                    [packed],
                    shape,
                    1,
                    lambda refs, target: [refs[0].at[target]],
                    lambda view: [view],
                    lambda out, source, s: out.at[source, s],
                )
            ]

        def cut(refs, target):
            lanes = pl.ds(pl.multiple_of(target * hidden_part, hidden_part), hidden_part)
            return [ref.at[l, rows_here(), lanes] for ref in refs]

        def fill(view):
            return [view.at[:, pl.ds(i * hidden_part, hidden_part)] for i in range(2)]

        return [
            Spread(
                [gate_weight, up_weight],
                shape,
                2,
                cut,
                fill,
                lambda out, source, s: out.at[source, s],
            )
        ]

    def unpack_rec(wide, gates):
        return wide.reshape(model, 2 * window), gates.reshape(2, 2, block_width, block_width)

    reach = window - own_width

    def out_window(strip):
        return lax.dynamic_slice_in_dim(strip, reach - offset, window, 0)

    packed = jnp.concatenate(
        [rate_bias[:, None], inflow_bias[:, None], conv_taps, conv_bias[:, None], lru_param[:, None]], axis=1
    )
    gains_own = jnp.stack([rec_gain, mlp_gain], axis=1)
    flat = jnp.concatenate([packed.reshape(-1), gains_own.reshape(-1)]).reshape(16, -1)
    x_all, flat, *got = comm("start", next(next_id), x=x0, jobs=[Everyone(flat, count)] + send_rec(0))
    flat = flat.reshape(count, -1)
    small_all = flat[:, : packed.size].reshape(count, layers, 8, own_width)
    small_all = jnp.transpose(small_all, (1, 2, 0, 3)).reshape(layers, 8, lru_width)
    gains = flat[:, packed.size :].reshape(count, layers, 2, d_rows)
    gains = jnp.transpose(gains, (1, 2, 0, 3)).reshape(layers, 2, model)
    small = window_of(small_all, 2).astype(f32)
    x_wide = x_all.astype(f32)
    scale = lax.rsqrt(jnp.mean(x_wide * x_wide, axis=-1, keepdims=True) + epsilon)
    normed = (x_wide * scale * gains[0, 0].astype(f32)).astype(bf16)

    masked = (cot.astype(f32) * valid[:, None].astype(f32)).astype(bf16)
    marks = stream_marks(lax.dynamic_index_in_dim(doc_starts, section, 0, False), tokens)
    first_state = window_of(lax.dynamic_index_in_dim(prev_state, section, 0, False), 1).astype(f32)
    first_state = jnp.broadcast_to(first_state[:, None], (layers, 8, window))
    rim = window_of(lax.dynamic_index_in_dim(prev_inputs, section, 0, False), 2).astype(f32)
    rim = jnp.concatenate([jnp.zeros((layers, 5, window), f32), rim], axis=1)
    channel = jnp.arange(window, dtype=jnp.int32)
    own = jnp.logical_and(channel >= offset, channel < offset + own_width).astype(f32)
    own = jnp.broadcast_to(own[None], (8, window))
    own_out = [
        lax.dynamic_update_slice(jnp.zeros((window, model), bf16), out_weight[l], (offset, 0)) for l in range(layers)
    ]

    x = x0
    kept = []
    rec_weights, mlp_weights = [], []
    for l in range(layers):
        wide_weight, gates = unpack_rec(*got)
        rec_weights.append((wide_weight, gates))
        wide = dot(normed, wide_weight)
        gated, *saved = middle_forward(wide, marks, gates, small[l], rim[l], first_state[l])
        part = dot(gated, own_out[l]).astype(bf16)
        kept.append((x, normed, wide, gated, saved))
        normed, x, *got = comm("forward", next(next_id), part, x, gain=gains[l, 1], jobs=send_mlp(l))
        mlp_weights.append(got[0].reshape(model, 2 * hidden_part))
        if l == 0:
            masked_all = lax.all_gather(lax.optimization_barrier((masked, x))[0], "seq", axis=0, tiled=True)
        both = dot(normed, mlp_weights[l])
        hidden = (jax.nn.gelu(both[:, :hidden_part]) * both[:, hidden_part:]).astype(bf16)
        part = dot(hidden, down_weight[l]).astype(bf16)
        kept.append((x, normed, both, hidden))
        if l + 1 < layers:
            normed, x, *got = comm("forward", next(next_id), part, x, gain=gains[l + 1, 0], jobs=send_rec(l + 1))
        else:
            last_part, last_x = part, x

    mlp_lanes = np.gcd(256, hidden_part).item()
    rec_lanes = np.gcd(128, 2 * own_width).item()

    def by_target(grad, lanes):
        chunks = grad.shape[1] // lanes
        grad = grad.astype(bf16).reshape(count, sections, quarter, chunks, lanes)
        return jnp.transpose(grad, (1, 0, 3, 2, 4)).reshape(sections, count, chunks * quarter, lanes)

    def by_section(grad, lanes):
        rows, chunks = grad.shape[0] // sections, grad.shape[1] // lanes
        grad = grad.astype(bf16).reshape(sections, rows, chunks, lanes)
        return jnp.transpose(grad, (0, 2, 1, 3)).reshape(sections, chunks * rows, lanes)

    def gates_by_target(grad, lanes):
        chunks = block_width // lanes
        grad = grad.astype(bf16).reshape(2, 2, count, sections, block_quarter, chunks, lanes)
        return jnp.transpose(grad, (3, 2, 0, 1, 5, 4, 6)).reshape(sections, count, -1, lanes)

    direct = hidden_part % 256 == 0 and rec_lanes == 128 and own_width % 64 == 0

    def bundle(swapped, shared):
        lanes = swapped.shape[3]
        return jnp.concatenate([swapped.reshape(sections, -1, lanes), shared], axis=1)

    def scatter(whole, rows):
        whole = whole.reshape(-1, whole.shape[-1])
        mine = lax.psum_scatter(whole, "section", scatter_dimension=0, tiled=True)
        return grad_jobs(mine, rows)

    def grad_jobs(mine, rows):
        def cut(refs, target):
            return [refs[0].at[pl.ds(pl.multiple_of(target * rows, 8), rows)]]

        return [
            Spread(
                [mine],
                (count, sections, rows, mine.shape[1]),
                1,
                cut,
                lambda view: [view],
                lambda out, source, s: out.at[source, s],
            ),
            Share(mine, count * rows, mine.shape[0] - count * rows),
        ]

    d_rows_own, d_all = masked, masked_all
    dgains = [[None, None] for _ in range(layers)]
    waiting, spread, sums_own = {}, {}, [None] * layers
    for l in reversed(range(layers)):
        x, normed, both, hidden = kept[2 * l + 1]
        d_hidden = dot_t(d_all, down_weight[l])
        gate, slope = gelu_pair(both[:, :hidden_part])
        d_gate = (d_hidden * both[:, hidden_part:] * slope).astype(bf16)
        d_up = (d_hidden * gate).astype(bf16)
        d_both = jnp.concatenate([d_gate, d_up], axis=1)
        part = dot_t(d_both, mlp_weights[l]).astype(bf16)
        if direct:
            whole = grads_mlp(normed, d_both, hidden, d_all, sections, count, mlp_lanes)
        else:
            down = by_section(dot_rows(hidden, d_all), mlp_lanes)
            whole = bundle(by_target(dot_rows(normed, d_both), mlp_lanes), down)
        part, whole = lax.optimization_barrier((part, whole))
        waiting["mlp", l] = scatter(whole, 2 * hidden_part // mlp_lanes * quarter)
        jobs = waiting["mlp", l + 1] if l + 1 < layers else []
        d_all, d_rows_own, dgains[l][1], strip, *got = comm(
            "back", next(next_id), part, x, d_rows_own, gains[l, 1], [Beside(out_weight, l, reach)] + jobs
        )
        if jobs:
            spread["mlp", l + 1] = got

        x, normed, wide, gated, saved = kept[2 * l]
        wide_weight, gates = rec_weights[l]
        d_gated = dot_t(d_all, out_window(strip))
        dib, d_rate, d_inflow, sums = middle_backward(
            d_gated, wide, saved, marks, gates, small[l], rim[l], own
        )
        part = dot_t(dib, wide_weight).astype(bf16)
        if direct:
            whole = grads_rec(
                normed, dib, gated, d_all, saved[0], d_rate, d_inflow, offset, own_width, sections, count, rec_lanes
            )
        else:
            grad_out = lax.dynamic_slice_in_dim(dot_rows(gated, d_all), offset, own_width, 0)
            grad_wide = dot_rows(normed, dib)
            swapped = by_target(
                jnp.concatenate(
                    [
                        lax.dynamic_slice_in_dim(grad_wide, offset, own_width, 1),
                        lax.dynamic_slice_in_dim(grad_wide, offset + window, own_width, 1),
                    ],
                    axis=1,
                ),
                rec_lanes,
            )
            low = saved[0].astype(bf16).reshape(tokens, 2, block_width)
            d_gates = jnp.stack([d_rate, d_inflow]).reshape(2, tokens, 2, block_width)
            grad_gates = jnp.einsum("tbi,gtbj->gbij", low, d_gates, preferred_element_type=f32)
            swapped = jnp.concatenate([swapped, gates_by_target(grad_gates, rec_lanes)], axis=2)
            whole = bundle(swapped, by_section(grad_out, rec_lanes))
        sums_own[l] = lax.dynamic_slice_in_dim(sums, offset, own_width, 1)
        part, whole = lax.optimization_barrier((part, whole))
        waiting["rec", l] = scatter(whole, (2 * own_width * quarter + 4 * block_width * block_quarter) // rec_lanes)
        jobs = waiting["rec", l + 1] if l + 1 < layers else []
        if l > 0:
            d_all, d_rows_own, dgains[l][0], *got = comm(
                "back", next(next_id), part, x, d_rows_own, gains[l, 0], jobs
            )
        else:
            input_grad, dgains[l][0], *got = comm("last", next(next_id), part, x, d_rows_own, gains[l, 0], jobs)
        if jobs:
            spread["rec", l + 1] = got

    last_part, last_x, _ = lax.optimization_barrier((last_part, last_x, input_grad))
    outputs, *got = comm("rows", next(next_id), last_part, last_x, jobs=waiting["mlp", 0])
    spread["mlp", 0] = got

    sums_lanes = -(-own_width // 256) * 256
    sums = jnp.pad(jnp.concatenate(sums_own, axis=0), ((0, 0), (0, sums_lanes - own_width)))
    sums = sums.reshape(-1, 256)
    dgain_all = jnp.concatenate([a for pair in dgains for a in pair], axis=0).reshape(2 * layers, count, d_rows)
    dgain_all = jnp.pad(jnp.transpose(dgain_all, (1, 0, 2)), ((0, 0), (0, 8 - 2 * layers), (0, 256 - d_rows)))
    tiny = jnp.concatenate([dgain_all.reshape(-1, 256), sums], axis=0)
    tiny, _ = lax.optimization_barrier((tiny, outputs))
    *got, dgain_all, sums = comm("none", next(next_id), jobs=waiting["rec", 0] + grad_jobs(tiny, 8))
    spread["rec", 0] = got
    sums = jnp.sum(sums, axis=0).reshape(layers, 8, sums_lanes)[:, :, :own_width]
    dgain_all = jnp.sum(dgain_all, axis=(0, 1))[: 2 * layers, :d_rows].reshape(layers, 2, d_rows)

    def both_layers(name):
        return [spread[name, l][0] for l in range(layers)], [spread[name, l][1] for l in range(layers)]

    def columns(parts, first, last, lanes):
        out = []
        for p in parts:
            chunks = p.shape[2] // quarter
            p = p[:, :, : chunks * quarter].reshape(count, sections, chunks, quarter, lanes)
            p = jnp.transpose(p, (1, 3, 0, 2, 4)).reshape(d_rows, count, chunks * lanes)
            out.append(p[:, :, first:last].reshape(d_rows, -1).astype(f32))
        return jnp.stack(out)

    def rows(parts, size, lanes):
        out = []
        for p in parts:
            p = jnp.transpose(p.reshape(sections, -1, size, lanes), (0, 2, 1, 3))
            out.append(p.reshape(sections * size, -1).astype(f32))
        return jnp.stack(out)

    mlp_swapped, mlp_shared = both_layers("mlp")
    rec_swapped, rec_shared = both_layers("rec")
    if direct:
        gate_grad, up_grad, down_grad = place_mlp(mlp_swapped, mlp_shared, quarter, hidden_part)
        in_grad, side_grad, out_grad = place_rec(rec_swapped, rec_shared, quarter, own_width)
    else:
        gate_grad = columns(mlp_swapped, 0, hidden_part, mlp_lanes)
        up_grad = columns(mlp_swapped, hidden_part, 2 * hidden_part, mlp_lanes)
        down_grad = rows(mlp_shared, hidden_part // sections, mlp_lanes)
        in_grad = columns(rec_swapped, 0, own_width, rec_lanes)
        side_grad = columns(rec_swapped, own_width, 2 * own_width, rec_lanes)
        out_grad = rows(rec_shared, own_width // sections, rec_lanes)

    gate_out = []
    for l in range(layers):
        got = rec_swapped[l][:, :, 2 * own_width // rec_lanes * quarter :]
        got = got.reshape(count, sections, 2, 2, block_width // rec_lanes, block_quarter, rec_lanes)
        blocks = jnp.stack([got[owner[b], :, :, b - first_block[owner[b]]] for b in range(block_count)])
        blocks = jnp.transpose(blocks, (2, 0, 1, 4, 3, 5))
        gate_out.append(blocks.reshape(2, block_count, block_rows, block_width))
    gate_out = jnp.stack(gate_out).astype(f32)

    return (
        outputs[None],
        input_grad[None],
        dgain_all[:, 0],
        in_grad,
        side_grad,
        out_grad,
        gate_out[:, 0],
        gate_out[:, 1],
        sums[:, 0],
        sums[:, 1],
        sums[:, 2:6],
        sums[:, 6],
        sums[:, 7],
        dgain_all[:, 1],
        gate_grad,
        up_grad,
        down_grad,
    )


def solution(mesh):
    return jax.shard_map(
        on_device,
        mesh=mesh,
        in_specs=(
            P(None, "seq", None),
            P(),
            P(None, "seq"),
            P(None, "seq", None),
            P(),
            P(),
            P(None, "seq"),
            P(None, "seq", None),
            P(None, "seq", None),
            P(None, "seq", None),
            P(None, None, "seq", None),
            P(None, None, "seq", None),
            P(None, "seq"),
            P(None, "seq"),
            P(None, None, "seq"),
            P(None, "seq"),
            P(None, "seq"),
            P(None, "seq"),
            P(None, "seq", None),
            P(None, "seq", None),
            P(None, "seq", None),
        ),
        out_specs=(
            P("section", "seq", None),
            P("section", "seq", None),
            P(None, "seq"),
            P(None, "seq", None),
            P(None, "seq", None),
            P(None, "seq", None),
            P(None, None, "seq", None),
            P(None, None, "seq", None),
            P(None, "seq"),
            P(None, "seq"),
            P(None, None, "seq"),
            P(None, "seq"),
            P(None, "seq"),
            P(None, "seq"),
            P(None, "seq", None),
            P(None, "seq", None),
            P(None, "seq", None),
        ),
        check_vma=False,
    )
```

time: 1540 us -> 1260 us (0.82)
  waiting for transfers between devices: 322 us -> 0.17 us
  Pallas kernels: 774 us -> 1090 us
  local copies, waits for them, and re-layouts: 172 us -> 31.3 us
  blocking collectives: 82.5 us -> 0 us
  matrix products: 117 us -> 86.5 us
  other arithmetic: 39.3 us -> 17 us
    pallas_call x17, Pallas kernels: 736 us -> 1060 us  [the longest x10 970 us: comm(): pl.pallas_call(lambda *refs: comm_body(mode, count, jobs, refs), out_shap...]
    psum x1 -> x0, waiting for transfers between devices: 161 us -> none  [on_device(): grads['out', l] = lax.psum(grad_out.astype(bf16), 'section')]
    all_gather x11 -> x1, waiting for transfers between devices: 81.3 us -> 0.02 us  [on_device(): lax.all_gather(lax.optimization_barrier((masked, x))[0], 'seq', axis=0, t...]
    reduce_scatter x5 -> x4, waiting for transfers between devices: 79.2 us -> 0.07 us  [scatter(): mine = lax.psum_scatter(whole, 'section', scatter_dimension=0, tiled=True)]
    convert_element_type x20 -> x0, local copies, waits for them, and re-layouts: 72.3 us -> none  [spread_rows(): return jnp.transpose(part, (0, 2, 1, 3)).reshape(d_rows, -1).astype(f32)]
    psum x2 -> x0, blocking collectives: 57.5 us -> none  [the longest x1 43.2 us: on_device(): dgain_all = lax.psum(dgain_all, ('section', 'seq'))]
    dot_general x10 -> x0, matrix products: 29.6 us -> none  [the longest x8 28.8 us: dot_rows(): lax.dot_general(a, b, (((0,), (0,)), ((), ())), preferred_element_type=f32)]
    all_gather x1 -> x0, blocking collectives: 24.9 us -> none  [on_device(): flat = lax.all_gather(flat, 'seq', axis=0)]
  transfers between devices with their start and end apart: 17 -> 5, of which waited for: 6 -> 0; matrix products, arithmetic and copies ran while one was open for 17% -> 6% of each run, Pallas kernels for 50% -> 66%
where the time goes in v2:
time: 1260 us; the launch traced here: 1250 us
  Pallas kernels  1090 us (87%)
  matrix products  86.5 us (7%)
  local copies, waits for them, and re-layouts  31.3 us (2%)
  other arithmetic  17 us (1%)
  between operations  15.7 us (1%)
    pallas_call x10, Pallas kernels, comm(): pl.pallas_call(lambda *refs: comm_body(mode, count, jobs, refs), out_shap...  970 us
    dot_general x8, matrix products, dot_t(): lax.dot_general(a, b, (((1,), (1,)), ((), ())), preferred_element_type=f32)  44.8 us
    dot_general x8, matrix products, dot(): return jnp.dot(a, b, preferred_element_type=f32)  41.6 us
    pallas_call x2, Pallas kernels, grads_mlp(): pl.pallas_call(body, grid=(count + down_blocks,), out_shape=jax.ShapeDtyp...  27.2 us
    pallas_call x2, Pallas kernels, grads_rec(): pl.pallas_call(body, grid_spec=pltpu.PrefetchScalarGridSpec(num_scalar_pr...  26.3 us
  transfers between devices with their start and end apart: 5, of which 0 were waited for; matrix products, arithmetic and copies ran while one was open for 6% of the time, Pallas kernels for 66%

profile of v2, /device:TPU:18, one launch (start us, length us, event | category | flops | bytes accessed | tf_op | source)
XLA Modules:
  0.0 1245.1 jit_solution(13205790184483674605)
XLA Ops:
  14.9 76.1 %shard_map.341 = (bf16[8,64,2048]{2,1,0:T(8,128)(2,1)}, bf16[8,16,384]{2,1,0:T(8,128)(2,1)}, bf16[8,4,64,1024]{3,2,1,0:T(8,128)(2,1)}, bf16[4,8,32,256]{3,2,1,0:T(8,128)(2,1)}) custom-call(bf16[64,2048]{1,0:T(8,128)(2,1)} %dynamic-slice_bitcast_fusion.refs_0_.refs_1_, bf16[16,384]{1,0:T(8,128)(2,1)} %reshape.300.refs_1_, bf16[2,256,2560]{2,1,0:T(8,128)(2,1)} %refs_3_.6, ...), custom_call_target="tpu_custom_call" | custom-call | flops 49999998976 | bytes 1000000 | tf_op jit(solution)/shard_map/pallas_call | solution.py:486
  110.0 7.1 shard_map.342
  123.2 106.4 %shard_map.343 = (bf16[8,64,2048]{2,1,0:T(8,128)(2,1)}, bf16[64,2048]{1,0:T(8,128)(2,1)}, bf16[8,4,64,1536]{3,2,1,0:T(8,128)(2,1)}) custom-call(bf16[8,64,2048]{2,1,0:T(8,128)(2,1)} %bitcast.393, bf16[64,2048]{1,0:T(8,128)(2,1)} %dynamic-slice_bitcast_fusion.refs_0_.refs_1_, f32[1,2048]{1,0:T(1,128)} %get-tuple-element.205.refs_2_.refs_3_, ...), custom_call_target="tpu_custom_call" | custom-call | flops 49999998976 | bytes 1000000 | tf_op jit(solution)/shard_map/pallas_call | solution.py:486
  244.9 108.0 %shard_map.344 = (bf16[8,64,2048]{2,1,0:T(8,128)(2,1)}, bf16[64,2048]{1,0:T(8,128)(2,1)}, bf16[8,4,64,1024]{3,2,1,0:T(8,128)(2,1)}, bf16[4,8,32,256]{3,2,1,0:T(8,128)(2,1)}) custom-call(bf16[8,64,2048]{2,1,0:T(8,128)(2,1)} %bitcast.394, bf16[64,2048]{1,0:T(8,128)(2,1)} %get-tuple-element.99.refs_1_, f32[1,2048]{1,0:T(1,128)} %get-tuple-element.204.refs_2_.refs_3_, ...), custom_call_target="tpu_custom_call" | custom-call | flops 49999998976 | bytes 1000000 | tf_op jit(solution)/shard_map/pallas_call | solution.py:486
  360.0 7.1 shard_map.345
  371.4 114.8 %shard_map.346 = (bf16[8,64,2048]{2,1,0:T(8,128)(2,1)}, bf16[64,2048]{1,0:T(8,128)(2,1)}, bf16[8,4,64,1536]{3,2,1,0:T(8,128)(2,1)}) custom-call(bf16[8,64,2048]{2,1,0:T(8,128)(2,1)} %bitcast.395, bf16[64,2048]{1,0:T(8,128)(2,1)} %get-tuple-element.104.refs_1_, f32[1,2048]{1,0:T(1,128)} %get-tuple-element.203.refs_2_.refs_3_, bf16[2,256,6144]{2,1,0:T(8,128)(2,1)} %refs_3_.7, ...), custom_call_target="tpu_custom_call" | custom-call | flops 49999998976 | bytes 1000000 | tf_op jit(solution)/shard_map/pallas_call | solution.py:486
  486.2 6.6 fusion.78
  492.8 6.8 fusion.48
  505.5 13.5 %shard_map.347 = bf16[4,12,384,256]{3,2,1,0:T(8,128)(2,1)} custom-call(bf16[512,2048]{1,0:T(8,128)(2,1)} %bitcast.316, bf16[512,1536]{1,0:T(8,128)(2,1)} %pad_maximum_fusion.both_ref, bf16[512,768]{1,0:T(8,128)(2,1)} %get-tuple-element.191.hidden_ref, bf16[512,2048]{1,0:T(8,128)(2,1)} %all-gather.2.cloned.1.call-done.all_ref), custom_call_target="tpu_custom_call" | custom-call | tf_op jit(solution)/shard_map/pallas_call | solution.py:806
  519.0 74.6 %shard_map.348 = (bf16[8,64,2048]{2,1,0:T(8,128)(2,1)}, bf16[64,2048]{1,0:T(8,128)(2,1)}, f32[1,2048]{1,0:T(1,128)}, bf16[704,2048]{1,0:T(8,128)(2,1)}) custom-call(bf16[8,64,2048]{2,1,0:T(8,128)(2,1)} %bitcast.389, bf16[64,2048]{1,0:T(8,128)(2,1)} %get-tuple-element.141.refs_1_, bf16[64,2048]{1,0:T(8,128)(2,1)} %fusion.56.refs_2_, ...), custom_call_target="tpu_custom_call" | custom-call | flops 49999998976 | bytes 1000000 | tf_op jit(solution)/shard_map/pallas_call | solution.py:486
  598.7 11.8 shard_map.349
  610.5 13.2 %shard_map.350 = bf16[4,12,384,128]{3,2,1,0:T(8,128)(2,1)} custom-call(s32[1]{0:T(128)} %bitcast.53.offset_ref, bf16[512,2048]{1,0:T(8,128)(2,1)} %bitcast.310, bf16[512,1024]{1,0:T(8,128)(2,1)} %get-tuple-element.117.dib_ref, bf16[512,512]{1,0:T(8,128)(2,1)} %get-tuple-element.103.gated_ref, bf16[512,2048]{1,0:T(8,128)(2,1)} %bitcast.314, ...), custom_call_target="tpu_custom_call" | custom-call | tf_op jit(solution)/shard_map/pallas_call | solution.py:880
  629.7 55.0 %shard_map.351 = (bf16[8,64,2048]{2,1,0:T(8,128)(2,1)}, bf16[64,2048]{1,0:T(8,128)(2,1)}, f32[1,2048]{1,0:T(1,128)}) custom-call(bf16[8,64,2048]{2,1,0:T(8,128)(2,1)} %bitcast.392, bf16[64,2048]{1,0:T(8,128)(2,1)} %get-tuple-element.104.refs_1_, bf16[64,2048]{1,0:T(8,128)(2,1)} %get-tuple-element.121.refs_2_, f32[1,2048]{1,0:T(1,128)} %get-tuple-element.204.refs_2_.refs_3_), custom_call_target="tpu_custom_call" | custom-call | flops 49999998976 | bytes 1000000 | tf_op jit(solution)/shard_map/pallas_call | solution.py:486
  692.2 13.7 %shard_map.352 = bf16[4,12,384,256]{3,2,1,0:T(8,128)(2,1)} custom-call(bf16[512,2048]{1,0:T(8,128)(2,1)} %bitcast.308, bf16[512,1536]{1,0:T(8,128)(2,1)} %pad_maximum_fusion.1.both_ref, bf16[512,768]{1,0:T(8,128)(2,1)} %copy-done.4, bf16[512,2048]{1,0:T(8,128)(2,1)} %bitcast.318), custom_call_target="tpu_custom_call" | custom-call | tf_op jit(solution)/shard_map/pallas_call | solution.py:806
  705.9 7.4 convolution_convert_fusion.2
  722.5 172.3 %shard_map.353 = (bf16[8,64,2048]{2,1,0:T(8,128)(2,1)}, bf16[64,2048]{1,0:T(8,128)(2,1)}, f32[1,2048]{1,0:T(1,128)}, bf16[704,2048]{1,0:T(8,128)(2,1)}, bf16[8,4...) custom-call(bf16[8,64,2048]{2,1,0:T(8,128)(2,1)} %bitcast.390, bf16[64,2048]{1,0:T(8,128)(2,1)} %get-tuple-element.99.refs_1_, ...), custom_call_target="tpu_custom_call" | custom-call | flops 49999998976 | bytes 1000000 | tf_op jit(solution)/shard_map/pallas_call | solution.py:486
  899.2 11.9 shard_map.354
  911.1 13.1 %shard_map.355 = bf16[4,12,384,128]{3,2,1,0:T(8,128)(2,1)} custom-call(s32[1]{0:T(128)} %bitcast.53.offset_ref, bf16[512,2048]{1,0:T(8,128)(2,1)} %fusion.1.normed_ref, bf16[512,1024]{1,0:T(8,128)(2,1)} %get-tuple-element.133.dib_ref, bf16[512,512]{1,0:T(8,128)(2,1)} %get-tuple-element.96.gated_ref, bf16[512,2048]{1,0:T(8,128)(2,1)} %bitcast.312, ...), custom_call_target="tpu_custom_call" | custom-call | tf_op jit(solution)/shard_map/pallas_call | solution.py:880
  930.1 91.4 %shard_map.356 = (bf16[64,2048]{1,0:T(8,128)(2,1)}, f32[1,2048]{1,0:T(1,128)}, bf16[8,4,384,128]{3,2,1,0:T(8,128)(2,1)}, bf16[4,1536,128]{2,1,0:T(8,128)(2,1)}) custom-call(bf16[8,64,2048]{2,1,0:T(8,128)(2,1)} %bitcast.391, bf16[64,2048]{1,0:T(8,128)(2,1)} %dynamic-slice_bitcast_fusion.refs_0_.refs_1_, bf16[64,2048]{1,0:T(8,128)(2,1)} %get-tuple-element.137.refs_2_, ...), custom_call_target="tpu_custom_call" | custom-call | flops 49999998976 | bytes 1000000 | tf_op jit(solution)/shard_map/pallas_call | solution.py:486
  1021.7 111.6 %shard_map.357 = (bf16[64,2048]{1,0:T(8,128)(2,1)}, bf16[8,4,384,256]{3,2,1,0:T(8,128)(2,1)}, bf16[4,1536,256]{2,1,0:T(8,128)(2,1)}) custom-call(bf16[8,64,2048]{2,1,0:T(8,128)(2,1)} %bitcast.388, bf16[64,2048]{1,0:T(8,128)(2,1)} %get-tuple-element.141.refs_1_, bf16[4608,256]{1,0:T(8,128)(2,1)} %reduce-scatter.9.cloned.1.call-done.refs_2_.refs_3_, ...), custom_call_target="tpu_custom_call" | custom-call | flops 49999998976 | bytes 1000000 | tf_op jit(solution)/shard_map/pallas_call | solution.py:486
  1135.2 14.0 %shard_map.360 = (f32[2,256,6144]{2,1,0:T(8,128)}, f32[2,256,6144]{2,1,0:T(8,128)}) custom-call(bf16[8,4,384,256]{3,2,1,0:T(8,128)(2,1)} %get-tuple-element.161.refs_0_, bf16[8,4,384,256]{3,2,1,0:T(8,128)(2,1)} %get-tuple-element.162.refs_1_), custom_call_target="tpu_custom_call" | custom-call | tf_op jit(solution)/shard_map/pallas_call | solution.py:926
  1149.2 8.0 shard_map.361
  1157.4 60.4 %shard_map.358 = (bf16[8,4,384,128]{3,2,1,0:T(8,128)(2,1)}, bf16[4,1536,128]{2,1,0:T(8,128)(2,1)}, f32[8,4,8,256]{3,2,1,0:T(8,128)}, f32[4,32,256]{2,1,0:T(8,128)}) custom-call(bf16[4608,128]{1,0:T(8,128)(2,1)} %reduce-scatter.11.cloned.1.call-done.refs_0_.refs_1_, bf16[4608,128]{1,0:T(8,128)(2,1)} %reduce-scatter.11.cloned.1.call-done.refs_0_.refs_1_, ...), custom_call_target="tpu_custom_call" | custom-call | flops 49999998976 | bytes 1000000 | tf_op jit(solution)/shard_map/pallas_call | solution.py:486
  1226.4 10.3 shard_map.359
  (199 shorter events, 114.5 us)
Async XLA Ops:
  7.2 485.6 %all-gather.2.cloned.1.call-start = ((), (), s32[]{:S(2)}) async-start(), calls=%async_computation.4 | async-start | bytes 2359296 | tf_op jit(solution)/shard_map/all_gather | solution.py:1198
  91.1 5.3 copy-start.29
  91.1 9.1 copy-start.2
  92.8 7.9 copy-start.15
  94.9 5.9 copy-start.18
  102.4 5.9 copy-start.7
  229.6 492.8 %reduce-scatter.5.cloned.1.call-start = ((), (), s32[]{:S(2)}) async-start(), calls=%async_computation.5 | async-start | bytes 11796480 | tf_op jit(solution)/shard_map/reduce_scatter | solution.py:1234
  492.8 6.8 copy-start.27
  519.0 411.2 %reduce-scatter.7.cloned.1.call-start = ((), (), s32[]{:S(2)}) async-start(), calls=%async_computation.6 | async-start | bytes 5898240 | tf_op jit(solution)/shard_map/reduce_scatter | solution.py:1234
  610.5 13.2 %copy-start.9 = (bf16[512,1024]{1,0:T(8,128)(2,1)S(1)}, bf16[512,1024]{1,0:T(8,128)(2,1)}, u32[]{:S(2)}) copy-start(bf16[512,1024]{1,0:T(8,128)(2,1)} %get-tuple-element.117.dib_ref) | copy-start | bytes 3145732
  629.6 392.0 %reduce-scatter.9.cloned.1.call-start = ((), (), s32[]{:S(2)}) async-start(), calls=%async_computation.7 | async-start | bytes 11796480 | tf_op jit(solution)/shard_map/reduce_scatter | solution.py:1234
  629.7 55.0 %copy-start.6 = (f32[512,1536]{1,0:T(8,128)S(1)}, f32[512,1536]{1,0:T(8,128)}, u32[]{:S(2)}) copy-start(f32[512,1536]{1,0:T(8,128)} %copy-done.5) | copy-start | bytes 9437188
  692.2 13.7 %copy-start.12 = (bf16[512,768]{1,0:T(8,128)(2,1)S(1)}, bf16[512,768]{1,0:T(8,128)(2,1)}, u32[]{:S(2)}) copy-start(bf16[512,768]{1,0:T(8,128)(2,1)} %copy-done.11) | copy-start | bytes 2359300
  713.3 444.1 %reduce-scatter.11.cloned.1.call-start = ((), (), s32[]{:S(2)}) async-start(), calls=%async_computation.8 | async-start | bytes 5898240 | tf_op jit(solution)/shard_map/reduce_scatter | solution.py:1234
  911.1 13.1 %copy-start.8 = (bf16[512,1024]{1,0:T(8,128)(2,1)S(1)}, bf16[512,1024]{1,0:T(8,128)(2,1)}, u32[]{:S(2)}) copy-start(bf16[512,1024]{1,0:T(8,128)(2,1)} %get-tuple-element.133.dib_ref) | copy-start | bytes 3145732
  1021.6 111.6 %copy-start.21 = (f32[8,512]{1,0:T(8,128)S(1)}, f32[8,512]{1,0:T(8,128)}, u32[]{:S(2)}) copy-start(f32[8,512]{1,0:T(8,128)} %get-tuple-element.149) | copy-start | bytes 49156
  1021.6 111.7 %copy-start.17 = (f32[8,320]{1,0:T(8,128)S(1)}, f32[8,320]{1,0:T(8,128)}, u32[]{:S(2)}) copy-start(f32[8,320]{1,0:T(8,128)} %constant_dynamic-slice_fusion) | copy-start | bytes 30724
  1021.6 111.7 %copy-start.22 = (f32[1,2048]{1,0:T(1,128)S(1)}, f32[1,2048]{1,0:T(1,128)}, u32[]{:S(2)}) copy-start(f32[1,2048]{1,0:T(1,128)} %get-tuple-element.148) | copy-start | bytes 24580
  1021.6 111.7 %copy-start.23 = (f32[1,2048]{1,0:T(1,128)S(1)}, f32[1,2048]{1,0:T(1,128)}, u32[]{:S(2)}) copy-start(f32[1,2048]{1,0:T(1,128)} %get-tuple-element.147) | copy-start | bytes 24580
  1021.6 111.7 %copy-start.24 = (f32[1,2048]{1,0:T(1,128)S(1)}, f32[1,2048]{1,0:T(1,128)}, u32[]{:S(2)}) copy-start(f32[1,2048]{1,0:T(1,128)} %get-tuple-element.146) | copy-start | bytes 24580
  1021.7 111.7 %copy-start.25 = (f32[1,2048]{1,0:T(1,128)S(1)}, f32[1,2048]{1,0:T(1,128)}, u32[]{:S(2)}) copy-start(f32[1,2048]{1,0:T(1,128)} %get-tuple-element.145) | copy-start | bytes 24580
  1226.4 10.4 copy-start.14
  1226.4 11.1 copy-start.13
  1226.4 11.8 copy-start.1
  (11 other events, 26.1 us)
Sparse Core Ops, SparseCore 0:
  229.8 45.2 all-gather.1
  519.1 101.7 reduce-scatter.4
  629.8 59.4 reduce-scatter.6
  713.4 143.5 reduce-scatter.8
  930.2 90.6 reduce-scatter.10

commit v3 on v2

--- a/solution.py
+++ b/solution.py
@@ -75,6 +75,22 @@
         self.to_up.wait_send()
 
 
+class Keep:
+    def __init__(self, pieces, places, stage, target, sems, out_sem):
+        self.come = [pltpu.make_async_copy(a, b, sems.at[i]) for i, (a, b) in enumerate(zip(pieces, places))]
+        self.go = pltpu.make_async_copy(stage, target, out_sem)
+        for copy in self.come:
+            copy.start()
+
+    def land(self):
+        for copy in self.come:
+            copy.wait()
+        self.go.start()
+
+    def finish(self):
+        self.go.wait()
+
+
 class Spread:
     on_line, in_plane = True, True
 
@@ -83,21 +99,20 @@
         self.shape = jax.ShapeDtypeStruct(shape, self.arrays[0].dtype)
 
     def scratch(self, count):
-        return [dma(2, self.pieces, count), dma(3, 2, count)]
+        return [dma(2, self.pieces, count), dma(3, 2, count), pltpu.VMEM(self.shape.shape[2:], self.shape.dtype)]
 
     def begin(self, refs, out, sems, place, count):
-        line, plane = sems
-        self.own, self.sends, self.items = [], [], []
+        line, plane, stage = sems
+        self.sends, self.items = [], []
         section = plane_place()[0]
-        for i, (piece, there) in enumerate(zip(self.cut(refs, place), self.fill(self.slot(out, place, section)))):
-            copy = pltpu.make_async_copy(piece, there, line.at[0, i, 0])
-            copy.start()
-            self.own.append(copy)
+        self.own = Keep(
+            self.cut(refs, place), self.fill(stage), stage, self.slot(out, place, section), line.at[0, :, 0], line.at[1, 0, 0]
+        )
         for k in range(count):
             source = (place + count - k) % count
             self.items.append(
                 Item(
-                    self.slot(out, source, section),
+                    self.slot(out, source, section) if k > 0 else stage,
                     lambda s, source=source: self.slot(out, source, s),
                     plane,
                     k,
@@ -120,8 +135,7 @@
         self.push = push
 
     def own_block(self):
-        for copy in self.own:
-            copy.wait()
+        self.own.land()
         self.items[0].start()
 
     def arrive(self, k):
@@ -132,6 +146,7 @@
 
     def finish(self):
         self.items[-1].forward()
+        self.own.finish()
         for item in self.items:
             item.finish()
         for group in self.sends:
@@ -139,6 +154,88 @@
                 copy.wait_send()
 
 
+class Line:
+    on_line, in_plane = True, False
+
+    def __init__(self, arrays, shape, pieces, cut, fill):
+        self.arrays, self.pieces, self.cut, self.fill = list(arrays), pieces, cut, fill
+        self.shape = jax.ShapeDtypeStruct(shape, self.arrays[0].dtype)
+
+    def scratch(self, count):
+        return [dma(2, self.pieces, count), pltpu.VMEM(self.shape.shape[1:], self.shape.dtype)]
+
+    def begin(self, refs, out, sems, place, count):
+        line, stage = sems
+        self.sends = []
+        self.own = Keep(
+            self.cut(refs, place), self.fill(stage), stage, out.at[place], line.at[0, :, 0], line.at[1, 0, 0]
+        )
+
+        def push():
+            for k in range(1, count):
+                peer = (place + k) % count
+                pieces = zip(self.cut(refs, peer), self.fill(out.at[place]))
+                group = [
+                    along(piece, there, line.at[0, i, k], line.at[1, i, k], peer)
+                    for i, (piece, there) in enumerate(pieces)
+                ]
+                for copy in group:
+                    copy.start()
+                self.sends.append(group)
+
+        self.push = push
+
+    def own_block(self):
+        self.own.land()
+
+    def arrive(self, k):
+        pass
+
+    def finish(self):
+        self.own.finish()
+        for group in self.sends:
+            for copy in group:
+                copy.wait()
+
+
+class Plane:
+    on_line, in_plane = False, True
+
+    def __init__(self, array, shape, slot, column):
+        self.arrays, self.slot, self.column = [array], slot, column
+        self.shape = jax.ShapeDtypeStruct(shape, array.dtype)
+
+    def scratch(self, count):
+        return [dma(3, 2, count), dma(2), pltpu.VMEM(self.arrays[0].shape, self.shape.dtype)]
+
+    def begin(self, refs, out, sems, place, count):
+        plane, own, stage = sems
+        section = plane_place()[0]
+        self.items = []
+        self.own = Keep([refs[0]], [stage], stage, self.column(out, section), own, own.at[1])
+        for k in range(count):
+            item = Item(refs[0].at[k], lambda s, k=k: self.slot(out, k, s), plane, k, k % 2 == 0)
+            item.start()
+            self.items.append(item)
+
+    def push(self):
+        pass
+
+    def own_block(self):
+        self.own.land()
+
+    def arrive(self, k):
+        if k > 1:
+            self.items[k - 2].forward()
+
+    def finish(self):
+        for item in self.items[-2:]:
+            item.forward()
+        for item in self.items:
+            item.finish()
+        self.own.finish()
+
+
 class Share:
     on_line, in_plane = False, True
 
@@ -147,14 +244,13 @@
         self.shape = jax.ShapeDtypeStruct((4, size, array.shape[1]), array.dtype)
 
     def scratch(self, count):
-        return [dma(3, 2, 2), dma(1)]
+        return [dma(3, 2, 2), dma(2), pltpu.VMEM(self.shape.shape[1:], self.shape.dtype)]
 
     def begin(self, refs, out, sems, place, count):
-        plane, own = sems
+        plane, own, stage = sems
         section = plane_place()[0]
         mine = refs[0].at[pl.ds(self.start, self.size)]
-        self.own = pltpu.make_async_copy(mine, out.at[section], own.at[0])
-        self.own.start()
+        self.own = Keep([mine], [stage], stage, out.at[section], own, own.at[1])
         half = self.size // 2
         self.items = []
         for h in range(2):
@@ -168,13 +264,14 @@
         pass
 
     def own_block(self):
-        self.own.wait()
+        self.own.land()
 
     def arrive(self, k):
         if k in (4, 6):
             self.items[k // 2 - 2].forward()
 
     def finish(self):
+        self.own.finish()
         for item in self.items:
             item.finish()
 
@@ -218,7 +315,7 @@
     def __init__(self, array, layer, reach):
         self.arrays, self.layer, self.reach = [array], layer, reach
         self.rows = array.shape[1]
-        self.shape = jax.ShapeDtypeStruct((self.rows + 2 * reach, array.shape[2]), array.dtype)
+        self.shape = jax.ShapeDtypeStruct((2, reach, array.shape[2]), array.dtype)
         self.sizes = [min(self.rows, reach - at) for at in range(0, reach, self.rows)]
 
     def scratch(self, count):
@@ -226,21 +323,19 @@
 
     def begin(self, refs, out, sems, place, count):
         mine, sem = refs[0].at[self.layer], sems[0]
-        self.own = pltpu.make_async_copy(mine, out.at[pl.ds(self.reach, self.rows)], sem.at[0, 0, 0])
-        self.own.start()
         self.ends = []
         done = 0
         for k, size in enumerate(self.sizes, 1):
             ahead = along(
                 mine.at[pl.ds(self.rows - size, size)],
-                out.at[pl.ds(self.reach - done - size, size)],
+                out.at[0, pl.ds(self.reach - done - size, size)],
                 sem.at[0, 0, k],
                 sem.at[0, 1, k],
                 place + k,
             )
             back = along(
                 mine.at[pl.ds(0, size)],
-                out.at[pl.ds(self.reach + self.rows + done, size)],
+                out.at[1, pl.ds(done, size)],
                 sem.at[1, 0, k],
                 sem.at[1, 1, k],
                 place - k,
@@ -255,7 +350,7 @@
         pass
 
     def own_block(self):
-        self.own.wait()
+        pass
 
     def arrive(self, k):
         pass
@@ -363,6 +458,8 @@
             pair_copies.append((k, copy))
     for job, ref, out, sems in zip(jobs, job_refs, job_outs, job_sems):
         job.begin(ref, out, sems, place, count)
+    for job in jobs:
+        job.push()
     if has_sum:
         sum_copies = []
         total = None
@@ -379,8 +476,6 @@
                 )
                 send.start()
                 sum_copies.append((k, send))
-    for job in jobs:
-        job.push()
     for job in jobs:
         job.own_block()
     for k in range(1, count):
@@ -1077,7 +1172,17 @@
     def rows_here():
         return pl.ds(pl.multiple_of(lax.axis_index("section") * quarter, quarter), quarter)
 
-    def send_rec(l):
+    def natural(out, source, s):
+        return out.at[source, s]
+
+    def by_piece(out, source, s):
+        return out.at[s, source]
+
+    wide_shape = (quarter, 2 * window)
+    gates_shape = (block_rows, block_width)
+    both_shape = (quarter, 2 * hidden_part)
+
+    def wide_pieces(l):
         def cut(refs, target):
             lanes = pl.ds(pl.multiple_of(block_of(target) * block_width, block_width), window)
             return [ref.at[l, rows_here(), lanes] for ref in refs]
@@ -1085,31 +1190,34 @@
         def fill(view):
             return [view.at[:, pl.ds(i * window, window)] for i in range(2)]
 
-        wide = Spread(
-            [in_weight, side_weight],
-            (count, sections, quarter, 2 * window),
-            2,
-            cut,
-            fill,
-            lambda out, source, s: out.at[source, s],
-        )
-
-        def cut_gates(refs, target):
+        return cut, fill
+
+    def gate_pieces(l):
+        def cut(refs, target):
             s = lax.axis_index("section")
             return [refs[0].at[s // 2, l, block_of(target) + s % 2]]
 
-        gates = Spread(
-            [gate_blocks],
-            (sections, count, block_rows, block_width),
-            1,
-            cut_gates,
-            lambda view: [view],
-            lambda out, source, s: out.at[s, source],
-        )
-        return [wide, gates]
-
-    def send_mlp(l):
-        shape = (count, sections, quarter, 2 * hidden_part)
+        return cut, lambda view: [view]
+
+    def line_rec(l):
+        return [
+            Line([in_weight, side_weight], (count,) + wide_shape, 2, *wide_pieces(l)),
+            Line([gate_blocks], (count,) + gates_shape, 1, *gate_pieces(l)),
+        ]
+
+    def plane_rec(wide, gates):
+        return [
+            Plane(wide, (count, sections) + wide_shape, natural, lambda out, s: out.at[:, s]),
+            Plane(gates, (sections, count) + gates_shape, by_piece, lambda out, s: out.at[s]),
+        ]
+
+    def spread_rec(l):
+        return [
+            Spread([in_weight, side_weight], (count, sections) + wide_shape, 2, *wide_pieces(l), natural),
+            Spread([gate_blocks], (sections, count) + gates_shape, 1, *gate_pieces(l), by_piece),
+        ]
+
+    def line_mlp(l):
         if hidden_part % 128:
             pair = [
                 lax.dynamic_slice_in_dim(a[l], section * quarter, quarter, 0).reshape(quarter, count, hidden_part)
@@ -1117,13 +1225,12 @@
             ]
             packed = jnp.transpose(jnp.concatenate(pair, axis=2), (1, 0, 2))
             return [
-                Spread(
+                Line(
                     [packed],
-                    shape,
+                    (count,) + both_shape,
                     1,
                     lambda refs, target: [refs[0].at[target]],
                     lambda view: [view],
-                    lambda out, source, s: out.at[source, s],
                 )
             ]
 
@@ -1134,23 +1241,18 @@
         def fill(view):
             return [view.at[:, pl.ds(i * hidden_part, hidden_part)] for i in range(2)]
 
-        return [
-            Spread(
-                [gate_weight, up_weight],
-                shape,
-                2,
-                cut,
-                fill,
-                lambda out, source, s: out.at[source, s],
-            )
-        ]
+        return [Line([gate_weight, up_weight], (count,) + both_shape, 2, cut, fill)]
+
+    def plane_mlp(both):
+        return [Plane(both, (count, sections) + both_shape, natural, lambda out, s: out.at[:, s])]
 
     def unpack_rec(wide, gates):
         return wide.reshape(model, 2 * window), gates.reshape(2, 2, block_width, block_width)
 
     reach = window - own_width
 
-    def out_window(strip):
+    def out_window(strip, l):
+        strip = jnp.concatenate([strip[0], out_weight[l], strip[1]], axis=0)
         return lax.dynamic_slice_in_dim(strip, reach - offset, window, 0)
 
     packed = jnp.concatenate(
@@ -1158,7 +1260,8 @@
     )
     gains_own = jnp.stack([rec_gain, mlp_gain], axis=1)
     flat = jnp.concatenate([packed.reshape(-1), gains_own.reshape(-1)]).reshape(16, -1)
-    x_all, flat, *got = comm("start", next(next_id), x=x0, jobs=[Everyone(flat, count)] + send_rec(0))
+    jobs = [Everyone(flat, count)] + spread_rec(0) + line_mlp(0)
+    x_all, flat, *rec_got, mlp_line = comm("start", next(next_id), x=x0, jobs=jobs)
     flat = flat.reshape(count, -1)
     small_all = flat[:, : packed.size].reshape(count, layers, 8, own_width)
     small_all = jnp.transpose(small_all, (1, 2, 0, 3)).reshape(layers, 8, lru_width)
@@ -1186,14 +1289,19 @@
     kept = []
     rec_weights, mlp_weights = [], []
     for l in range(layers):
-        wide_weight, gates = unpack_rec(*got)
+        wide_weight, gates = unpack_rec(*rec_got)
         rec_weights.append((wide_weight, gates))
         wide = dot(normed, wide_weight)
         gated, *saved = middle_forward(wide, marks, gates, small[l], rim[l], first_state[l])
         part = dot(gated, own_out[l]).astype(bf16)
         kept.append((x, normed, wide, gated, saved))
-        normed, x, *got = comm("forward", next(next_id), part, x, gain=gains[l, 1], jobs=send_mlp(l))
-        mlp_weights.append(got[0].reshape(model, 2 * hidden_part))
+        jobs = plane_mlp(mlp_line)
+        if l + 1 < layers:
+            jobs += line_rec(l + 1)
+        else:
+            jobs += [Beside(out_weight, m, reach) for m in range(layers)]
+        normed, x, both, *rec_line = comm("forward", next(next_id), part, x, gain=gains[l, 1], jobs=jobs)
+        mlp_weights.append(both.reshape(model, 2 * hidden_part))
         if l == 0:
             masked_all = lax.all_gather(lax.optimization_barrier((masked, x))[0], "seq", axis=0, tiled=True)
         both = dot(normed, mlp_weights[l])
@@ -1201,9 +1309,12 @@
         part = dot(hidden, down_weight[l]).astype(bf16)
         kept.append((x, normed, both, hidden))
         if l + 1 < layers:
-            normed, x, *got = comm("forward", next(next_id), part, x, gain=gains[l + 1, 0], jobs=send_rec(l + 1))
+            jobs = plane_rec(*rec_line) + line_mlp(l + 1)
+            normed, x, *rec_got, mlp_line = comm("forward", next(next_id), part, x, gain=gains[l + 1, 0], jobs=jobs)
         else:
             last_part, last_x = part, x
+
+    strips = rec_line
 
     mlp_lanes = np.gcd(256, hidden_part).item()
     rec_lanes = np.gcd(128, 2 * own_width).item()
@@ -1229,10 +1340,15 @@
         lanes = swapped.shape[3]
         return jnp.concatenate([swapped.reshape(sections, -1, lanes), shared], axis=1)
 
-    def scatter(whole, rows):
-        whole = whole.reshape(-1, whole.shape[-1])
-        mine = lax.psum_scatter(whole, "section", scatter_dimension=0, tiled=True)
-        return grad_jobs(mine, rows)
+    def scatter(whole):
+        return lax.psum_scatter(
+            whole.reshape(-1, whole.shape[-1]), "section", scatter_dimension=0, tiled=True
+        )
+
+    rows_of = {
+        "mlp": 2 * hidden_part // mlp_lanes * quarter,
+        "rec": (2 * own_width * quarter + 4 * block_width * block_quarter) // rec_lanes,
+    }
 
     def grad_jobs(mine, rows):
         def cut(refs, target):
@@ -1267,17 +1383,14 @@
             down = by_section(dot_rows(hidden, d_all), mlp_lanes)
             whole = bundle(by_target(dot_rows(normed, d_both), mlp_lanes), down)
         part, whole = lax.optimization_barrier((part, whole))
-        waiting["mlp", l] = scatter(whole, 2 * hidden_part // mlp_lanes * quarter)
-        jobs = waiting["mlp", l + 1] if l + 1 < layers else []
-        d_all, d_rows_own, dgains[l][1], strip, *got = comm(
-            "back", next(next_id), part, x, d_rows_own, gains[l, 1], [Beside(out_weight, l, reach)] + jobs
-        )
-        if jobs:
-            spread["mlp", l + 1] = got
+        waiting["mlp", l] = scatter(whole)
+        if l + 1 < layers:
+            part, waiting["rec", l + 1] = lax.optimization_barrier((part, waiting["rec", l + 1]))
+        d_all, d_rows_own, dgains[l][1] = comm("back", next(next_id), part, x, d_rows_own, gains[l, 1])
 
         x, normed, wide, gated, saved = kept[2 * l]
         wide_weight, gates = rec_weights[l]
-        d_gated = dot_t(d_all, out_window(strip))
+        d_gated = dot_t(d_all, out_window(strips[l], l))
         dib, d_rate, d_inflow, sums = middle_backward(
             d_gated, wide, saved, marks, gates, small[l], rim[l], own
         )
@@ -1306,20 +1419,16 @@
             whole = bundle(swapped, by_section(grad_out, rec_lanes))
         sums_own[l] = lax.dynamic_slice_in_dim(sums, offset, own_width, 1)
         part, whole = lax.optimization_barrier((part, whole))
-        waiting["rec", l] = scatter(whole, (2 * own_width * quarter + 4 * block_width * block_quarter) // rec_lanes)
-        jobs = waiting["rec", l + 1] if l + 1 < layers else []
+        waiting["rec", l] = scatter(whole)
+        part, waiting["mlp", l] = lax.optimization_barrier((part, waiting["mlp", l]))
         if l > 0:
-            d_all, d_rows_own, dgains[l][0], *got = comm(
-                "back", next(next_id), part, x, d_rows_own, gains[l, 0], jobs
-            )
-        else:
-            input_grad, dgains[l][0], *got = comm("last", next(next_id), part, x, d_rows_own, gains[l, 0], jobs)
-        if jobs:
-            spread["rec", l + 1] = got
-
-    last_part, last_x, _ = lax.optimization_barrier((last_part, last_x, input_grad))
-    outputs, *got = comm("rows", next(next_id), last_part, last_x, jobs=waiting["mlp", 0])
-    spread["mlp", 0] = got
+            d_all, d_rows_own, dgains[l][0] = comm("back", next(next_id), part, x, d_rows_own, gains[l, 0])
+            continue
+        names = [(kind, m) for m in range(1, layers) for kind in ("mlp", "rec")]
+        jobs = [job for name in names for job in grad_jobs(waiting[name], rows_of[name[0]])]
+        input_grad, dgains[l][0], *got = comm("last", next(next_id), part, x, d_rows_own, gains[l, 0], jobs)
+        for i, name in enumerate(names):
+            spread[name] = got[2 * i : 2 * i + 2]
 
     sums_lanes = -(-own_width // 256) * 256
     sums = jnp.pad(jnp.concatenate(sums_own, axis=0), ((0, 0), (0, sums_lanes - own_width)))
@@ -1327,9 +1436,12 @@
     dgain_all = jnp.concatenate([a for pair in dgains for a in pair], axis=0).reshape(2 * layers, count, d_rows)
     dgain_all = jnp.pad(jnp.transpose(dgain_all, (1, 0, 2)), ((0, 0), (0, 8 - 2 * layers), (0, 256 - d_rows)))
     tiny = jnp.concatenate([dgain_all.reshape(-1, 256), sums], axis=0)
-    tiny, _ = lax.optimization_barrier((tiny, outputs))
-    *got, dgain_all, sums = comm("none", next(next_id), jobs=waiting["rec", 0] + grad_jobs(tiny, 8))
-    spread["rec", 0] = got
+    last_part, last_x, _ = lax.optimization_barrier((last_part, last_x, input_grad))
+    jobs = [job for kind in ("mlp", "rec") for job in grad_jobs(waiting[kind, 0], rows_of[kind])]
+    outputs, *got, dgain_all, sums = comm(
+        "rows", next(next_id), last_part, last_x, jobs=jobs + grad_jobs(tiny, 8)
+    )
+    spread["mlp", 0], spread["rec", 0] = got[:2], got[2:]
     sums = jnp.sum(sums, axis=0).reshape(layers, 8, sums_lanes)[:, :, :own_width]
     dgain_all = jnp.sum(dgain_all, axis=(0, 1))[: 2 * layers, :d_rows].reshape(layers, 2, d_rows)
 

time: 1260 us -> 1140 us (0.905)
  Pallas kernels: 1090 us -> 963 us
    pallas_call x10 -> x9, Pallas kernels: 970 us -> 839 us  [comm(): pl.pallas_call(lambda *refs: comm_body(mode, count, jobs, refs), out_shap...]
  transfers between devices with their start and end apart: 5 -> 5, of which waited for: 0 -> 1; matrix products, arithmetic and copies ran while one was open for 6% -> 7% of each run, Pallas kernels for 66% -> 51%
where the time goes in v3:
time: 1140 us; the launch traced here: 1130 us
  Pallas kernels  963 us (84%)
  matrix products  87.1 us (8%)
  local copies, waits for them, and re-layouts  37.5 us (3%)
  other arithmetic  17.7 us (2%)
  between operations  15.6 us (1%)
    pallas_call x9, Pallas kernels, comm(): pl.pallas_call(lambda *refs: comm_body(mode, count, jobs, refs), out_shap...  839 us
    dot_general x8, matrix products, dot_t(): lax.dot_general(a, b, (((1,), (1,)), ((), ())), preferred_element_type=f32)  45.5 us
    dot_general x8, matrix products, dot(): return jnp.dot(a, b, preferred_element_type=f32)  41.7 us
    pallas_call x2, Pallas kernels, grads_mlp(): pl.pallas_call(body, grid=(count + down_blocks,), out_shape=jax.ShapeDtyp...  27.2 us
    pallas_call x2, Pallas kernels, grads_rec(): pl.pallas_call(body, grid_spec=pltpu.PrefetchScalarGridSpec(num_scalar_pr...  27.1 us
    pallas_call x2, Pallas kernels, middle_backward(): pl.pallas_call(partial(middle_backward_body, rows, width), grid=(steps,),...  23.6 us
  transfers between devices with their start and end apart: 5, of which 1 were waited for; matrix products, arithmetic and copies ran while one was open for 7% of the time, Pallas kernels for 51%

profile of v3, /device:TPU:18, one launch (start us, length us, event | category | flops | bytes accessed | tf_op | source)
XLA Modules:
  0.0 1125.6 jit_solution(18421361825031359135)
XLA Ops:
  14.9 104.1 %shard_map.341 = (bf16[8,64,2048]{2,1,0:T(8,128)(2,1)}, bf16[8,16,384]{2,1,0:T(8,128)(2,1)}, bf16[8,4,64,1024]{3,2,1,0:T(8,128)(2,1)}, bf16[4,8,32,256]{3,2,1,0:T(8,128)(2,1)}, bf16[8,64,1536]{2,1,0:T(8,128)(2,1)}) custom-call(bf16[64,2048]{1,0:T(8,128)(2,1)} %dynamic-slice_bitcast_fusion.refs_0_.refs_1_, bf16[16,384]{1,0:T(8,128)(2,1)} %reshape.300.refs_1_, ...), custom_call_target="tpu_custom_call" | custom-call | flops 49999998976 | bytes 1000000 | tf_op jit(solution)/shard_map/pallas_call | solution.py:581
  138.0 7.1 shard_map.342
  151.2 73.7 %shard_map.343 = (bf16[8,64,2048]{2,1,0:T(8,128)(2,1)}, bf16[64,2048]{1,0:T(8,128)(2,1)}, bf16[8,4,64,1536]{3,2,1,0:T(8,128)(2,1)}, bf16[8,64,1024]{2,1,0:T(8,128)(2,1)}, bf16[8,32,256]{2,1,0:T(8,128)(2,1)}) custom-call(bf16[8,64,2048]{2,1,0:T(8,128)(2,1)} %bitcast.405, bf16[64,2048]{1,0:T(8,128)(2,1)} %dynamic-slice_bitcast_fusion.refs_0_.refs_1_, ...), custom_call_target="tpu_custom_call" | custom-call | flops 49999998976 | bytes 1000000 | tf_op jit(solution)/shard_map/pallas_call | solution.py:581
  240.1 98.5 %shard_map.344 = (bf16[8,64,2048]{2,1,0:T(8,128)(2,1)}, bf16[64,2048]{1,0:T(8,128)(2,1)}, bf16[8,4,64,1024]{3,2,1,0:T(8,128)(2,1)}, bf16[4,8,32,256]{3,2,1,0:T(8,128)(2,1)}, bf16[8,64,1536]{2,1,0:T(8,128)(2,1)}) custom-call(bf16[8,64,2048]{2,1,0:T(8,128)(2,1)} %bitcast.406, bf16[64,2048]{1,0:T(8,128)(2,1)} %get-tuple-element.109.refs_1_, ...), custom_call_target="tpu_custom_call" | custom-call | flops 49999998976 | bytes 1000000 | tf_op jit(solution)/shard_map/pallas_call | solution.py:581
  338.7 6.5 fusion.83.is_ref
  345.7 7.1 shard_map.345
  357.1 70.8 %shard_map.346 = (bf16[8,64,2048]{2,1,0:T(8,128)(2,1)}, bf16[64,2048]{1,0:T(8,128)(2,1)}, bf16[8,4,64,1536]{3,2,1,0:T(8,128)(2,1)}, bf16[2,192,2048]{2,1,0:T(8,128)(2,1)}, bf16[2,192,2048]{2,1,0:T(8,128)(2,1)}) custom-call(bf16[8,64,2048]{2,1,0:T(8,128)(2,1)} %bitcast.407, bf16[64,2048]{1,0:T(8,128)(2,1)} %get-tuple-element.116.refs_1_, ...), custom_call_target="tpu_custom_call" | custom-call | flops 49999998976 | bytes 1000000 | tf_op jit(solution)/shard_map/pallas_call | solution.py:581
  428.0 6.6 fusion.84
  434.6 6.8 fusion.52
  447.3 13.5 %shard_map.347 = bf16[4,12,384,256]{3,2,1,0:T(8,128)(2,1)} custom-call(bf16[512,2048]{1,0:T(8,128)(2,1)} %bitcast.328, bf16[512,1536]{1,0:T(8,128)(2,1)} %pad_maximum_fusion.both_ref, bf16[512,768]{1,0:T(8,128)(2,1)} %get-tuple-element.209.hidden_ref, bf16[512,2048]{1,0:T(8,128)(2,1)} %all-gather.2.cloned.1.call-done.all_ref), custom_call_target="tpu_custom_call" | custom-call | tf_op jit(solution)/shard_map/pallas_call | solution.py:901
  465.1 55.9 %shard_map.348 = (bf16[8,64,2048]{2,1,0:T(8,128)(2,1)}, bf16[64,2048]{1,0:T(8,128)(2,1)}, f32[1,2048]{1,0:T(1,128)}) custom-call(bf16[8,64,2048]{2,1,0:T(8,128)(2,1)} %bitcast.401, bf16[64,2048]{1,0:T(8,128)(2,1)} %get-tuple-element.160.refs_1_, bf16[64,2048]{1,0:T(8,128)(2,1)} %fusion.60.refs_2_, f32[1,2048]{1,0:T(1,128)} %get-tuple-element.227.refs_2_.refs_3_), custom_call_target="tpu_custom_call" | custom-call | flops 49999998976 | bytes 1000000 | tf_op jit(solution)/shard_map/pallas_call | solution.py:581
  526.4 11.9 %shard_map.349 = (bf16[512,1024]{1,0:T(8,128)(2,1)}, bf16[512,512]{1,0:T(8,128)(2,1)}, bf16[512,512]{1,0:T(8,128)(2,1)}, f32[8,512]{1,0:T(8,128)}) custom-call(f32[512,512]{1,0:T(8,128)} %fusion.26.dg_ref, f32[512,1024]{1,0:T(8,128)} %fusion.83.is_ref, f32[512,512]{1,0:T(8,128)} %get-tuple-element.125.mixed_ref, f32[512,512]{1,0:T(8,128)} %get-tuple-element.126.rate_ref, ...), custom_call_target="tpu_custom_call" | custom-call | tf_op jit(solution)/shard_map/pallas_call | solution.py:849
  538.4 13.5 %shard_map.350 = bf16[4,12,384,128]{3,2,1,0:T(8,128)(2,1)} custom-call(s32[1]{0:T(128)} %bitcast.55.offset_ref, bf16[512,2048]{1,0:T(8,128)(2,1)} %bitcast.322, bf16[512,1024]{1,0:T(8,128)(2,1)} %get-tuple-element.130.dib_ref, bf16[512,512]{1,0:T(8,128)(2,1)} %get-tuple-element.115.gated_ref, bf16[512,2048]{1,0:T(8,128)(2,1)} %bitcast.326, ...), custom_call_target="tpu_custom_call" | custom-call | tf_op jit(solution)/shard_map/pallas_call | solution.py:975
  562.3 53.4 %shard_map.351 = (bf16[8,64,2048]{2,1,0:T(8,128)(2,1)}, bf16[64,2048]{1,0:T(8,128)(2,1)}, f32[1,2048]{1,0:T(1,128)}) custom-call(bf16[8,64,2048]{2,1,0:T(8,128)(2,1)} %bitcast.404, bf16[64,2048]{1,0:T(8,128)(2,1)} %get-tuple-element.116.refs_1_, bf16[64,2048]{1,0:T(8,128)(2,1)} %get-tuple-element.136.refs_2_, f32[1,2048]{1,0:T(1,128)} %get-tuple-element.228.refs_2_.refs_3_), custom_call_target="tpu_custom_call" | custom-call | flops 49999998976 | bytes 1000000 | tf_op jit(solution)/shard_map/pallas_call | solution.py:581
  623.2 13.7 %shard_map.352 = bf16[4,12,384,256]{3,2,1,0:T(8,128)(2,1)} custom-call(bf16[512,2048]{1,0:T(8,128)(2,1)} %bitcast.320, bf16[512,1536]{1,0:T(8,128)(2,1)} %pad_maximum_fusion.1.both_ref, bf16[512,768]{1,0:T(8,128)(2,1)} %copy-done.6, bf16[512,2048]{1,0:T(8,128)(2,1)} %bitcast.330), custom_call_target="tpu_custom_call" | custom-call | tf_op jit(solution)/shard_map/pallas_call | solution.py:901
  636.9 7.4 convolution_convert_fusion.2
  649.3 53.6 %shard_map.353 = (bf16[8,64,2048]{2,1,0:T(8,128)(2,1)}, bf16[64,2048]{1,0:T(8,128)(2,1)}, f32[1,2048]{1,0:T(1,128)}) custom-call(bf16[8,64,2048]{2,1,0:T(8,128)(2,1)} %bitcast.403, bf16[64,2048]{1,0:T(8,128)(2,1)} %get-tuple-element.109.refs_1_, bf16[64,2048]{1,0:T(8,128)(2,1)} %get-tuple-element.141.refs_2_, f32[1,2048]{1,0:T(1,128)} %get-tuple-element.229.refs_2_.refs_3_), custom_call_target="tpu_custom_call" | custom-call | flops 49999998976 | bytes 1000000 | tf_op jit(solution)/shard_map/pallas_call | solution.py:581
  707.7 11.6 %shard_map.354 = (bf16[512,1024]{1,0:T(8,128)(2,1)}, bf16[512,512]{1,0:T(8,128)(2,1)}, bf16[512,512]{1,0:T(8,128)(2,1)}, f32[8,512]{1,0:T(8,128)}) custom-call(f32[512,512]{1,0:T(8,128)} %fusion.22.dg_ref, f32[512,1024]{1,0:T(8,128)} %fusion.81.is_ref, f32[512,512]{1,0:T(8,128)} %get-tuple-element.144.mixed_ref, f32[512,512]{1,0:T(8,128)} %get-tuple-element.145.rate_ref, ...), custom_call_target="tpu_custom_call" | custom-call | tf_op jit(solution)/shard_map/pallas_call | solution.py:849
  719.3 13.6 %shard_map.355 = bf16[4,12,384,128]{3,2,1,0:T(8,128)(2,1)} custom-call(s32[1]{0:T(128)} %bitcast.55.offset_ref, bf16[512,2048]{1,0:T(8,128)(2,1)} %fusion.1.normed_ref, bf16[512,1024]{1,0:T(8,128)(2,1)} %get-tuple-element.149.dib_ref, bf16[512,512]{1,0:T(8,128)(2,1)} %get-tuple-element.105.gated_ref, bf16[512,2048]{1,0:T(8,128)(2,1)} %bitcast.324, ...), custom_call_target="tpu_custom_call" | custom-call | tf_op jit(solution)/shard_map/pallas_call | solution.py:975
  745.2 173.2 %shard_map.356 = (bf16[64,2048]{1,0:T(8,128)(2,1)}, f32[1,2048]{1,0:T(1,128)}, bf16[8,4,384,256]{3,2,1,0:T(8,128)(2,1)}, bf16[4,1536,256]{2,1,0:T(8,128)(2,1)}, ...) custom-call(bf16[8,64,2048]{2,1,0:T(8,128)(2,1)} %bitcast.402, ...), custom_call_target="tpu_custom_call" | custom-call | flops 49999998976 | bytes 1000000 | tf_op jit(solution)/shard_map/pallas_call | solution.py:581
  919.9 155.4 %shard_map.357 = (bf16[64,2048]{1,0:T(8,128)(2,1)}, bf16[8,4,384,256]{3,2,1,0:T(8,128)(2,1)}, bf16[4,1536,256]{2,1,0:T(8,128)(2,1)}, bf16[8,4,384,128]{3,2,1,0:T...) custom-call(bf16[8,64,2048]{2,1,0:T(8,128)(2,1)} %bitcast.400, ...), custom_call_target="tpu_custom_call" | custom-call | flops 49999998976 | bytes 1000000 | tf_op jit(solution)/shard_map/pallas_call | solution.py:581
  1085.2 10.2 shard_map.358
  1095.4 14.0 %shard_map.359 = (f32[2,256,6144]{2,1,0:T(8,128)}, f32[2,256,6144]{2,1,0:T(8,128)}) custom-call(bf16[8,4,384,256]{3,2,1,0:T(8,128)(2,1)} %get-tuple-element.179.refs_0_, bf16[8,4,384,256]{3,2,1,0:T(8,128)(2,1)} %get-tuple-element.180.refs_1_), custom_call_target="tpu_custom_call" | custom-call | tf_op jit(solution)/shard_map/pallas_call | solution.py:1021
  1109.4 7.9 shard_map.360
  (207 shorter events, 120.0 us)
Async XLA Ops:
  7.2 427.4 %all-gather.2.cloned.1.call-start = ((), (), s32[]{:S(2)}) async-start(), calls=%async_computation.4 | async-start | bytes 2359296 | tf_op jit(solution)/shard_map/all_gather | solution.py:1306
  119.1 9.1 copy-start.2
  120.8 7.9 copy-start.20
  122.9 5.9 copy-start.22
  130.4 5.9 copy-start.4
  224.9 337.4 %reduce-scatter.5.cloned.1.call-start = ((), (), s32[]{:S(2)}) async-start(), calls=%async_computation.5 | async-start | bytes 11796480 | tf_op jit(solution)/shard_map/reduce_scatter | solution.py:1344
  434.6 6.8 copy-start.30
  460.8 188.6 %reduce-scatter.7.cloned.1.call-start = ((), (), s32[]{:S(2)}) async-start(), calls=%async_computation.6 | async-start | bytes 5898240 | tf_op jit(solution)/shard_map/reduce_scatter | solution.py:1344
  465.1 55.9 %copy-start.10 = (bf16[320,2048]{1,0:T(8,128)(2,1)S(1)}, bf16[320,2048]{1,0:T(8,128)(2,1)}, u32[]{:S(2)}) copy-start(bf16[320,2048]{1,0:T(8,128)(2,1)} %get-tuple-element.211) | copy-start | bytes 3932164
  465.1 55.9 %copy-start.15 = (bf16[192,2048]{1,0:T(8,128)(2,1)S(1)}, bf16[192,2048]{1,0:T(8,128)(2,1)}, u32[]{:S(2)}) copy-start(bf16[192,2048]{1,0:T(8,128)(2,1)} %get-tuple-element.215) | copy-start | bytes 2359300
  538.4 13.5 %copy-start.12 = (bf16[512,1024]{1,0:T(8,128)(2,1)S(1)}, bf16[512,1024]{1,0:T(8,128)(2,1)}, u32[]{:S(2)}) copy-start(bf16[512,1024]{1,0:T(8,128)(2,1)} %get-tuple-element.130.dib_ref) | copy-start | bytes 3145732
  557.9 187.3 %reduce-scatter.9.cloned.1.call-start = ((), (), s32[]{:S(2)}) async-start(), calls=%async_computation.7 | async-start | bytes 11796480 | tf_op jit(solution)/shard_map/reduce_scatter | solution.py:1344
  562.3 53.4 %copy-start.8 = (f32[512,1536]{1,0:T(8,128)S(1)}, f32[512,1536]{1,0:T(8,128)}, u32[]{:S(2)}) copy-start(f32[512,1536]{1,0:T(8,128)} %copy-done.7) | copy-start | bytes 9437188
  623.2 13.7 %copy-start.17 = (bf16[512,768]{1,0:T(8,128)(2,1)S(1)}, bf16[512,768]{1,0:T(8,128)(2,1)}, u32[]{:S(2)}) copy-start(bf16[512,768]{1,0:T(8,128)(2,1)} %copy-done.16) | copy-start | bytes 2359300
  644.4 275.5 %reduce-scatter.11.cloned.1.call-start = ((), (), s32[]{:S(2)}) async-start(), calls=%async_computation.8 | async-start | bytes 5898240 | tf_op jit(solution)/shard_map/reduce_scatter | solution.py:1344
  649.3 53.6 %copy-start.9 = (bf16[320,2048]{1,0:T(8,128)(2,1)S(1)}, bf16[320,2048]{1,0:T(8,128)(2,1)}, u32[]{:S(2)}) copy-start(bf16[320,2048]{1,0:T(8,128)(2,1)} %get-tuple-element.210) | copy-start | bytes 3932164
  649.3 53.6 %copy-start.14 = (bf16[192,2048]{1,0:T(8,128)(2,1)S(1)}, bf16[192,2048]{1,0:T(8,128)(2,1)}, u32[]{:S(2)}) copy-start(bf16[192,2048]{1,0:T(8,128)(2,1)} %get-tuple-element.213) | copy-start | bytes 2359300
  719.3 13.6 %copy-start.11 = (bf16[512,1024]{1,0:T(8,128)(2,1)S(1)}, bf16[512,1024]{1,0:T(8,128)(2,1)}, u32[]{:S(2)}) copy-start(bf16[512,1024]{1,0:T(8,128)(2,1)} %get-tuple-element.149.dib_ref) | copy-start | bytes 3145732
  745.2 173.3 %copy-start.26 = (f32[1,2048]{1,0:T(1,128)S(1)}, f32[1,2048]{1,0:T(1,128)}, u32[]{:S(2)}) copy-start(f32[1,2048]{1,0:T(1,128)} %get-tuple-element.166) | copy-start | bytes 24580
  745.2 173.3 %copy-start.27 = (f32[1,2048]{1,0:T(1,128)S(1)}, f32[1,2048]{1,0:T(1,128)}, u32[]{:S(2)}) copy-start(f32[1,2048]{1,0:T(1,128)} %get-tuple-element.165) | copy-start | bytes 24580
  745.2 173.3 %copy-start.28 = (f32[1,2048]{1,0:T(1,128)S(1)}, f32[1,2048]{1,0:T(1,128)}, u32[]{:S(2)}) copy-start(f32[1,2048]{1,0:T(1,128)} %get-tuple-element.164) | copy-start | bytes 24580
  1109.4 7.9 copy-start.19
  1109.4 8.6 copy-start.18
  1109.4 9.3 copy-start.1
  (14 other events, 39.7 us)
Sparse Core Ops, SparseCore 0:
  225.0 52.3 all-gather.1
  460.9 101.3 reduce-scatter.4
  565.9 57.0 reduce-scatter.6
  644.5 97.2 reduce-scatter.8
  745.1 95.0 reduce-scatter.10

commit v4 on v3

--- a/solution.py
+++ b/solution.py
@@ -92,6 +92,7 @@
 
 
 class Spread:
+    queued = True
     on_line, in_plane = True, True
 
     def __init__(self, arrays, shape, pieces, cut, fill, slot):
@@ -120,32 +121,28 @@
                 )
             )
 
-        def push():
-            for k in range(1, count):
-                peer = (place + k) % count
-                pieces = zip(self.cut(refs, peer), self.fill(self.slot(out, place, section)))
-                group = [
+        for k in range(1, count):
+            peer = (place + k) % count
+            pieces = zip(self.cut(refs, peer), self.fill(self.slot(out, place, section)))
+            self.sends.append(
+                [
                     along(piece, there, line.at[0, i, k], line.at[1, i, k], peer)
                     for i, (piece, there) in enumerate(pieces)
                 ]
-                for copy in group:
-                    copy.start()
-                self.sends.append(group)
-
-        self.push = push
+            )
 
     def own_block(self):
         self.own.land()
         self.items[0].start()
+        return self.items[:1]
 
     def arrive(self, k):
         for copy in self.sends[k - 1]:
             copy.wait_recv()
         self.items[k].start()
-        self.items[k - 1].forward()
+        return self.items[k : k + 1]
 
     def finish(self):
-        self.items[-1].forward()
         self.own.finish()
         for item in self.items:
             item.finish()
@@ -155,6 +152,7 @@
 
 
 class Line:
+    queued = True
     on_line, in_plane = True, False
 
     def __init__(self, arrays, shape, pieces, cut, fill):
@@ -171,34 +169,34 @@
             self.cut(refs, place), self.fill(stage), stage, out.at[place], line.at[0, :, 0], line.at[1, 0, 0]
         )
 
-        def push():
-            for k in range(1, count):
-                peer = (place + k) % count
-                pieces = zip(self.cut(refs, peer), self.fill(out.at[place]))
-                group = [
+        for k in range(1, count):
+            peer = (place + k) % count
+            pieces = zip(self.cut(refs, peer), self.fill(out.at[place]))
+            self.sends.append(
+                [
                     along(piece, there, line.at[0, i, k], line.at[1, i, k], peer)
                     for i, (piece, there) in enumerate(pieces)
                 ]
-                for copy in group:
-                    copy.start()
-                self.sends.append(group)
-
-        self.push = push
+            )
 
     def own_block(self):
         self.own.land()
+        return []
 
     def arrive(self, k):
-        pass
+        for copy in self.sends[k - 1]:
+            copy.wait_recv()
+        return []
 
     def finish(self):
         self.own.finish()
         for group in self.sends:
             for copy in group:
-                copy.wait()
+                copy.wait_send()
 
 
 class Plane:
+    queued = False
     on_line, in_plane = False, True
 
     def __init__(self, array, shape, slot, column):
@@ -218,25 +216,22 @@
             item.start()
             self.items.append(item)
 
-    def push(self):
-        pass
-
     def own_block(self):
         self.own.land()
+        return []
 
     def arrive(self, k):
-        if k > 1:
-            self.items[k - 2].forward()
+        self.items[k - 1].forward()
 
     def finish(self):
-        for item in self.items[-2:]:
-            item.forward()
+        self.items[-1].forward()
         for item in self.items:
             item.finish()
         self.own.finish()
 
 
 class Share:
+    queued = False
     on_line, in_plane = False, True
 
     def __init__(self, array, start, size):
@@ -260,15 +255,12 @@
             item.start()
             self.items.append(item)
 
-    def push(self):
-        pass
-
     def own_block(self):
         self.own.land()
+        return self.items
 
     def arrive(self, k):
-        if k in (4, 6):
-            self.items[k // 2 - 2].forward()
+        return []
 
     def finish(self):
         self.own.finish()
@@ -277,6 +269,7 @@
 
 
 class Everyone:
+    queued = False
     on_line, in_plane = True, False
 
     def __init__(self, array, count):
@@ -295,21 +288,20 @@
             copy.start()
             self.sends.append(copy)
 
-    def push(self):
-        pass
-
     def own_block(self):
         self.own.wait()
+        return []
 
     def arrive(self, k):
-        self.sends[k - 1].wait_recv()
+        pass
 
     def finish(self):
         for copy in self.sends:
-            copy.wait_send()
+            copy.wait()
 
 
 class Beside:
+    queued = False
     on_line, in_plane = True, False
 
     def __init__(self, array, layer, reach):
@@ -346,11 +338,8 @@
             done += size
         self.place, self.count = place, count
 
-    def push(self):
-        pass
-
     def own_block(self):
-        pass
+        return []
 
     def arrive(self, k):
         pass
@@ -363,7 +352,7 @@
             pl.when(self.place >= k)(back.wait_send)
 
 
-def comm_body(mode, count, jobs, refs):
+def comm_body(mode, count, jobs, groups, window, refs):
     chips = count // 2
     has_sum = mode in ("forward", "back", "last", "rows")
     has_gather = mode in ("start", "forward", "back")
@@ -445,24 +434,40 @@
                 pl.when(goes_on(way))(hop(way, k).start)
                 across(way, k).start()
 
-    if mode == "start":
-        begin_gather(x_ref[...])
-    if has_sum:
-        pair_copies = []
-        for k in list(range(1, chips)) + [0]:
-            to_chip = (chip + k) % chips
-            copy = along(
-                part_ref.at[to_chip * 2 + 1 - core], pair_ref.at[k], pair_sem.at[0, k], pair_sem.at[1, k], mate
-            )
-            copy.start()
-            pair_copies.append((k, copy))
+    early = mode in ("start", "forward", "back")
     for job, ref, out, sems in zip(jobs, job_refs, job_outs, job_sems):
         job.begin(ref, out, sems, place, count)
-    for job in jobs:
-        job.push()
-    if has_sum:
-        sum_copies = []
+    queue = []
+    for group in groups:
+        members = [job for job in jobs[group[0] : group[1]] if job.queued]
+        queue += [(job, k) for k in range(1, count) for job in members]
+    issued, arrived, flowing, lag = [0], [0], [], 5
+
+    def issue(number):
+        for job, k in queue[issued[0] : issued[0] + number]:
+            for copy in job.sends[k - 1]:
+                copy.start()
+        issued[0] += number
+
+    def tick(k):
+        until = -(-len(queue) * k // (count - 1))
+        for job, index in queue[arrived[0] : until]:
+            flowing.extend(job.arrive(index))
+            issue(1)
+            if len(flowing) > lag:
+                flowing.pop(0).forward()
+        arrived[0] = max(arrived[0], until)
+        for job in jobs:
+            if not job.queued:
+                job.arrive(k)
+
+    def own_blocks():
+        for job in jobs:
+            flowing.extend(job.own_block())
+
+    def send_sums():
         total = None
+        copies = []
         for k, copy in pair_copies:
             to_chip = (chip + k) % chips
             copy.wait_recv()
@@ -475,14 +480,30 @@
                     staged_ref.at[k], landed_ref.at[k], sum_sem.at[0, k], sum_sem.at[1, k], to_chip * 2 + core
                 )
                 send.start()
-                sum_copies.append((k, send))
-    for job in jobs:
-        job.own_block()
-    for k in range(1, count):
-        for job in jobs:
-            job.arrive(k)
-        if mode == "start" and k % 2 == 0:
-            land(k // 2)
+                copies.append((k, send))
+        return total, copies
+
+    if has_sum:
+        pair_copies = []
+        for k in list(range(1, chips)) + [0]:
+            to_chip = (chip + k) % chips
+            copy = along(
+                part_ref.at[to_chip * 2 + 1 - core], pair_ref.at[k], pair_sem.at[0, k], pair_sem.at[1, k], mate
+            )
+            copy.start()
+            pair_copies.append((k, copy))
+    if mode == "start":
+        begin_gather(x_ref[...])
+    if not early or mode == "start":
+        issue(window)
+    if has_sum:
+        total, sum_copies = send_sums()
+    if early and mode != "start":
+        issue(window)
+    own_blocks()
+    if not early:
+        for k in range(1, count):
+            tick(k)
     if has_sum:
         for k, send in sum_copies:
             send.wait_recv()
@@ -507,11 +528,15 @@
         sent = (dy_ref[...].astype(f32) + back).astype(bf16)
         rows_ref[...] = sent
 
-    if has_gather and mode != "start":
-        begin_gather(sent)
-        for k in range(1, chips):
-            land(k)
-
+    if early:
+        if mode != "start":
+            begin_gather(sent)
+        for k in range(1, count):
+            tick(k)
+            if k % 2 == 0:
+                land(k // 2)
+    for item in flowing:
+        item.forward()
     for job in jobs:
         job.finish()
     if has_gather:
@@ -533,7 +558,7 @@
             send.wait_send()
 
 
-def comm(mode, collective_id, part=None, x=None, dy=None, gain=None, jobs=(), us=50):
+def comm(mode, collective_id, part=None, x=None, dy=None, gain=None, jobs=(), groups=None, window=4, us=50):
     count = lax.axis_size("seq")
     chips = count // 2
     has_sum = mode in ("forward", "back", "last", "rows")
@@ -579,7 +604,7 @@
     for job in jobs:
         scratch += job.scratch(count)
     outs = pl.pallas_call(
-        lambda *refs: comm_body(mode, count, jobs, refs),
+        lambda *refs: comm_body(mode, count, jobs, groups or [(0, len(jobs))], window, refs),
         out_shape=shapes,
         in_specs=in_specs,
         out_specs=out_specs,
@@ -641,6 +666,7 @@
     small_ref,
     rim_ref,
     first_ref,
+    pick_ref,
     gated_ref,
     mixed_ref,
     rate_ref,
@@ -697,7 +723,8 @@
         return jnp.broadcast_to(h[7:8], (8, width))
 
     carry[...] = lax.fori_loop(0, rows // 8, step, carry[...])
-    gated_ref[...] = (states_ref[...] * gelu_pair(is_ref[:, width:])[0]).astype(bf16)
+    gated = (states_ref[...] * gelu_pair(is_ref[:, width:])[0]).astype(bf16)
+    gated_ref[...] = dot(gated, pick_ref[...]).astype(bf16)
 
 
 def middle_backward_body(
@@ -817,19 +844,19 @@
     return pl.BlockSpec(shape, lambda i: (0,) * len(shape))
 
 
-def middle_forward(wide, marks, blocks, small, rim, first):
+def middle_forward(wide, marks, blocks, small, rim, first, pick):
     tokens, width = wide.shape[0], wide.shape[1] // 2
     rows = min(256, tokens)
     steps = tokens // rows
     here = partial(row_spec, rows, steps=steps, reverse=False)
-    whole = [blocks, small, rim, first]
-    kinds = [bf16, f32, f32, f32, f32, f32]
+    whole = [blocks, small, rim, first, pick]
+    own_width = pick.shape[1]
     return pl.pallas_call(
         partial(middle_forward_body, rows, width),
         grid=(steps,),
-        out_shape=[jax.ShapeDtypeStruct((tokens, width), kind) for kind in kinds],
+        out_shape=[jax.ShapeDtypeStruct((tokens, own_width), bf16)] + [jax.ShapeDtypeStruct((tokens, width), f32)] * 5,
         in_specs=[here(2 * width), here(8)] + [whole_spec(a.shape) for a in whole],
-        out_specs=[here(width)] * 6,
+        out_specs=[here(own_width)] + [here(width)] * 5,
         scratch_shapes=[
             pltpu.VMEM((rows + 8, width), f32),
             pltpu.VMEM((rows, width), f32),
@@ -913,9 +940,9 @@
     )(normed, d_both, hidden, d_all)
 
 
-def grads_rec(normed, dib, gated, d_all, mixed, d_rate, d_inflow, offset, own_width, sections, count, lanes):
+def grads_rec(normed, dib, gated, d_all, mixed, d_rate, d_inflow, pick, own_width, sections, count, lanes):
     tokens, model = normed.shape
-    window = gated.shape[1]
+    window = mixed.shape[1]
     block = window // 2
     d_rows = model // count
     quarter = d_rows // sections
@@ -928,15 +955,12 @@
     per_block = rows // padded
     out_blocks = model // lanes // per_block
 
-    def body(offset_ref, normed_ref, dib_ref, gated_ref, all_ref, mixed_ref, rate_ref, inflow_ref, out_ref, own, gates, out_grad):
+    def body(normed_ref, dib_ref, gated_ref, all_ref, mixed_ref, rate_ref, inflow_ref, pick_ref, out_ref, own, gates):
         j = pl.program_id(0)
-        first = offset_ref[0]
 
         @pl.when(j == 0)
         def _():
-            row = lax.broadcasted_iota(jnp.int32, (window, own_width), 0)
-            column = lax.broadcasted_iota(jnp.int32, (window, own_width), 1)
-            pick = (row == column + first).astype(f32).astype(bf16)
+            pick = pick_ref[...]
             own[...] = jnp.concatenate(
                 [dot(dib_ref[:, :window], pick), dot(dib_ref[:, window:], pick)], axis=1
             ).astype(bf16)
@@ -962,40 +986,35 @@
 
         @pl.when(j >= count)
         def _():
-            out_grad[...] = dot_rows(gated_ref[...], all_ref[...])
+            grad = dot_rows(gated_ref[...], all_ref[...])
             for s in range(sections):
-                here = pl.ds(pl.multiple_of(first + s * out_rows, 8), out_rows)
                 for ch in range(per_block):
-                    out_ref[s, 0, ch * padded : ch * padded + out_rows] = out_grad[
-                        here, ch * lanes : (ch + 1) * lanes
+                    out_ref[s, 0, ch * padded : ch * padded + out_rows] = grad[
+                        s * out_rows : (s + 1) * out_rows, ch * lanes : (ch + 1) * lanes
                     ].astype(bf16)
                     out_ref[s, 0, ch * padded + out_rows : (ch + 1) * padded] = jnp.zeros((16, lanes), bf16)
 
-    whole = lambda a: pl.BlockSpec(a.shape, lambda j, o, n=a.ndim: (0,) * n)
+    def whole(a):
+        return pl.BlockSpec(a.shape, lambda j: (0,) * a.ndim)
+
     return pl.pallas_call(
         body,
-        grid_spec=pltpu.PrefetchScalarGridSpec(
-            num_scalar_prefetch=1,
-            grid=(count + out_blocks,),
-            in_specs=[
-                pl.BlockSpec((tokens, d_rows), lambda j, o: (0, jnp.minimum(j, count - 1))),
-                whole(dib),
-                whole(gated),
-                pl.BlockSpec((tokens, per_block * lanes), lambda j, o: (0, jnp.maximum(j - count, 0))),
-                whole(mixed),
-                whole(d_rate),
-                whole(d_inflow),
-            ],
-            out_specs=pl.BlockSpec((sections, 1, rows, lanes), lambda j, o: (0, j, 0, 0)),
-            scratch_shapes=[
-                pltpu.VMEM((tokens, 2 * own_width), bf16),
-                pltpu.VMEM((4, block, block), f32),
-                pltpu.VMEM((window, per_block * lanes), f32),
-            ],
-        ),
+        grid=(count + out_blocks,),
+        in_specs=[
+            pl.BlockSpec((tokens, d_rows), lambda j: (0, jnp.minimum(j, count - 1))),
+            whole(dib),
+            whole(gated),
+            pl.BlockSpec((tokens, per_block * lanes), lambda j: (0, jnp.maximum(j - count, 0))),
+            whole(mixed),
+            whole(d_rate),
+            whole(d_inflow),
+            whole(pick),
+        ],
+        out_specs=pl.BlockSpec((sections, 1, rows, lanes), lambda j: (0, j, 0, 0)),
+        scratch_shapes=[pltpu.VMEM((tokens, 2 * own_width), bf16), pltpu.VMEM((4, block, block), f32)],
         out_shape=jax.ShapeDtypeStruct((sections, count + out_blocks, rows, lanes), bf16),
         compiler_params=pltpu.CompilerParams(vmem_limit_bytes=VMEM_LIMIT),
-    )(offset.reshape(1), normed, dib, gated, d_all, mixed, d_rate, d_inflow)
+    )(normed, dib, gated, d_all, mixed, d_rate, d_inflow, pick)
 
 
 def place_mlp(swapped, shared, quarter, hidden_part):
@@ -1045,7 +1064,7 @@
     return gate, up, down
 
 
-def place_rec(swapped, shared, quarter, own_width):
+def place_rec(swapped, shared, quarter, own_width, block_width, first_block, owner):
     layers = len(swapped)
     count, sections, _, lanes = swapped[0].shape
     chunks = 2 * own_width // lanes
@@ -1053,8 +1072,11 @@
     padded = out_rows + 16
     model = shared[0].shape[1] // padded * lanes
 
+    gate_rows = block_width // count // sections
+    gate_chunks = block_width // lanes
+
     def body(*refs):
-        in_ref, side_ref, out_ref = refs[2 * layers :]
+        in_ref, side_ref, out_ref, gate_ref = refs[2 * layers :]
         for l in range(layers):
 
             @pl.when(pl.program_id(0) == l)
@@ -1074,6 +1096,15 @@
                                 side_ref[0, rows, base + begin - own_width : base + last - own_width] = value[
                                     :, begin - first :
                                 ]
+                for b, q in enumerate(owner):
+                    for s in range(sections):
+                        value = refs[l][q, s, chunks * quarter :].astype(f32)
+                        for g in range(2):
+                            for ch in range(gate_chunks):
+                                at = ((2 * g + b - first_block[q]) * gate_chunks + ch) * gate_rows
+                                gate_ref[
+                                    g, 0, b, s * gate_rows : (s + 1) * gate_rows, ch * lanes : (ch + 1) * lanes
+                                ] = value[at : at + gate_rows]
                 for s in range(sections):
                     for ch in range(model // lanes):
                         out_ref[0, s * out_rows : (s + 1) * out_rows, ch * lanes : (ch + 1) * lanes] = refs[
@@ -1085,12 +1116,18 @@
     return pl.pallas_call(
         body,
         grid=(layers,),
-        out_shape=[wide, wide, jax.ShapeDtypeStruct((layers, own_width, model), f32)],
+        out_shape=[
+            wide,
+            wide,
+            jax.ShapeDtypeStruct((layers, own_width, model), f32),
+            jax.ShapeDtypeStruct((2, layers, len(owner), gate_rows * sections, block_width), f32),
+        ],
         in_specs=[pl.BlockSpec(a.shape, lambda l, n=a.ndim: (0,) * n) for a in arrays],
         out_specs=[
             pl.BlockSpec((1, sections * quarter, count * own_width), lambda l: (l, 0, 0)),
             pl.BlockSpec((1, sections * quarter, count * own_width), lambda l: (l, 0, 0)),
             pl.BlockSpec((1, own_width, model), lambda l: (l, 0, 0)),
+            pl.BlockSpec((2, 1, len(owner), gate_rows * sections, block_width), lambda l: (0, l, 0, 0, 0)),
         ],
         compiler_params=pltpu.CompilerParams(vmem_limit_bytes=VMEM_LIMIT),
     )(*arrays)
@@ -1261,7 +1298,7 @@
     gains_own = jnp.stack([rec_gain, mlp_gain], axis=1)
     flat = jnp.concatenate([packed.reshape(-1), gains_own.reshape(-1)]).reshape(16, -1)
     jobs = [Everyone(flat, count)] + spread_rec(0) + line_mlp(0)
-    x_all, flat, *rec_got, mlp_line = comm("start", next(next_id), x=x0, jobs=jobs)
+    x_all, flat, *rec_got, mlp_line = comm("start", next(next_id), x=x0, jobs=jobs, groups=[(0, 3), (3, 4)])
     flat = flat.reshape(count, -1)
     small_all = flat[:, : packed.size].reshape(count, layers, 8, own_width)
     small_all = jnp.transpose(small_all, (1, 2, 0, 3)).reshape(layers, 8, lru_width)
@@ -1281,9 +1318,7 @@
     channel = jnp.arange(window, dtype=jnp.int32)
     own = jnp.logical_and(channel >= offset, channel < offset + own_width).astype(f32)
     own = jnp.broadcast_to(own[None], (8, window))
-    own_out = [
-        lax.dynamic_update_slice(jnp.zeros((window, model), bf16), out_weight[l], (offset, 0)) for l in range(layers)
-    ]
+    pick = (channel[:, None] == jnp.arange(own_width, dtype=jnp.int32)[None] + offset).astype(bf16)
 
     x = x0
     kept = []
@@ -1292,8 +1327,8 @@
         wide_weight, gates = unpack_rec(*rec_got)
         rec_weights.append((wide_weight, gates))
         wide = dot(normed, wide_weight)
-        gated, *saved = middle_forward(wide, marks, gates, small[l], rim[l], first_state[l])
-        part = dot(gated, own_out[l]).astype(bf16)
+        gated, *saved = middle_forward(wide, marks, gates, small[l], rim[l], first_state[l], pick)
+        part = dot(gated, out_weight[l]).astype(bf16)
         kept.append((x, normed, wide, gated, saved))
         jobs = plane_mlp(mlp_line)
         if l + 1 < layers:
@@ -1302,8 +1337,6 @@
             jobs += [Beside(out_weight, m, reach) for m in range(layers)]
         normed, x, both, *rec_line = comm("forward", next(next_id), part, x, gain=gains[l, 1], jobs=jobs)
         mlp_weights.append(both.reshape(model, 2 * hidden_part))
-        if l == 0:
-            masked_all = lax.all_gather(lax.optimization_barrier((masked, x))[0], "seq", axis=0, tiled=True)
         both = dot(normed, mlp_weights[l])
         hidden = (jax.nn.gelu(both[:, :hidden_part]) * both[:, hidden_part:]).astype(bf16)
         part = dot(hidden, down_weight[l]).astype(bf16)
@@ -1311,6 +1344,9 @@
         if l + 1 < layers:
             jobs = plane_rec(*rec_line) + line_mlp(l + 1)
             normed, x, *rec_got, mlp_line = comm("forward", next(next_id), part, x, gain=gains[l + 1, 0], jobs=jobs)
+            if l + 2 == layers:
+                tied, normed = lax.optimization_barrier((masked, normed))
+                masked_all = lax.all_gather(tied, "seq", axis=0, tiled=True)
         else:
             last_part, last_x = part, x
 
@@ -1397,10 +1433,10 @@
         part = dot_t(dib, wide_weight).astype(bf16)
         if direct:
             whole = grads_rec(
-                normed, dib, gated, d_all, saved[0], d_rate, d_inflow, offset, own_width, sections, count, rec_lanes
+                normed, dib, gated, d_all, saved[0], d_rate, d_inflow, pick, own_width, sections, count, rec_lanes
             )
         else:
-            grad_out = lax.dynamic_slice_in_dim(dot_rows(gated, d_all), offset, own_width, 0)
+            grad_out = dot_rows(gated, d_all)
             grad_wide = dot_rows(normed, dib)
             swapped = by_target(
                 jnp.concatenate(
@@ -1426,7 +1462,8 @@
             continue
         names = [(kind, m) for m in range(1, layers) for kind in ("mlp", "rec")]
         jobs = [job for name in names for job in grad_jobs(waiting[name], rows_of[name[0]])]
-        input_grad, dgains[l][0], *got = comm("last", next(next_id), part, x, d_rows_own, gains[l, 0], jobs)
+        groups = [(2 * i, 2 * i + 2) for i in range(len(names))]
+        input_grad, dgains[l][0], *got = comm("last", next(next_id), part, x, d_rows_own, gains[l, 0], jobs, groups)
         for i, name in enumerate(names):
             spread[name] = got[2 * i : 2 * i + 2]
 
@@ -1439,7 +1476,7 @@
     last_part, last_x, _ = lax.optimization_barrier((last_part, last_x, input_grad))
     jobs = [job for kind in ("mlp", "rec") for job in grad_jobs(waiting[kind, 0], rows_of[kind])]
     outputs, *got, dgain_all, sums = comm(
-        "rows", next(next_id), last_part, last_x, jobs=jobs + grad_jobs(tiny, 8)
+        "rows", next(next_id), last_part, last_x, jobs=jobs + grad_jobs(tiny, 8), groups=[(0, 2), (2, 4), (4, 6)]
     )
     spread["mlp", 0], spread["rec", 0] = got[:2], got[2:]
     sums = jnp.sum(sums, axis=0).reshape(layers, 8, sums_lanes)[:, :, :own_width]
@@ -1468,7 +1505,9 @@
     rec_swapped, rec_shared = both_layers("rec")
     if direct:
         gate_grad, up_grad, down_grad = place_mlp(mlp_swapped, mlp_shared, quarter, hidden_part)
-        in_grad, side_grad, out_grad = place_rec(rec_swapped, rec_shared, quarter, own_width)
+        in_grad, side_grad, out_grad, gate_out = place_rec(
+            rec_swapped, rec_shared, quarter, own_width, block_width, first_block, owner
+        )
     else:
         gate_grad = columns(mlp_swapped, 0, hidden_part, mlp_lanes)
         up_grad = columns(mlp_swapped, hidden_part, 2 * hidden_part, mlp_lanes)
@@ -1477,14 +1516,14 @@
         side_grad = columns(rec_swapped, own_width, 2 * own_width, rec_lanes)
         out_grad = rows(rec_shared, own_width // sections, rec_lanes)
 
-    gate_out = []
-    for l in range(layers):
-        got = rec_swapped[l][:, :, 2 * own_width // rec_lanes * quarter :]
-        got = got.reshape(count, sections, 2, 2, block_width // rec_lanes, block_quarter, rec_lanes)
-        blocks = jnp.stack([got[owner[b], :, :, b - first_block[owner[b]]] for b in range(block_count)])
-        blocks = jnp.transpose(blocks, (2, 0, 1, 4, 3, 5))
-        gate_out.append(blocks.reshape(2, block_count, block_rows, block_width))
-    gate_out = jnp.stack(gate_out).astype(f32)
+        gate_out = []
+        for l in range(layers):
+            got = rec_swapped[l][:, :, 2 * own_width // rec_lanes * quarter :]
+            got = got.reshape(count, sections, 2, 2, block_width // rec_lanes, block_quarter, rec_lanes)
+            blocks = jnp.stack([got[owner[b], :, :, b - first_block[owner[b]]] for b in range(block_count)])
+            blocks = jnp.transpose(blocks, (2, 0, 1, 4, 3, 5))
+            gate_out.append(blocks.reshape(2, block_count, block_rows, block_width))
+        gate_out = jnp.stack(gate_out, axis=1).astype(f32)
 
     return (
         outputs[None],
@@ -1493,8 +1532,8 @@
         in_grad,
         side_grad,
         out_grad,
-        gate_out[:, 0],
-        gate_out[:, 1],
+        gate_out[0],
+        gate_out[1],
         sums[:, 0],
         sums[:, 1],
         sums[:, 2:6],

time: 1140 us -> 1070 us (0.939)
  Pallas kernels: 963 us -> 903 us
    pallas_call x11, Pallas kernels: 866 us -> 805 us  [the longest x9 778 us: comm(): pl.pallas_call(lambda *refs: comm_body(mode, count, jobs, groups or [(0,...]
  transfers between devices with their start and end apart: 5 -> 5, of which waited for: 1 -> 1; matrix products, arithmetic and copies ran while one was open for 7% -> 6% of each run, Pallas kernels for 51% -> 44%
where the time goes in v4:
time: 1070 us; the launch traced here: 1060 us
  Pallas kernels  903 us (84%)
  matrix products  85.1 us (8%)
  local copies, waits for them, and re-layouts  31.9 us (3%)
  other arithmetic  18.7 us (2%)
  between operations  15.6 us (1%)
    pallas_call x9, Pallas kernels, comm(): pl.pallas_call(lambda *refs: comm_body(mode, count, jobs, groups or [(0,...  778 us
    dot_general x8, matrix products, dot_t(): lax.dot_general(a, b, (((1,), (1,)), ((), ())), preferred_element_type=f32)  45.4 us
    dot_general x8, matrix products, dot(): return jnp.dot(a, b, preferred_element_type=f32)  39.7 us
    pallas_call x2, Pallas kernels, grads_mlp(): pl.pallas_call(body, grid=(count + down_blocks,), out_shape=jax.ShapeDtyp...  27 us
    pallas_call x2, Pallas kernels, grads_rec(): pl.pallas_call(body, grid=(count + out_blocks,), in_specs=[pl.BlockSpec((...  26.8 us
    pallas_call x2, Pallas kernels, middle_backward(): pl.pallas_call(partial(middle_backward_body, rows, width), grid=(steps,),...  23.4 us
  transfers between devices with their start and end apart: 5, of which 1 were waited for; matrix products, arithmetic and copies ran while one was open for 6% of the time, Pallas kernels for 44%

profile of v4, /device:TPU:18, one launch (start us, length us, event | category | flops | bytes accessed | tf_op | source)
XLA Modules:
  0.0 1059.9 jit_solution(5156224619364233120)
XLA Ops:
  14.9 79.6 %shard_map.341 = (bf16[8,64,2048]{2,1,0:T(8,128)(2,1)}, bf16[8,16,384]{2,1,0:T(8,128)(2,1)}, bf16[8,4,64,1024]{3,2,1,0:T(8,128)(2,1)}, bf16[4,8,32,256]{3,2,1,0:T(8,128)(2,1)}, bf16[8,64,1536]{2,1,0:T(8,128)(2,1)}) custom-call(bf16[64,2048]{1,0:T(8,128)(2,1)} %dynamic-slice_bitcast_fusion.refs_0_.refs_1_, bf16[16,384]{1,0:T(8,128)(2,1)} %reshape.295.refs_1_, ...), custom_call_target="tpu_custom_call" | custom-call | flops 49999998976 | bytes 1000000 | tf_op jit(solution)/shard_map/pallas_call | solution.py:606
  111.7 7.7 shard_map.342
  123.0 84.6 %shard_map.343 = (bf16[8,64,2048]{2,1,0:T(8,128)(2,1)}, bf16[64,2048]{1,0:T(8,128)(2,1)}, bf16[8,4,64,1536]{3,2,1,0:T(8,128)(2,1)}, bf16[8,64,1024]{2,1,0:T(8,128)(2,1)}, bf16[8,32,256]{2,1,0:T(8,128)(2,1)}) custom-call(bf16[8,64,2048]{2,1,0:T(8,128)(2,1)} %bitcast.252, bf16[64,2048]{1,0:T(8,128)(2,1)} %dynamic-slice_bitcast_fusion.refs_0_.refs_1_, ...), custom_call_target="tpu_custom_call" | custom-call | flops 49999998976 | bytes 1000000 | tf_op jit(solution)/shard_map/pallas_call | solution.py:606
  223.0 92.6 %shard_map.344 = (bf16[8,64,2048]{2,1,0:T(8,128)(2,1)}, bf16[64,2048]{1,0:T(8,128)(2,1)}, bf16[8,4,64,1024]{3,2,1,0:T(8,128)(2,1)}, bf16[4,8,32,256]{3,2,1,0:T(8,128)(2,1)}, bf16[8,64,1536]{2,1,0:T(8,128)(2,1)}) custom-call(bf16[8,64,2048]{2,1,0:T(8,128)(2,1)} %bitcast.253, bf16[64,2048]{1,0:T(8,128)(2,1)} %get-tuple-element.111.refs_1_, ...), custom_call_target="tpu_custom_call" | custom-call | flops 49999998976 | bytes 1000000 | tf_op jit(solution)/shard_map/pallas_call | solution.py:606
  315.7 6.5 fusion.84.is_ref
  322.7 8.0 shard_map.345
  334.3 74.7 %shard_map.346 = (bf16[8,64,2048]{2,1,0:T(8,128)(2,1)}, bf16[64,2048]{1,0:T(8,128)(2,1)}, bf16[8,4,64,1536]{3,2,1,0:T(8,128)(2,1)}, bf16[2,192,2048]{2,1,0:T(8,128)(2,1)}, bf16[2,192,2048]{2,1,0:T(8,128)(2,1)}) custom-call(bf16[8,64,2048]{2,1,0:T(8,128)(2,1)} %bitcast.254, bf16[64,2048]{1,0:T(8,128)(2,1)} %get-tuple-element.119.refs_1_, ...), custom_call_target="tpu_custom_call" | custom-call | flops 49999998976 | bytes 1000000 | tf_op jit(solution)/shard_map/pallas_call | solution.py:606
  409.0 6.2 fusion.85
  415.2 6.8 fusion.52
  427.8 13.5 %shard_map.347 = bf16[4,12,384,256]{3,2,1,0:T(8,128)(2,1)} custom-call(bf16[512,2048]{1,0:T(8,128)(2,1)} %bitcast.195, bf16[512,1536]{1,0:T(8,128)(2,1)} %pad_maximum_fusion.both_ref, bf16[512,768]{1,0:T(8,128)(2,1)} %get-tuple-element.213.hidden_ref, bf16[512,2048]{1,0:T(8,128)(2,1)} %all-gather.2.cloned.1.call-done.all_ref), custom_call_target="tpu_custom_call" | custom-call | tf_op jit(solution)/shard_map/pallas_call | solution.py:928
  445.8 51.7 %shard_map.348 = (bf16[8,64,2048]{2,1,0:T(8,128)(2,1)}, bf16[64,2048]{1,0:T(8,128)(2,1)}, f32[1,2048]{1,0:T(1,128)}) custom-call(bf16[8,64,2048]{2,1,0:T(8,128)(2,1)} %bitcast.249, bf16[64,2048]{1,0:T(8,128)(2,1)} %get-tuple-element.163.refs_1_, bf16[64,2048]{1,0:T(8,128)(2,1)} %fusion.61.refs_2_, f32[1,2048]{1,0:T(1,128)} %get-tuple-element.231.refs_2_.refs_3_), custom_call_target="tpu_custom_call" | custom-call | flops 49999998976 | bytes 1000000 | tf_op jit(solution)/shard_map/pallas_call | solution.py:606
  502.9 11.7 %shard_map.349 = (bf16[512,1024]{1,0:T(8,128)(2,1)}, bf16[512,512]{1,0:T(8,128)(2,1)}, bf16[512,512]{1,0:T(8,128)(2,1)}, f32[8,512]{1,0:T(8,128)}) custom-call(f32[512,512]{1,0:T(8,128)} %fusion.26.dg_ref, f32[512,1024]{1,0:T(8,128)} %fusion.84.is_ref, f32[512,512]{1,0:T(8,128)} %get-tuple-element.128.mixed_ref, f32[512,512]{1,0:T(8,128)} %get-tuple-element.129.rate_ref, ...), custom_call_target="tpu_custom_call" | custom-call | tf_op jit(solution)/shard_map/pallas_call | solution.py:876
  514.6 13.3 %shard_map.350 = bf16[4,12,384,128]{3,2,1,0:T(8,128)(2,1)} custom-call(bf16[512,2048]{1,0:T(8,128)(2,1)} %bitcast.189, bf16[512,1024]{1,0:T(8,128)(2,1)} %get-tuple-element.133.dib_ref, bf16[512,320]{1,0:T(8,128)(2,1)} %get-tuple-element.118.gated_ref, bf16[512,2048]{1,0:T(8,128)(2,1)} %bitcast.193, f32[512,512]{1,0:T(8,128)} %get-tuple-element.128.mixed_ref, ...), custom_call_target="tpu_custom_call" | custom-call | tf_op jit(solution)/shard_map/pallas_call | solution.py:1000
  538.4 53.4 %shard_map.351 = (bf16[8,64,2048]{2,1,0:T(8,128)(2,1)}, bf16[64,2048]{1,0:T(8,128)(2,1)}, f32[1,2048]{1,0:T(1,128)}) custom-call(bf16[8,64,2048]{2,1,0:T(8,128)(2,1)} %bitcast.251, bf16[64,2048]{1,0:T(8,128)(2,1)} %get-tuple-element.119.refs_1_, bf16[64,2048]{1,0:T(8,128)(2,1)} %get-tuple-element.139.refs_2_, f32[1,2048]{1,0:T(1,128)} %get-tuple-element.232.refs_2_.refs_3_), custom_call_target="tpu_custom_call" | custom-call | flops 49999998976 | bytes 1000000 | tf_op jit(solution)/shard_map/pallas_call | solution.py:606
  599.3 13.5 %shard_map.352 = bf16[4,12,384,256]{3,2,1,0:T(8,128)(2,1)} custom-call(bf16[512,2048]{1,0:T(8,128)(2,1)} %bitcast.187, bf16[512,1536]{1,0:T(8,128)(2,1)} %pad_maximum_fusion.1.both_ref, bf16[512,768]{1,0:T(8,128)(2,1)} %copy-done.4, bf16[512,2048]{1,0:T(8,128)(2,1)} %bitcast.197), custom_call_target="tpu_custom_call" | custom-call | tf_op jit(solution)/shard_map/pallas_call | solution.py:928
  612.9 7.4 convolution_convert_fusion.2
  625.3 53.5 %shard_map.353 = (bf16[8,64,2048]{2,1,0:T(8,128)(2,1)}, bf16[64,2048]{1,0:T(8,128)(2,1)}, f32[1,2048]{1,0:T(1,128)}) custom-call(bf16[8,64,2048]{2,1,0:T(8,128)(2,1)} %bitcast.250, bf16[64,2048]{1,0:T(8,128)(2,1)} %get-tuple-element.111.refs_1_, bf16[64,2048]{1,0:T(8,128)(2,1)} %get-tuple-element.144.refs_2_, f32[1,2048]{1,0:T(1,128)} %get-tuple-element.233.refs_2_.refs_3_), custom_call_target="tpu_custom_call" | custom-call | flops 49999998976 | bytes 1000000 | tf_op jit(solution)/shard_map/pallas_call | solution.py:606
  683.5 11.6 %shard_map.354 = (bf16[512,1024]{1,0:T(8,128)(2,1)}, bf16[512,512]{1,0:T(8,128)(2,1)}, bf16[512,512]{1,0:T(8,128)(2,1)}, f32[8,512]{1,0:T(8,128)}) custom-call(f32[512,512]{1,0:T(8,128)} %fusion.22.dg_ref, f32[512,1024]{1,0:T(8,128)} %fusion.82.is_ref, f32[512,512]{1,0:T(8,128)} %get-tuple-element.147.mixed_ref, f32[512,512]{1,0:T(8,128)} %get-tuple-element.148.rate_ref, ...), custom_call_target="tpu_custom_call" | custom-call | tf_op jit(solution)/shard_map/pallas_call | solution.py:876
  695.1 13.5 %shard_map.355 = bf16[4,12,384,128]{3,2,1,0:T(8,128)(2,1)} custom-call(bf16[512,2048]{1,0:T(8,128)(2,1)} %fusion.1.normed_ref, bf16[512,1024]{1,0:T(8,128)(2,1)} %get-tuple-element.152.dib_ref, bf16[512,320]{1,0:T(8,128)(2,1)} %get-tuple-element.107.gated_ref, bf16[512,2048]{1,0:T(8,128)(2,1)} %bitcast.191, f32[512,512]{1,0:T(8,128)} %get-tuple-element.147.mixed_ref, ...), custom_call_target="tpu_custom_call" | custom-call | tf_op jit(solution)/shard_map/pallas_call | solution.py:1000
  720.8 162.0 %shard_map.356 = (bf16[64,2048]{1,0:T(8,128)(2,1)}, f32[1,2048]{1,0:T(1,128)}, bf16[8,4,384,256]{3,2,1,0:T(8,128)(2,1)}, bf16[4,1536,256]{2,1,0:T(8,128)(2,1)}, ...) custom-call(bf16[8,64,2048]{2,1,0:T(8,128)(2,1)} %bitcast.248, ...), custom_call_target="tpu_custom_call" | custom-call | flops 49999998976 | bytes 1000000 | tf_op jit(solution)/shard_map/pallas_call | solution.py:606
  884.3 126.2 %shard_map.357 = (bf16[64,2048]{1,0:T(8,128)(2,1)}, bf16[8,4,384,256]{3,2,1,0:T(8,128)(2,1)}, bf16[4,1536,256]{2,1,0:T(8,128)(2,1)}, bf16[8,4,384,128]{3,2,1,0:T...) custom-call(bf16[8,64,2048]{2,1,0:T(8,128)(2,1)} %bitcast.247, ...), custom_call_target="tpu_custom_call" | custom-call | flops 49999998976 | bytes 1000000 | tf_op jit(solution)/shard_map/pallas_call | solution.py:606
  1013.6 10.6 shard_map.358
  1029.6 14.0 %shard_map.359 = (f32[2,256,6144]{2,1,0:T(8,128)}, f32[2,256,6144]{2,1,0:T(8,128)}) custom-call(bf16[8,4,384,256]{3,2,1,0:T(8,128)(2,1)} %get-tuple-element.183.refs_0_, bf16[8,4,384,256]{3,2,1,0:T(8,128)(2,1)} %get-tuple-element.184.refs_1_), custom_call_target="tpu_custom_call" | custom-call | tf_op jit(solution)/shard_map/pallas_call | solution.py:1040
  1043.5 7.9 shard_map.360
  (180 shorter events, 114.0 us)
Async XLA Ops:
  7.2 408.0 %all-gather.2.cloned.1.call-start = ((), (), s32[]{:S(2)}) async-start(), calls=%async_computation.4 | async-start | bytes 2359296 | tf_op jit(solution)/shard_map/all_gather | solution.py:1349
  94.6 10.0 copy-start.2
  97.0 8.1 copy-start.20
  110.5 9.0 copy-start.7
  216.0 7.0 copy-start.4
  315.6 222.8 %reduce-scatter.5.cloned.1.call-start = ((), (), s32[]{:S(2)}) async-start(), calls=%async_computation.5 | async-start | bytes 11796480 | tf_op jit(solution)/shard_map/reduce_scatter | solution.py:1380
  415.2 6.8 copy-start.30
  441.3 184.0 %reduce-scatter.7.cloned.1.call-start = ((), (), s32[]{:S(2)}) async-start(), calls=%async_computation.6 | async-start | bytes 5898240 | tf_op jit(solution)/shard_map/reduce_scatter | solution.py:1380
  445.8 51.7 %copy-start.10 = (bf16[320,2048]{1,0:T(8,128)(2,1)S(1)}, bf16[320,2048]{1,0:T(8,128)(2,1)}, u32[]{:S(2)}) copy-start(bf16[320,2048]{1,0:T(8,128)(2,1)} %get-tuple-element.215) | copy-start | bytes 3932164
  445.8 51.7 %copy-start.15 = (bf16[192,2048]{1,0:T(8,128)(2,1)S(1)}, bf16[192,2048]{1,0:T(8,128)(2,1)}, u32[]{:S(2)}) copy-start(bf16[192,2048]{1,0:T(8,128)(2,1)} %get-tuple-element.219) | copy-start | bytes 2359300
  514.6 13.4 %copy-start.12 = (bf16[512,1024]{1,0:T(8,128)(2,1)S(1)}, bf16[512,1024]{1,0:T(8,128)(2,1)}, u32[]{:S(2)}) copy-start(bf16[512,1024]{1,0:T(8,128)(2,1)} %get-tuple-element.133.dib_ref) | copy-start | bytes 3145732
  534.0 186.8 %reduce-scatter.9.cloned.1.call-start = ((), (), s32[]{:S(2)}) async-start(), calls=%async_computation.7 | async-start | bytes 11796480 | tf_op jit(solution)/shard_map/reduce_scatter | solution.py:1380
  538.4 53.4 %copy-start.6 = (f32[512,1536]{1,0:T(8,128)S(1)}, f32[512,1536]{1,0:T(8,128)}, u32[]{:S(2)}) copy-start(f32[512,1536]{1,0:T(8,128)} %copy-done.5) | copy-start | bytes 9437188
  599.3 13.5 %copy-start.17 = (bf16[512,768]{1,0:T(8,128)(2,1)S(1)}, bf16[512,768]{1,0:T(8,128)(2,1)}, u32[]{:S(2)}) copy-start(bf16[512,768]{1,0:T(8,128)(2,1)} %copy-done.16) | copy-start | bytes 2359300
  620.3 263.9 %reduce-scatter.11.cloned.1.call-start = ((), (), s32[]{:S(2)}) async-start(), calls=%async_computation.8 | async-start | bytes 5898240 | tf_op jit(solution)/shard_map/reduce_scatter | solution.py:1380
  625.3 53.5 %copy-start.9 = (bf16[320,2048]{1,0:T(8,128)(2,1)S(1)}, bf16[320,2048]{1,0:T(8,128)(2,1)}, u32[]{:S(2)}) copy-start(bf16[320,2048]{1,0:T(8,128)(2,1)} %get-tuple-element.214) | copy-start | bytes 3932164
  625.3 53.5 %copy-start.14 = (bf16[192,2048]{1,0:T(8,128)(2,1)S(1)}, bf16[192,2048]{1,0:T(8,128)(2,1)}, u32[]{:S(2)}) copy-start(bf16[192,2048]{1,0:T(8,128)(2,1)} %get-tuple-element.217) | copy-start | bytes 2359300
  695.1 13.5 %copy-start.11 = (bf16[512,1024]{1,0:T(8,128)(2,1)S(1)}, bf16[512,1024]{1,0:T(8,128)(2,1)}, u32[]{:S(2)}) copy-start(bf16[512,1024]{1,0:T(8,128)(2,1)} %get-tuple-element.152.dib_ref) | copy-start | bytes 3145732
  720.8 162.1 %copy-start.26 = (f32[1,2048]{1,0:T(1,128)S(1)}, f32[1,2048]{1,0:T(1,128)}, u32[]{:S(2)}) copy-start(f32[1,2048]{1,0:T(1,128)} %get-tuple-element.169) | copy-start | bytes 24580
  720.8 162.1 %copy-start.27 = (f32[1,2048]{1,0:T(1,128)S(1)}, f32[1,2048]{1,0:T(1,128)}, u32[]{:S(2)}) copy-start(f32[1,2048]{1,0:T(1,128)} %get-tuple-element.168) | copy-start | bytes 24580
  720.8 162.1 %copy-start.28 = (f32[1,2048]{1,0:T(1,128)S(1)}, f32[1,2048]{1,0:T(1,128)}, u32[]{:S(2)}) copy-start(f32[1,2048]{1,0:T(1,128)} %get-tuple-element.167) | copy-start | bytes 24580
  1043.5 7.9 copy-start.19
  1043.5 8.6 copy-start.18
  1043.5 9.3 copy-start.1
  (14 other events, 43.0 us)
Sparse Core Ops, SparseCore 0:
  315.7 35.7 all-gather.1
  441.4 96.9 reduce-scatter.4
  542.0 57.0 reduce-scatter.6
  620.4 97.1 reduce-scatter.8
  721.0 95.0 reduce-scatter.10
